TPU v7x, 32 devices: a whole 2x2x4 slice. The times are simulated.
32 devices in a mesh: parts: 2 (over x), col: 16 (over z, y, core).
Axes of the slice: x: 2, y: 2, z: 4, core: 2. Of those that a mesh axis runs over, the one named last changes fastest.
Arguments:
- outages: int32 [2048], P(('parts', 'col')), parts along dimension 0, may hold values from 0 to 20479
- branch_from: int32 [20480], replicated, may hold values from 0 to 8191
- branch_to: int32 [20480], replicated, may hold values from 0 to 8191, as said below
- bus_slot: int32 [8192], replicated, may hold values from 0 to 8191, each once
- susceptance: float32 [20480], replicated, may hold values from 0.03 to 0.09
- charging: float32 [20480], replicated, may hold values from 0.04 to 0.12
- rating: float32 [20480], replicated, may hold values from 0.018 to 0.063
- base_angles: float32 [16384], P('parts'), parts along dimension 0, may hold values from -1.2 to 1.2
- zinv: float32 [8192, 8192], P(None, 'col'), may hold values from -0.6 to 2, as said below
Outputs:
- injections: float32 [2, 2048], P(None, ('parts', 'col')), parts along dimension 1
- deviation: float32 [2048, 8192], P('parts', 'col'), parts along dimension 0
- worst: float32 [2048], P(('parts', 'col')), parts along dimension 0
There are 2 independent parts, one for each index of `parts`. A program takes and returns all parts, laid end to end along the dimension named above; an argument that names none is the same for every part. Nothing has to cross between parts.
Inputs may be any that keep to these rules, and one draw needn't show every extreme that they name: branch_to differs from branch_from on every branch. zinv is symmetric; its diagonal lies in [1, 2] and every other entry in [-0.6, 0.6].
All inputs are finite; a program needn't handle non-finite values.
Results may differ from a plain program's by a relative error of at most 0.0003.
Values sent between devices are 32-bit elements; how exact they have to be, the bound alone decides.
No kernel may reach another device: no remote copies, remote signals or barrier semaphores. Data moves between devices by JAX's collectives and lax.ppermute only.
A program may use at most 128 MiB of HBM per device.

v0:
```python
import math

import jax
import jax.numpy as jnp
from jax import lax
from jax.sharding import PartitionSpec as P

STEPS = 3


def newton(a_head, a_tail, self_head, cross_head, cross_tail, self_tail, bsus, hchg):
    inj_head = jnp.zeros_like(a_head)
    inj_tail = jnp.zeros_like(a_head)
    for step in range(1, STEPS + 1):
        level = step / STEPS
        end_head = a_head + self_head * inj_head + cross_head * inj_tail
        end_tail = a_tail + cross_tail * inj_head + self_tail * inj_tail
        spread = end_head - end_tail
        sine_val = jnp.sin(spread)
        cosine_val = jnp.cos(spread)
        resid_head = inj_head - level * (bsus * sine_val + hchg * end_head)
        resid_tail = inj_tail - level * (-bsus * sine_val + hchg * end_tail)
        diag_term = bsus * cosine_val + hchg
        cross_term = -bsus * cosine_val
        jac_one = 1.0 - level * (diag_term * self_head + cross_term * cross_tail)
        jac_two = -level * (diag_term * cross_head + cross_term * self_tail)
        jac_three = -level * (cross_term * self_head + diag_term * cross_tail)
        jac_four = 1.0 - level * (cross_term * cross_head + diag_term * self_tail)
        determinant = jac_one * jac_four - jac_two * jac_three
        inj_head = inj_head - (jac_four * resid_head - jac_two * resid_tail) / determinant
        inj_tail = inj_tail - (jac_one * resid_tail - jac_three * resid_head) / determinant
    return (inj_head, inj_tail)


def worst_loading(angles, ids, from_slot, to_slot, susceptance, rating):
    branch_total = susceptance.shape[0]
    block_len = math.gcd(branch_total, 4096)
    blocks = branch_total // block_len
    by_bus = angles.T
    branch_ids = jnp.arange(branch_total, dtype=jnp.int32)

    def one_block(packed):
        block_from, block_to, block_sus, block_rate, block_ids = packed
        spread = jnp.take(by_bus, block_from, axis=0) - jnp.take(by_bus, block_to, axis=0)
        load = jnp.abs(block_sus[:, None] * jnp.sin(spread)) / block_rate[:, None]
        load = jnp.where(block_ids[:, None] == ids[None, :], jnp.zeros_like(load), load)
        return jnp.max(load, axis=0)

    packed = (
        from_slot.reshape(blocks, block_len),
        to_slot.reshape(blocks, block_len),
        susceptance.reshape(blocks, block_len),
        rating.reshape(blocks, block_len),
        branch_ids.reshape(blocks, block_len),
    )
    return jnp.max(lax.map(one_block, packed), axis=0)


def entry_at(values, target):
    return jnp.take_along_axis(values, target[:, None], axis=1)[:, 0]


def per_device(
    outages, branch_from, branch_to, bus_slot, susceptance, charging, rating, base_angles, zinv
):
    all_ids = lax.all_gather(outages, "col", axis=0, tiled=True)
    from_slot = bus_slot[branch_from]
    to_slot = bus_slot[branch_to]
    head = from_slot[all_ids]
    tail = to_slot[all_ids]
    row_head = zinv[head]
    row_tail = zinv[tail]
    own_head = from_slot[outages]
    own_tail = to_slot[outages]
    pieces = jnp.stack([row_head, row_tail], axis=1)
    received = lax.all_to_all(pieces, "col", split_axis=0, concat_axis=2, tiled=True)
    full_head = received[:, 0]
    full_tail = received[:, 1]
    inj_head, inj_tail = newton(
        base_angles[own_head],
        base_angles[own_tail],
        entry_at(full_head, own_head),
        entry_at(full_head, own_tail),
        entry_at(full_tail, own_head),
        entry_at(full_tail, own_tail),
        susceptance[outages],
        charging[outages],
    )
    shifted = inj_head[:, None] * full_head + inj_tail[:, None] * full_tail
    deviation = lax.all_to_all(shifted, "col", split_axis=1, concat_axis=0, tiled=True)
    worst = worst_loading(
        base_angles[None, :] + shifted, outages, from_slot, to_slot, susceptance, rating
    )
    return (jnp.stack([inj_head, inj_tail]), deviation, worst)


def solution(mesh):
    return jax.shard_map(
        per_device,
        mesh=mesh,
        in_specs=(P(("parts", "col")), P(), P(), P(), P(), P(), P(), P("parts"), P(None, "col")),
        out_specs=(P(None, ("parts", "col")), P("parts", "col"), P(("parts", "col"))),
        check_vma=False,
    )
```

profile of v0, /device:TPU:9, one launch (start us, length us, event | category | flops | bytes accessed | tf_op | source)
XLA Modules:
  0.0 635.4 jit_solution(13339843235086763925)
XLA Ops:
  0.7 0.9 fusion.9
  1.6 0.9 fusion.8
  2.5 113.0 %gather_fusion.8 = s32[20480]{0:T(1024)S(1)} fusion(s32[8192]{0:T(1024)S(1)} %copy-done.2, s32[20480]{0:T(1024)S(1)} %fusion.9), kind=kCustom, calls=%fused_computation.12 | custom fusion | bytes 245760 | tf_op jit(solution)/shard_map/gather | solution.py:68
  115.6 113.0 %gather_fusion.3 = s32[20480]{0:T(1024)S(1)} fusion(s32[8192]{0:T(1024)S(1)} %copy-done.2, s32[20480]{0:T(1024)S(1)} %fusion.8), kind=kCustom, calls=%fused_computation.7 | custom fusion | bytes 245760 | tf_op jit(solution)/shard_map/gather | solution.py:67
  228.7 0.6 dynamic-slice
  230.2 8.7 %all-reduce = s32[1024]{0:T(1024)S(1)} all-reduce(s32[1024]{0:T(1024)S(1)} %dynamic-update-slice), channel_id=1, replica_groups=mesh['parts'=2,'col'=16] {'col'}, use_global_device_ids=true, to_apply=%add | all-reduce | flops 1024 | bytes 8192
  238.9 6.1 gather_fusion.9
  245.1 6.2 gather_fusion.6
  251.3 9.8 %gather_fusion.10 = f32[1024,512]{1,0:T(8,128)S(1)} fusion(f32[8192,512]{1,0:T(8,128)} %param.23, s32[1024]{0:T(1024)S(1)} %broadcast_clamp_fusion), kind=kCustom, calls=%fused_computation.14 | custom fusion | bytes 4198400 | tf_op jit(solution)/shard_map/gather | solution.py:72
  261.1 11.0 %gather_fusion.7 = f32[1024,512]{1,0:T(8,128)} fusion(f32[8192,512]{1,0:T(8,128)} %param.23, s32[1024]{0:T(1024)S(1)} %broadcast_clamp_fusion.1), kind=kCustom, calls=%fused_computation.11 | custom fusion | bytes 4198400 | tf_op jit(solution)/shard_map/gather | solution.py:71
  272.1 2.0 pad_maximum_fusion
  274.2 5.2 copy.17
  279.3 8.7 %all-to-all-start = ((f32[1024,2,512]{2,1,0:T(2,128)}), f32[1024,2,512]{2,1,0:T(2,128)}, u32[]{:S(2)}, u32[]{:S(2)}) async-start(f32[1024,2,512]{2,1,0:T(2,128)} %copy.17), calls=%async_computation | async-start | bytes 8388608 | tf_op jit(solution)/shard_map/all_to_all | solution.py:76
  288.1 0.8 gather_fusion.11
  288.9 0.8 gather_fusion.4
  289.7 0.8 gather_fusion.2
  290.5 0.8 gather_fusion.13
  291.3 0.8 gather_fusion.12
  292.1 0.8 gather_fusion.5
  293.0 85.4 %all-to-all-done = f32[1024,2,512]{2,1,0:T(2,128)} async-done(((f32[1024,2,512]{2,1,0:T(2,128)}), f32[1024,2,512]{2,1,0:T(2,128)}, u32[]{:S(2)}, u32[]{:S(2)}) %all-to-all-start) | async-done | bytes 4194336 | tf_op jit(solution)/shard_map/all_to_all | solution.py:76
  378.4 8.4 %copy.18 = f32[16,64,2,512]{1,3,0,2:T(8,128)} copy(f32[16,64,2,512]{3,2,1,0:T(2,128)} %bitcast.17) | data formatting | bytes 8388608 | tf_op jit(solution)/shard_map/all_to_all | solution.py:76
  386.8 9.8 %fusion.131 = (f32[64,1,8192]{0,2,1:T(8,128)}, f32[64,8192]{0,1:T(8,128)}, f32[64,8192]{0,1:T(8,128)}, f32[64,1,8192]{0,2,1:T(8,128)}) fusion(f32[64,2,8192]{0,2,1:T(8,128)} %bitcast.594), kind=kLoop, calls=%fused_computation.279 | loop fusion | bytes 12582912 | tf_op jit(solution)/shard_map/slice | solution.py:77
  396.6 1.7 gather_fusion.16
  398.2 1.7 gather_fusion.17
  399.9 1.7 gather_fusion.14
  401.6 1.7 gather_fusion.15
  403.3 2.8 copy.20
  406.1 3.8 copy.19
  410.3 5.6 add_bitcast_fusion
  415.9 1.9 multiply_add_fusion
  417.8 7.0 %all-to-all-start.1 = ((f32[64,16,512]{2,0,1:T(8,128)}), f32[64,16,512]{2,0,1:T(8,128)}, u32[]{:S(2)}, u32[]{:S(2)}) async-start(f32[64,16,512]{2,0,1:T(8,128)} %multiply_add_fusion), calls=%async_computation.1 | async-start | bytes 4194304 | tf_op jit(solution)/shard_map/all_to_all | solution.py:90
  424.9 205.9 %while.10 = (s32[]{:T(128)}, f32[5,64]{1,0:T(8,128)S(1)}, s32[5,4096]{1,0:T(8,128)S(1)}, s32[64]{0:T(128)S(1)}, f32[5,4096]{1,0:T(8,128)S(1)}, /*index=5*/s32[5,...) while((s32[]{:T(128)}, f32[5,64]{1,0:T(8,128)S(1)}, ...), condition=%wide.region_2.5_spmd, body=%wide.region_0.4_spmd.sunk | while | flops 2441154 | bytes 6653061 | solution.py:56
  424.9 13.0 %gather_fusion = f32[4096,64]{1,0:T(8,128)S(1)} fusion(f32[8192,64]{1,0:T(8,128)} %get-tuple-element.240, s32[4096]{0:T(1024)S(1)} %fusion.135), kind=kCustom, calls=%fused_computation.5.clone.clone.1 | custom fusion | bytes 2113536 | tf_op jit(solution)/shard_map/while/body/eval_jaxpr/jit(_take)/gather | solution.py:44
  437.9 16.3 %gather_fusion.1 = f32[4096,64]{1,0:T(8,128)} fusion(f32[8192,64]{1,0:T(8,128)} %get-tuple-element.240, s32[4096]{0:T(1024)S(1)} %fusion.136), kind=kCustom, calls=%fused_computation.1.clone.clone.1 | custom fusion | bytes 2113536 | tf_op jit(solution)/shard_map/while/body/eval_jaxpr/jit(_take)/gather | solution.py:44
  454.3 11.7 %fusion.137 = f32[64]{0:T(128)S(1)} fusion(f32[4096,64]{1,0:T(8,128)S(1)} %gather_fusion, f32[4096,64]{1,0:T(8,128)} %gather_fusion.1, f32[4096]{0:T(1024)S(1)} %bitcast.605, f32[4096]{0:T(1024)S(1)} %bitcast.606, s32[64]{0:T(128)S(1)} %get-tuple-element.237, s32[4096]{0:T(1024)S(1)} %bitcast.604, pred[4096]{0:T(1024)(128)(4,1)S(1)} %compare_and_fusion.6, ...), kind=kLoop, calls=%fused_computation.24.clone.1 | loop fusion | flops 2359232 | bytes 2155008 | tf_op jit(solution)/shard_map/while/body/eval_jaxpr/reduce_max | solution.py:47
  466.1 13.0 %gather_fusion = f32[4096,64]{1,0:T(8,128)S(1)} fusion(f32[8192,64]{1,0:T(8,128)} %get-tuple-element.240, s32[4096]{0:T(1024)S(1)} %fusion.135), kind=kCustom, calls=%fused_computation.5.clone.clone.1 | custom fusion | bytes 2113536 | tf_op jit(solution)/shard_map/while/body/eval_jaxpr/jit(_take)/gather | solution.py:44
  479.1 16.3 %gather_fusion.1 = f32[4096,64]{1,0:T(8,128)} fusion(f32[8192,64]{1,0:T(8,128)} %get-tuple-element.240, s32[4096]{0:T(1024)S(1)} %fusion.136), kind=kCustom, calls=%fused_computation.1.clone.clone.1 | custom fusion | bytes 2113536 | tf_op jit(solution)/shard_map/while/body/eval_jaxpr/jit(_take)/gather | solution.py:44
  495.5 11.7 %fusion.137 = f32[64]{0:T(128)S(1)} fusion(f32[4096,64]{1,0:T(8,128)S(1)} %gather_fusion, f32[4096,64]{1,0:T(8,128)} %gather_fusion.1, f32[4096]{0:T(1024)S(1)} %bitcast.605, f32[4096]{0:T(1024)S(1)} %bitcast.606, s32[64]{0:T(128)S(1)} %get-tuple-element.237, s32[4096]{0:T(1024)S(1)} %bitcast.604, pred[4096]{0:T(1024)(128)(4,1)S(1)} %compare_and_fusion.6, ...), kind=kLoop, calls=%fused_computation.24.clone.1 | loop fusion | flops 2359232 | bytes 2155008 | tf_op jit(solution)/shard_map/while/body/eval_jaxpr/reduce_max | solution.py:47
  507.3 13.0 %gather_fusion = f32[4096,64]{1,0:T(8,128)S(1)} fusion(f32[8192,64]{1,0:T(8,128)} %get-tuple-element.240, s32[4096]{0:T(1024)S(1)} %fusion.135), kind=kCustom, calls=%fused_computation.5.clone.clone.1 | custom fusion | bytes 2113536 | tf_op jit(solution)/shard_map/while/body/eval_jaxpr/jit(_take)/gather | solution.py:44
  520.3 16.3 %gather_fusion.1 = f32[4096,64]{1,0:T(8,128)} fusion(f32[8192,64]{1,0:T(8,128)} %get-tuple-element.240, s32[4096]{0:T(1024)S(1)} %fusion.136), kind=kCustom, calls=%fused_computation.1.clone.clone.1 | custom fusion | bytes 2113536 | tf_op jit(solution)/shard_map/while/body/eval_jaxpr/jit(_take)/gather | solution.py:44
  536.7 11.7 %fusion.137 = f32[64]{0:T(128)S(1)} fusion(f32[4096,64]{1,0:T(8,128)S(1)} %gather_fusion, f32[4096,64]{1,0:T(8,128)} %gather_fusion.1, f32[4096]{0:T(1024)S(1)} %bitcast.605, f32[4096]{0:T(1024)S(1)} %bitcast.606, s32[64]{0:T(128)S(1)} %get-tuple-element.237, s32[4096]{0:T(1024)S(1)} %bitcast.604, pred[4096]{0:T(1024)(128)(4,1)S(1)} %compare_and_fusion.6, ...), kind=kLoop, calls=%fused_computation.24.clone.1 | loop fusion | flops 2359232 | bytes 2155008 | tf_op jit(solution)/shard_map/while/body/eval_jaxpr/reduce_max | solution.py:47
  548.5 13.0 %gather_fusion = f32[4096,64]{1,0:T(8,128)S(1)} fusion(f32[8192,64]{1,0:T(8,128)} %get-tuple-element.240, s32[4096]{0:T(1024)S(1)} %fusion.135), kind=kCustom, calls=%fused_computation.5.clone.clone.1 | custom fusion | bytes 2113536 | tf_op jit(solution)/shard_map/while/body/eval_jaxpr/jit(_take)/gather | solution.py:44
  561.5 16.3 %gather_fusion.1 = f32[4096,64]{1,0:T(8,128)} fusion(f32[8192,64]{1,0:T(8,128)} %get-tuple-element.240, s32[4096]{0:T(1024)S(1)} %fusion.136), kind=kCustom, calls=%fused_computation.1.clone.clone.1 | custom fusion | bytes 2113536 | tf_op jit(solution)/shard_map/while/body/eval_jaxpr/jit(_take)/gather | solution.py:44
  577.9 11.7 %fusion.137 = f32[64]{0:T(128)S(1)} fusion(f32[4096,64]{1,0:T(8,128)S(1)} %gather_fusion, f32[4096,64]{1,0:T(8,128)} %gather_fusion.1, f32[4096]{0:T(1024)S(1)} %bitcast.605, f32[4096]{0:T(1024)S(1)} %bitcast.606, s32[64]{0:T(128)S(1)} %get-tuple-element.237, s32[4096]{0:T(1024)S(1)} %bitcast.604, pred[4096]{0:T(1024)(128)(4,1)S(1)} %compare_and_fusion.6, ...), kind=kLoop, calls=%fused_computation.24.clone.1 | loop fusion | flops 2359232 | bytes 2155008 | tf_op jit(solution)/shard_map/while/body/eval_jaxpr/reduce_max | solution.py:47
  589.7 13.0 %gather_fusion = f32[4096,64]{1,0:T(8,128)S(1)} fusion(f32[8192,64]{1,0:T(8,128)} %get-tuple-element.240, s32[4096]{0:T(1024)S(1)} %fusion.135), kind=kCustom, calls=%fused_computation.5.clone.clone.1 | custom fusion | bytes 2113536 | tf_op jit(solution)/shard_map/while/body/eval_jaxpr/jit(_take)/gather | solution.py:44
  602.6 16.3 %gather_fusion.1 = f32[4096,64]{1,0:T(8,128)} fusion(f32[8192,64]{1,0:T(8,128)} %get-tuple-element.240, s32[4096]{0:T(1024)S(1)} %fusion.136), kind=kCustom, calls=%fused_computation.1.clone.clone.1 | custom fusion | bytes 2113536 | tf_op jit(solution)/shard_map/while/body/eval_jaxpr/jit(_take)/gather | solution.py:44
  619.1 11.7 %fusion.137 = f32[64]{0:T(128)S(1)} fusion(f32[4096,64]{1,0:T(8,128)S(1)} %gather_fusion, f32[4096,64]{1,0:T(8,128)} %gather_fusion.1, f32[4096]{0:T(1024)S(1)} %bitcast.605, f32[4096]{0:T(1024)S(1)} %bitcast.606, s32[64]{0:T(128)S(1)} %get-tuple-element.237, s32[4096]{0:T(1024)S(1)} %bitcast.604, pred[4096]{0:T(1024)(128)(4,1)S(1)} %compare_and_fusion.6, ...), kind=kLoop, calls=%fused_computation.24.clone.1 | loop fusion | flops 2359232 | bytes 2155008 | tf_op jit(solution)/shard_map/while/body/eval_jaxpr/reduce_max | solution.py:47
  632.3 3.1 copy.30
  (97 shorter events, 3.1 us)
Async XLA Ops:
  0.6 289.9 %copy-start = (f32[20480]{0:T(1024)S(1)}, f32[20480]{0:T(1024)}, u32[]{:S(2)}) copy-start(f32[20480]{0:T(1024)} %param.20) | copy-start | bytes 245764
  0.6 1.9 copy-start.2
  115.6 113.1 %copy-start.8 = (u32[32]{0:T(128)S(1)}, u32[32]{0:T(128)}, u32[]{:S(2)}) copy-start(u32[32]{0:T(128)} %constant.123) | copy-start | bytes 388
  115.6 114.3 %copy-start.7 = (s32[64]{0:T(128)S(1)}, s32[64]{0:T(128)}, u32[]{:S(2)}) copy-start(s32[64]{0:T(128)} %param.15) | copy-start | bytes 772
  279.3 10.3 %copy-start.5 = (f32[20480]{0:T(1024)S(1)}, f32[20480]{0:T(1024)}, u32[]{:S(2)}) copy-start(f32[20480]{0:T(1024)} %param.19) | copy-start | bytes 245764
  279.3 99.1 %all-to-all-start = ((f32[1024,2,512]{2,1,0:T(2,128)}), f32[1024,2,512]{2,1,0:T(2,128)}, u32[]{:S(2)}, u32[]{:S(2)}) async-start(f32[1024,2,512]{2,1,0:T(2,128)} %copy.17), calls=%async_computation | async-start | bytes 8388608 | tf_op jit(solution)/shard_map/all_to_all | solution.py:76
  288.1 3.2 copy-start.3
  288.1 4.8 copy-start.6
  410.3 5.6 copy-start.4
  417.8 214.5 %all-to-all-start.1 = ((f32[64,16,512]{2,0,1:T(8,128)}), f32[64,16,512]{2,0,1:T(8,128)}, u32[]{:S(2)}, u32[]{:S(2)}) async-start(f32[64,16,512]{2,0,1:T(8,128)} %multiply_add_fusion), calls=%async_computation.1 | async-start | bytes 4194304 | tf_op jit(solution)/shard_map/all_to_all | solution.py:90
  632.3 3.1 copy-start.1
where the time goes:
time: 638 us; the launch traced here: 635 us
  local copies, waits for them, and re-layouts  452 us (71%)
  waiting for transfers between devices  85.4 us (13%)
  other arithmetic  71.8 us (11%)
  starting transfers between devices  15.8 us (2%)
  blocking collectives  8.74 us (1%)
    gather x1, local copies, waits for them, and re-layouts, per_device(): to_slot = bus_slot[branch_to]  113 us
    gather x1, local copies, waits for them, and re-layouts, per_device(): from_slot = bus_slot[branch_from]  113 us
    all_to_all x1, waiting for transfers between devices, per_device(): lax.all_to_all(pieces, 'col', split_axis=0, concat_axis=2, tiled=True)  85.4 us
    gather x5, local copies, waits for them, and re-layouts, one_block(): jnp.take(by_bus, block_from, axis=0) - jnp.take(by_bus, block_to, axis=0)  81.7 us
    gather x5, local copies, waits for them, and re-layouts, one_block(): jnp.take(by_bus, block_to, axis=0)  64.8 us
    reduce_max x5, other arithmetic, one_block(): return jnp.max(load, axis=0)  58.3 us
  transfers between devices with their start and end apart: 2, of which 1 were waited for; matrix products, arithmetic and copies ran while one was open for 33% of the time, Pallas kernels for 0%

commit v1 on v0

v1 whole, which is shorter than its diff:
```python
import functools
import math

import jax
import jax.numpy as jnp
from jax import lax
from jax.experimental import pallas as pl
from jax.experimental.pallas import tpu as pltpu
from jax.sharding import PartitionSpec as P

STEPS = 3
LANES = 128
FIXED = float(2**30)
SINE = (3.1415926444, -5.1677100819, 2.5500775297, -0.5982913039, 0.0776576582)
VMEM = pl.BlockSpec(memory_space=pltpu.VMEM)
SMEM = pl.BlockSpec(memory_space=pltpu.SMEM)
ANY = pl.BlockSpec(memory_space=pl.ANY)


def params(mib):
    return pltpu.CompilerParams(vmem_limit_bytes=mib * 2**20)


def split(table, parts):
    out = []
    for _ in range(parts):
        piece = table.astype(jnp.bfloat16)
        out.append(piece)
        table = table - piece.astype(jnp.float32)
    return out


def lookup(pieces, index):
    rows = pieces[0].shape[0]
    n = index.shape[1]
    hot = lax.broadcasted_iota(jnp.int32, (rows, n), 0) == (index >> 7)
    hot = jnp.where(hot, 1.0, 0.0).astype(jnp.bfloat16)
    dims = (((0,), (0,)), ((), ()))
    total = sum(lax.dot_general(p, hot, dims, preferred_element_type=jnp.float32) for p in pieces)
    lane = lax.broadcasted_iota(jnp.int32, (LANES, n), 0) == (index & 127)
    return jnp.sum(jnp.where(lane, total, 0.0), axis=0, keepdims=True)


def newton(a_head, a_tail, self_head, cross, self_tail, bsus, hchg):
    inj_head = jnp.zeros_like(a_head)
    inj_tail = jnp.zeros_like(a_head)
    for step in range(1, STEPS + 1):
        level = step / STEPS
        end_head = a_head + self_head * inj_head + cross * inj_tail
        end_tail = a_tail + cross * inj_head + self_tail * inj_tail
        spread = end_head - end_tail
        sine_val = jnp.sin(spread)
        cosine_val = jnp.cos(spread)
        resid_head = inj_head - level * (bsus * sine_val + hchg * end_head)
        resid_tail = inj_tail - level * (-bsus * sine_val + hchg * end_tail)
        diag_term = bsus * cosine_val + hchg
        cross_term = -bsus * cosine_val
        jac_one = 1.0 - level * (diag_term * self_head + cross_term * cross)
        jac_two = -level * (diag_term * cross + cross_term * self_tail)
        jac_three = -level * (cross_term * self_head + diag_term * cross)
        jac_four = 1.0 - level * (cross_term * cross + diag_term * self_tail)
        determinant = jac_one * jac_four - jac_two * jac_three
        inj_head = inj_head - (jac_four * resid_head - jac_two * resid_tail) / determinant
        inj_tail = inj_tail - (jac_one * resid_tail - jac_three * resid_head) / determinant
    return inj_head, inj_tail


def ends_kernel(cols, me_ref, ids_ref, from_ref, to_ref, slot_ref, sus_ref, chg_ref, base_ref, zinv_ref,
                head_ref, tail_ref, pick_ref, state_ref, cross_ref, tile_s, rows, tiles, sem):
    blocks = ids_ref.shape[0]
    width = cols // LANES
    first = me_ref[0] * cols
    f_parts = split(from_ref[...].astype(jnp.float32), 2)
    t_parts = split(to_ref[...].astype(jnp.float32), 2)
    s_parts = split(slot_ref[...].astype(jnp.float32), 2)
    sus_parts = split(sus_ref[...], 3)
    chg_parts = split(chg_ref[...], 3)
    base_parts = split(base_ref[...], 3)
    for b in range(blocks):
        row = pl.ds(b, 1)
        ids = ids_ref[row, :]
        head = lookup(s_parts, lookup(f_parts, ids).astype(jnp.int32)).astype(jnp.int32)
        tail = lookup(s_parts, lookup(t_parts, ids).astype(jnp.int32)).astype(jnp.int32)
        head_ref[0, row, :] = head
        tail_ref[0, row, :] = tail
        head_ref[1, row, :] = (head >> 3) * (8 * width) + (head & 7)
        tail_ref[1, row, :] = (tail >> 3) * (8 * width) + (tail & 7)
        state_ref[0, row, :] = lookup(base_parts, head)
        state_ref[1, row, :] = lookup(base_parts, tail)
        state_ref[2, row, :] = lookup(sus_parts, ids)
        state_ref[3, row, :] = lookup(chg_parts, ids)
        pick_ref[row, :] = tail - first
        column = jnp.clip((tail - first) >> 7, 0, width - 1)
        tiles[row, :] = (head >> 3) * (8 * width) + (head & 7) + column * 8
    copy = pltpu.make_async_copy(tiles, tile_s, sem)
    copy.start()
    copy.wait()

    def block(b, carry):
        for j in range(LANES):
            rows[pl.ds(j, 1), :] = zinv_ref[pl.ds(tile_s[b, j], 1), :]
        offset = pick_ref[pl.ds(b, 1), :]
        inside = (offset >= 0) & (offset < cols)
        hit = lax.broadcasted_iota(jnp.int32, (LANES, LANES), 0) == jnp.where(inside, offset & 127, -1)
        entry = jnp.sum(jnp.where(hit, rows[...].T, 0.0), axis=0, keepdims=True)
        cross_ref[pl.ds(b, 1), :] = jnp.round(entry * FIXED).astype(jnp.int32)
        return carry

    lax.fori_loop(0, blocks, block, 0)


def spread_kernel(me_ref, head_s, tail_s, head_ref, tail_ref, state_ref, cross_ref, diag_ref, base_ref,
                  zinv_ref, inj_ref, dev_ref, *rest):
    units, (rows_h, rows_t) = rest[:-2], rest[-2:]
    blocks, cols = cross_ref.shape[0], units[0].shape[0]
    tiles = cols // LANES
    me = me_ref[0]
    chip = me >> 1
    d_parts = split(diag_ref[...], 3)
    self_h = [lookup(d_parts, head_ref[0, pl.ds(b, 1), :]) for b in range(blocks)]
    self_t = [lookup(d_parts, tail_ref[0, pl.ds(b, 1), :]) for b in range(blocks)]
    cross = cross_ref[...].astype(jnp.float32) * (1.0 / FIXED)
    inj_h, inj_t = newton(state_ref[0], state_ref[1], jnp.concatenate(self_h, 0), cross,
                          jnp.concatenate(self_t, 0), state_ref[2], state_ref[3])
    inj_ref[0] = inj_h
    inj_ref[1] = inj_t
    for d, unit in enumerate(units):
        blk = chip ^ d

        def fetch(j, carry):
            for i in range(16):
                o = j * 16 + i
                for t in range(tiles):
                    rows_h[t, pl.ds(o, 1), :] = zinv_ref[pl.ds(head_s[1, blk, o] + 8 * t, 1), :]
                    rows_t[t, pl.ds(o, 1), :] = zinv_ref[pl.ds(tail_s[1, blk, o] + 8 * t, 1), :]
            return carry

        lax.fori_loop(0, LANES // 16, fetch, 0)
        scale_h = jnp.broadcast_to(inj_ref[0, pl.ds(blk, 1), :], (LANES, LANES)).T
        scale_t = jnp.broadcast_to(inj_ref[1, pl.ds(blk, 1), :], (LANES, LANES)).T
        for t in range(tiles):
            at = slice(t * LANES, (t + 1) * LANES)
            dev = scale_h * rows_h[t] + scale_t * rows_t[t]
            dev_ref[pl.ds(pl.multiple_of(blk * LANES, LANES), LANES), at] = dev
            angle = base_ref[pl.ds(me * tiles + t, 1), :] + dev
            unit[at, :] = (angle * (1.0 / math.pi)).T


def prep_kernel(me_ref, from_ref, to_ref, slot_ref, sus_ref, rate_ref, f_ref, t_ref, ratio_ref):
    half = f_ref.shape[0]
    me = me_ref[0]
    start = (me & 1) * half
    flip = me * (slot_ref.shape[0] * LANES // me_ref[1])
    s_parts = split(slot_ref[...].astype(jnp.float32), 2)

    def group(g, carry):
        for i in range(8):
            row = pl.ds(start + g * 8 + i, 1)
            out = pl.ds(g * 8 + i, 1)
            f_ref[out, :] = lookup(s_parts, from_ref[row, :]).astype(jnp.int32) ^ flip
            t_ref[out, :] = lookup(s_parts, to_ref[row, :]).astype(jnp.int32) ^ flip
            ratio_ref[out, :] = sus_ref[row, :] / rate_ref[row, :]
        return carry

    lax.fori_loop(0, half // 8, group, 0)


def worst_kernel(me_ref, f_s, t_s, ratio_ref, ids_ref, *rest):
    pieces, (out_ref, table, diff, best, sem) = rest[:-5], rest[-5:]
    unit = pieces[0].shape[0]
    copies = []
    for i, piece in enumerate(pieces):
        copy = pltpu.make_async_copy(piece, table.at[pl.ds(i * unit, unit)], sem.at[i])
        copy.start()
        copies.append(copy)
    for copy in copies:
        copy.wait()
    half = f_s.shape[0]
    me = me_ref[0]
    ids = ids_ref[pl.ds(me >> 1, 1), :]
    start = (me & 1) * half
    best[...] = jnp.zeros_like(best)

    def block(b, carry):
        for j in range(LANES):
            diff[pl.ds(j, 1), :] = table[pl.ds(f_s[b, j], 1), :] - table[pl.ds(t_s[b, j], 1), :]
        turn = diff[...]
        turn = turn - jnp.round(turn)
        square = turn * turn
        poly = SINE[4]
        for c in SINE[3::-1]:
            poly = poly * square + c
        ratio = jnp.broadcast_to(ratio_ref[pl.ds(b, 1), :], (LANES, LANES)).T
        load = jnp.abs(turn * poly) * ratio
        branch = lax.broadcasted_iota(jnp.int32, (LANES, LANES), 0) + (start + b) * LANES
        load = jnp.where(branch == ids, 0.0, load)
        best[...] = jnp.maximum(best[...], jnp.max(load.reshape(LANES // 8, 8, LANES), axis=0))
        return carry

    lax.fori_loop(0, half, block, 0)
    out_ref[...] = jnp.max(best[...], axis=0, keepdims=True)


def per_device(
    outages, branch_from, branch_to, bus_slot, susceptance, charging, rating, base_angles, zinv
):
    n_col = lax.axis_size("col")
    buses, cols = zinv.shape
    own = outages.shape[0]
    total = own * n_col
    blocks = total // LANES
    chips = n_col // 2
    assert own * 2 == LANES and chips & (chips - 1) == 0
    me = lax.axis_index("col")
    where = jnp.stack([me, jnp.int32(n_col)])
    tab = lambda a: a.reshape(-1, LANES)
    from2, to2, slot2, sus2, chg2, rate2, base2 = map(
        tab, (branch_from, branch_to, bus_slot, susceptance, charging, rating, base_angles)
    )
    i32 = lambda *s: jax.ShapeDtypeStruct(s, jnp.int32)
    f32 = lambda *s: jax.ShapeDtypeStruct(s, jnp.float32)

    flat = zinv.reshape(buses // 8, 8, cols // LANES, LANES).transpose(0, 2, 1, 3).reshape(-1, LANES)
    square = lax.dynamic_slice(zinv, (me * cols, 0), (cols, cols))
    diag = jnp.sum(jnp.where(jnp.eye(cols, dtype=bool), square, 0.0), axis=0)
    diag = tab(lax.all_gather(diag, "col", tiled=True))
    ids = lax.dynamic_update_slice(jnp.zeros((total,), jnp.int32), outages, (me * own,))
    ids = lax.psum(tab(ids), "col")

    head, tail, _, state, cross = pl.pallas_call(
        functools.partial(ends_kernel, cols),
        name="ends",
        out_shape=[i32(2, blocks, LANES), i32(2, blocks, LANES), i32(blocks, LANES),
                   f32(4, blocks, LANES), i32(blocks, LANES)],
        in_specs=[SMEM] + [VMEM] * 8,
        out_specs=[VMEM] * 5,
        scratch_shapes=[pltpu.SMEM((blocks, LANES), jnp.int32), pltpu.VMEM((LANES, LANES), jnp.float32),
                        pltpu.VMEM((blocks, LANES), jnp.int32), pltpu.SemaphoreType.DMA],
        compiler_params=params(24),
    )(where, ids, from2, to2, slot2, sus2, chg2, base2, flat)
    cross = lax.psum(cross, "col")

    injections, deviation, *units = pl.pallas_call(
        spread_kernel,
        name="spread",
        out_shape=[f32(2, blocks, LANES), f32(total, cols)] + [f32(cols, LANES)] * chips,
        in_specs=[SMEM] * 3 + [VMEM] * 7,
        out_specs=[VMEM] * (2 + chips),
        scratch_shapes=[pltpu.VMEM((cols // LANES, LANES, LANES), jnp.float32)] * 2,
        compiler_params=params(32),
    )(where, head, tail, head, tail, state, cross, diag, base2, flat)

    half = from2.shape[0] // 2
    f_rel, t_rel, ratio = pl.pallas_call(
        prep_kernel,
        name="prep",
        out_shape=[i32(half, LANES), i32(half, LANES), f32(half, LANES)],
        in_specs=[SMEM] + [VMEM] * 5,
        out_specs=[VMEM] * 3,
        cost_estimate=pl.CostEstimate(flops=10**9, bytes_accessed=10**6, transcendentals=0),
    )(where, from2, to2, slot2, sus2, rate2)

    far = sorted(range(1, chips), reverse=True)
    got = {0: units[0]}
    for d in far:
        got[d] = lax.ppermute(units[d], "col", [(i, i ^ (2 * d)) for i in range(n_col)])
    pieces = []
    for d in range(chips):
        pieces.append(got[d])
        pieces.append(lax.ppermute(got[d], "col", [(i, i ^ 1) for i in range(n_col)]))

    worst = pl.pallas_call(
        worst_kernel,
        name="worst",
        out_shape=f32(1, LANES),
        in_specs=[SMEM] * 3 + [VMEM] * 2 + [ANY] * n_col,
        out_specs=VMEM,
        scratch_shapes=[pltpu.VMEM((buses, LANES), jnp.float32), pltpu.VMEM((LANES, LANES), jnp.float32),
                        pltpu.VMEM((8, LANES), jnp.float32), pltpu.SemaphoreType.DMA((n_col,))],
        compiler_params=params(16),
    )(where, f_rel, t_rel, ratio, ids, *pieces)
    other = lax.ppermute(worst, "col", [(i, i ^ 1) for i in range(n_col)])
    worst = lax.dynamic_slice(jnp.maximum(worst, other)[0], ((me & 1) * own,), (own,))
    inj = lax.dynamic_slice(injections.reshape(2, total), (0, me * own), (2, own))
    return inj, deviation, worst


def solution(mesh):
    return jax.shard_map(
        per_device,
        mesh=mesh,
        in_specs=(P(("parts", "col")), P(), P(), P(), P(), P(), P(), P("parts"), P(None, "col")),
        out_specs=(P(None, ("parts", "col")), P("parts", "col"), P(("parts", "col"))),
        check_vma=False,
    )
```

time: 638 us -> 161 us (0.25)
  local copies, waits for them, and re-layouts: 452 us -> 21.7 us
  waiting for transfers between devices: 85.4 us -> 9.67 us
  other arithmetic: 71.8 us -> 1.36 us
  Pallas kernels: 0 us -> 45.8 us
  blocking collectives: 8.74 us -> 36.5 us
  starting transfers between devices: 15.8 us -> 42.9 us
    gather x26 -> x0, local copies, waits for them, and re-layouts: 417 us -> none  [the longest x1 113 us: per_device(): to_slot = bus_slot[branch_to]]
    all_to_all x2 -> x0, waiting for transfers between devices: 85.4 us -> none  [the longest x1 85.4 us: per_device(): lax.all_to_all(pieces, 'col', split_axis=0, concat_axis=2, tiled=True)]
    reduce_max x6 -> x0, other arithmetic: 58.8 us -> none  [the longest x5 58.3 us: one_block(): return jnp.max(load, axis=0)]
    pallas_call x0 -> x4, Pallas kernels: none -> 45.8 us  [the longest x1 19.4 us: per_device(): pl.pallas_call(worst_kernel, name='worst', out_shape=f32(1, LANES), in_sp...]
    ppermute x0 -> x16, starting transfers between devices: none -> 42.9 us  [the longest x8 34.3 us: per_device(): lax.ppermute(got[d], 'col', [(i, i ^ 1) for i in range(n_col)])]
    all_gather x0 -> x1, blocking collectives: none -> 19.3 us  [per_device(): diag = tab(lax.all_gather(diag, 'col', tiled=True))]
    psum x0 -> x2, blocking collectives: none -> 17.2 us  [the longest x1 8.75 us: per_device(): ids = lax.psum(tab(ids), 'col')]
    all_to_all x2 -> x0, starting transfers between devices: 15.8 us -> none  [the longest x1 8.73 us: per_device(): lax.all_to_all(pieces, 'col', split_axis=0, concat_axis=2, tiled=True)]
  transfers between devices with their start and end apart: 2 -> 16, of which waited for: 1 -> 2; matrix products, arithmetic and copies ran while one was open for 33% -> 0% of each run, Pallas kernels for 0% -> 4%
where the time goes in v1:
time: 161 us; the launch traced here: 159 us
  Pallas kernels  45.8 us (28%)
  starting transfers between devices  42.9 us (27%)
  blocking collectives  36.5 us (23%)
  local copies, waits for them, and re-layouts  21.7 us (13%)
  waiting for transfers between devices  9.67 us (6%)
    ppermute x8, starting transfers between devices, per_device(): lax.ppermute(got[d], 'col', [(i, i ^ 1) for i in range(n_col)])  34.3 us
    unnamed x29, local copies, waits for them, and re-layouts  19.6 us
    pallas_call x1, Pallas kernels, per_device(): pl.pallas_call(worst_kernel, name='worst', out_shape=f32(1, LANES), in_sp...  19.4 us
    all_gather x1, blocking collectives, per_device(): diag = tab(lax.all_gather(diag, 'col', tiled=True))  19.3 us
    pallas_call x1, Pallas kernels, per_device(): pl.pallas_call(spread_kernel, name='spread', out_shape=[f32(2, blocks, LA...  11.7 us
    ppermute x7, waiting for transfers between devices, per_device(): lax.ppermute(units[d], 'col', [(i, i ^ 2 * d) for i in range(n_col)])  9.46 us
    psum x1, blocking collectives, per_device(): ids = lax.psum(tab(ids), 'col')  8.75 us
    psum x1, blocking collectives, per_device(): cross = lax.psum(cross, 'col')  8.48 us
  transfers between devices with their start and end apart: 16, of which 2 were waited for; matrix products, arithmetic and copies ran while one was open for 0% of the time, Pallas kernels for 4%

profile of v1, /device:TPU:9, one launch (start us, length us, event | category | flops | bytes accessed | tf_op | source)
XLA Modules:
  0.0 158.6 jit_solution(16797108759006236270)
XLA Ops:
  0.6 0.0 copy-start.3
  0.7 0.9 dynamic_update_slice.3
  1.5 8.7 %psum.14.ids_ref = s32[8,128]{1,0:T(8,128)S(1)} all-reduce(s32[8,128]{1,0:T(8,128)S(1)} %bitcast.37), channel_id=1, replica_groups=mesh['parts'=2,'col'=16] {'col'}, use_global_device_ids=true, to_apply=%region_0.1 | all-reduce | flops 1024 | bytes 8192 | tf_op jit(solution)/shard_map/psum | solution.py:228
  10.3 1.3 select_reduce_fusion
  11.6 19.3 %all-gather = f32[16,1,512]{2,1,0:T(1,128)S(1)} all-gather(f32[1,1,512]{2,1,0:T(1,128)S(1)} %bitcast.39), channel_id=1, replica_groups=mesh['parts'=2,'col'=16] {'col'}, dimensions={0}, use_global_device_ids=true | all-gather | bytes 34816 | tf_op jit(solution)/shard_map/all_gather | solution.py:226
  30.8 0.1 pad_add_fusion.me_ref
  30.9 5.8 %copy-done = f32[8192,512]{1,0:T(8,128)S(1)} copy-done((f32[8192,512]{1,0:T(8,128)S(1)}, f32[8192,512]{1,0:T(8,128)}, u32[]{:S(2)}) %copy-start) | copy-done | bytes 16777240
  36.7 0.8 copy-done.2
  37.4 0.9 copy-done.4
  38.3 0.9 copy-done.5
  39.2 0.9 copy-done.6
  40.1 0.9 copy-done.7
  41.0 0.8 copy-done.11
  41.7 8.2 %ends.1 = (s32[2,8,128]{2,1,0:T(8,128)S(1)}, s32[2,8,128]{2,1,0:T(8,128)S(1)}, s32[8,128]{1,0:T(8,128)}, f32[4,8,128]{2,1,0:T(8,128)S(1)}, s32[8,128]{1,0:T(8,128)S(1)}) custom-call(s32[2]{0:T(128)S(1)} %pad_add_fusion.me_ref, s32[8,128]{1,0:T(8,128)S(1)} %psum.14.ids_ref, s32[160,128]{1,0:T(8,128)S(1)} %bitcast.29, s32[160,128]{1,0:T(8,128)S(1)} %bitcast.31, ...), custom_call_target="tpu_custom_call" | custom-call | tf_op jit(solution)/shard_map/ends/pallas_call | solution.py:230
  49.9 8.5 %psum.15.cross_ref = s32[8,128]{1,0:T(8,128)S(1)} all-reduce(s32[8,128]{1,0:T(8,128)S(1)} %get-tuple-element.23), channel_id=1, replica_groups=mesh['parts'=2,'col'=16] {'col'}, use_global_device_ids=true, to_apply=%region_1.2 | all-reduce | flops 1024 | bytes 8192 | tf_op jit(solution)/shard_map/psum | solution.py:241
  58.4 5.8 %copy-done.1 = f32[8192,512]{1,0:T(8,128)S(1)} copy-done((f32[8192,512]{1,0:T(8,128)S(1)}, f32[8192,512]{1,0:T(8,128)}, u32[]{:S(2)}) %copy-start.1) | copy-done | bytes 16777240
  64.2 11.7 %spread.1 = (f32[2,8,128]{2,1,0:T(8,128)S(1)}, f32[1024,512]{1,0:T(8,128)}, f32[512,128]{1,0:T(8,128)S(1)}, f32[512,128]{1,0:T(8,128)S(1)}, f32[512,128]{1,0:T(8...) custom-call(s32[2]{0:T(128)S(1)} %pad_add_fusion.me_ref, ...), custom_call_target="tpu_custom_call" | custom-call | tf_op jit(solution)/shard_map/spread/pallas_call | solution.py:243
  75.9 0.6 collective-permute-start.1
  76.5 0.5 collective-permute-start.3
  77.0 1.6 collective-permute-start.5
  78.5 2.6 %collective-permute-start.7 = (f32[512,128]{1,0:T(8,128)S(1)}, f32[512,128]{1,0:T(8,128)S(1)}, u32[]{:S(2)}, u32[]{:S(2)}) collective-permute-start(f32[512,128]{1,0:T(8,128)S(1)} %get-tuple-element.33), channel_id=1, source_target_pairs={{0,8},{1,9},{2,10},{3,11},{4,12},{5,13},{6,14},{7,15},{8,0},{9,1},... | collective-permute-start | bytes 786440 | tf_op jit(solution)/shard_map/ppermute | solution.py:266
  81.2 0.3 collective-permute-start.9
  81.5 0.0 collective-permute-done.1.rest_2_
  81.5 1.2 collective-permute-start.11
  82.6 0.0 collective-permute-done.3.rest_4_
  82.7 1.4 collective-permute-start.13
  84.0 9.4 %collective-permute-done.5.rest_6_ = f32[512,128]{1,0:T(8,128)S(1)} collective-permute-done((f32[512,128]{1,0:T(8,128)S(1)}, f32[512,128]{1,0:T(8,128)S(1)}, u32[]{:S(2)}, u32[]{:S(2)}) %collective-permute-start.5) | collective-permute-done | bytes 262176 | tf_op jit(solution)/shard_map/ppermute | solution.py:266
  93.5 4.2 %collective-permute-start = (f32[512,128]{1,0:T(8,128)S(1)}, f32[512,128]{1,0:T(8,128)S(1)}, u32[]{:S(2)}, u32[]{:S(2)}) collective-permute-start(f32[512,128]{1,0:T(8,128)S(1)} %get-tuple-element.29.rest_0_), channel_id=1, source_target_pairs={{0,1},{1,0},{2,3},{3,2},{4,5},{5,4},{6,7},{7,6},{8,9},{9,8},{10,11... | collective-permute-start | bytes 786440 | tf_op jit(solution)/shard_map/ppermute | solution.py:270
  97.6 0.0 collective-permute-done.7.rest_8_
  97.6 16.7 %collective-permute-start.2 = (f32[512,128]{1,0:T(8,128)S(1)}, f32[512,128]{1,0:T(8,128)S(1)}, u32[]{:S(2)}, u32[]{:S(2)}) collective-permute-start(f32[512,128]{1,0:T(8,128)S(1)} %collective-permute-done.1.rest_2_), channel_id=1, source_target_pairs={{0,1},{1,0},{2,3},{3,2},{4,5},{5,4},{6,7},{7,6},{8,9},{9,8},{10,11... | collective-permute-start | bytes 786440 | tf_op jit(solution)/shard_map/ppermute | solution.py:270
  114.3 5.6 %collective-permute-start.4 = (f32[512,128]{1,0:T(8,128)S(1)}, f32[512,128]{1,0:T(8,128)S(1)}, u32[]{:S(2)}, u32[]{:S(2)}) collective-permute-start(f32[512,128]{1,0:T(8,128)S(1)} %collective-permute-done.3.rest_4_), channel_id=1, source_target_pairs={{0,1},{1,0},{2,3},{3,2},{4,5},{5,4},{6,7},{7,6},{8,9},{9,8},{10,11... | collective-permute-start | bytes 786440 | tf_op jit(solution)/shard_map/ppermute | solution.py:270
  119.9 0.0 collective-permute-done.11.rest_12_
  119.9 4.4 %collective-permute-start.6 = (f32[512,128]{1,0:T(8,128)S(1)}, f32[512,128]{1,0:T(8,128)S(1)}, u32[]{:S(2)}, u32[]{:S(2)}) collective-permute-start(f32[512,128]{1,0:T(8,128)S(1)} %collective-permute-done.5.rest_6_), channel_id=1, source_target_pairs={{0,1},{1,0},{2,3},{3,2},{4,5},{5,4},{6,7},{7,6},{8,9},{9,8},{10,11... | collective-permute-start | bytes 786440 | tf_op jit(solution)/shard_map/ppermute | solution.py:270
  124.3 0.0 collective-permute-done.13.rest_14_
  124.3 2.8 %collective-permute-start.8 = (f32[512,128]{1,0:T(8,128)S(1)}, f32[512,128]{1,0:T(8,128)S(1)}, u32[]{:S(2)}, u32[]{:S(2)}) collective-permute-start(f32[512,128]{1,0:T(8,128)S(1)} %collective-permute-done.7.rest_8_), channel_id=1, source_target_pairs={{0,1},{1,0},{2,3},{3,2},{4,5},{5,4},{6,7},{7,6},{8,9},{9,8},{10,11... | collective-permute-start | bytes 786440 | tf_op jit(solution)/shard_map/ppermute | solution.py:270
  127.2 0.0 collective-permute-start.10
  127.2 0.5 collective-permute-start.12
  127.7 0.1 collective-permute-start.14
  127.8 6.5 %prep.1 = (s32[80,128]{1,0:T(8,128)}, s32[80,128]{1,0:T(8,128)}, f32[80,128]{1,0:T(8,128)}) custom-call(s32[2]{0:T(128)} %copy-done.12, s32[160,128]{1,0:T(8,128)} %bitcast.28, s32[160,128]{1,0:T(8,128)} %bitcast.30, s32[64,128]{1,0:T(8,128)} %bitcast.34, f32[160,128]{1,0:T(8,128)} %bitcast.32, f32[160,128]{1,0:T(8,128)} %bitcast.40), custom_call_target="tpu_custom_call" | custom-call | flops 1000000000 | bytes 1000000 | tf_op jit(solution)/shard_map/prep/pallas_call | solution.py:254
  134.3 0.8 copy-done.8
  135.0 0.8 copy-done.9
  135.8 0.8 copy-done.10
  136.6 0.7 copy-done.13
  137.3 19.4 %worst.1 = f32[1,128]{1,0:T(1,128)S(1)} custom-call(s32[2]{0:T(128)S(1)} %copy-done.13, s32[80,128]{1,0:T(8,128)S(1)} %copy-done.8, s32[80,128]{1,0:T(8,128)S(1)} %copy-done.9, f32[80,128]{1,0:T(8,128)S(1)} %copy-done.10, s32[8,128]{1,0:T(8,128)S(1)} %psum.14.ids_ref, f32[512,128]{1,0:T(8,128)S(1)} %get-tuple-element.29.rest_0_, ...), custom_call_target="tpu_custom_call" | custom-call | tf_op jit(solution)/shard_map/worst/pallas_call | solution.py:272
  156.7 0.5 collective-permute-start.15
  157.2 0.6 constant_dynamic-slice_fusion.1
  157.8 0.2 collective-permute-done.15
  158.0 0.6 fusion
  (27 shorter events, 0.1 us)
Async XLA Ops:
  0.6 57.8 %copy-start.3 = (f32[8192]{0:T(1024)S(1)}, f32[8192]{0:T(1024)}, u32[]{:S(2)}) copy-start(f32[8192]{0:T(1024)} %param.16) | copy-start | bytes 98308
  30.9 45.0 %copy-start.12 = (s32[2]{0:T(128)}, s32[2]{0:T(128)S(1)}, u32[]{:S(2)}) copy-start(s32[2]{0:T(128)S(1)} %pad_add_fusion.me_ref) | copy-start | bytes 28
  30.9 5.8 %copy-start = (f32[8192,512]{1,0:T(8,128)S(1)}, f32[8192,512]{1,0:T(8,128)}, u32[]{:S(2)}) copy-start(f32[8192,512]{1,0:T(8,128)} %param.17) | copy-start | bytes 50331652
  36.7 0.8 copy-start.2
  37.4 0.9 copy-start.4
  38.3 0.9 copy-start.5
  39.2 0.9 copy-start.6
  40.1 0.9 copy-start.7
  41.0 0.8 copy-start.11
  58.4 5.8 %copy-start.1 = (f32[8192,512]{1,0:T(8,128)S(1)}, f32[8192,512]{1,0:T(8,128)}, u32[]{:S(2)}) copy-start(f32[8192,512]{1,0:T(8,128)} %param.17) | copy-start | bytes 50331652
  75.9 5.6 %collective-permute-start.1 = (f32[512,128]{1,0:T(8,128)S(1)}, f32[512,128]{1,0:T(8,128)S(1)}, u32[]{:S(2)}, u32[]{:S(2)}) collective-permute-start(f32[512,128]{1,0:T(8,128)S(1)} %get-tuple-element.30), channel_id=1, source_target_pairs={{0,2},{1,3},{2,0},{3,1},{4,6},{5,7},{6,4},{7,5},{8,10},{9,11},{10,... | collective-permute-start | bytes 786440 | tf_op jit(solution)/shard_map/ppermute | solution.py:266
  76.5 6.2 %collective-permute-start.3 = (f32[512,128]{1,0:T(8,128)S(1)}, f32[512,128]{1,0:T(8,128)S(1)}, u32[]{:S(2)}, u32[]{:S(2)}) collective-permute-start(f32[512,128]{1,0:T(8,128)S(1)} %get-tuple-element.31), channel_id=1, source_target_pairs={{0,4},{1,5},{2,6},{3,7},{4,0},{5,1},{6,2},{7,3},{8,12},{9,13},{10,... | collective-permute-start | bytes 786440 | tf_op jit(solution)/shard_map/ppermute | solution.py:266
  77.0 16.5 %collective-permute-start.5 = (f32[512,128]{1,0:T(8,128)S(1)}, f32[512,128]{1,0:T(8,128)S(1)}, u32[]{:S(2)}, u32[]{:S(2)}) collective-permute-start(f32[512,128]{1,0:T(8,128)S(1)} %get-tuple-element.32), channel_id=1, source_target_pairs={{0,6},{1,7},{2,4},{3,5},{4,2},{5,3},{6,0},{7,1},{8,14},{9,15},{10,... | collective-permute-start | bytes 786440 | tf_op jit(solution)/shard_map/ppermute | solution.py:266
  78.5 19.1 %collective-permute-start.7 = (f32[512,128]{1,0:T(8,128)S(1)}, f32[512,128]{1,0:T(8,128)S(1)}, u32[]{:S(2)}, u32[]{:S(2)}) collective-permute-start(f32[512,128]{1,0:T(8,128)S(1)} %get-tuple-element.33), channel_id=1, source_target_pairs={{0,8},{1,9},{2,10},{3,11},{4,12},{5,13},{6,14},{7,15},{8,0},{9,1},... | collective-permute-start | bytes 786440 | tf_op jit(solution)/shard_map/ppermute | solution.py:266
  81.2 33.1 %collective-permute-start.9 = (f32[512,128]{1,0:T(8,128)S(1)}, f32[512,128]{1,0:T(8,128)S(1)}, u32[]{:S(2)}, u32[]{:S(2)}) collective-permute-start(f32[512,128]{1,0:T(8,128)S(1)} %get-tuple-element.34), channel_id=1, source_target_pairs={{0,10},{1,11},{2,8},{3,9},{4,14},{5,15},{6,12},{7,13},{8,2},{9,3},... | collective-permute-start | bytes 786440 | tf_op jit(solution)/shard_map/ppermute | solution.py:266
  81.5 38.5 %collective-permute-start.11 = (f32[512,128]{1,0:T(8,128)S(1)}, f32[512,128]{1,0:T(8,128)S(1)}, u32[]{:S(2)}, u32[]{:S(2)}) collective-permute-start(f32[512,128]{1,0:T(8,128)S(1)} %get-tuple-element.35), channel_id=1, source_target_pairs={{0,12},{1,13},{2,14},{3,15},{4,8},{5,9},{6,10},{7,11},{8,4},{9,5},... | collective-permute-start | bytes 786440 | tf_op jit(solution)/shard_map/ppermute | solution.py:266
  82.7 41.7 %collective-permute-start.13 = (f32[512,128]{1,0:T(8,128)S(1)}, f32[512,128]{1,0:T(8,128)S(1)}, u32[]{:S(2)}, u32[]{:S(2)}) collective-permute-start(f32[512,128]{1,0:T(8,128)S(1)} %get-tuple-element.36), channel_id=1, source_target_pairs={{0,14},{1,15},{2,12},{3,13},{4,10},{5,11},{6,8},{7,9},{8,6},{9,7},... | collective-permute-start | bytes 786440 | tf_op jit(solution)/shard_map/ppermute | solution.py:266
  93.5 33.7 %collective-permute-start = (f32[512,128]{1,0:T(8,128)S(1)}, f32[512,128]{1,0:T(8,128)S(1)}, u32[]{:S(2)}, u32[]{:S(2)}) collective-permute-start(f32[512,128]{1,0:T(8,128)S(1)} %get-tuple-element.29.rest_0_), channel_id=1, source_target_pairs={{0,1},{1,0},{2,3},{3,2},{4,5},{5,4},{6,7},{7,6},{8,9},{9,8},{10,11... | collective-permute-start | bytes 786440 | tf_op jit(solution)/shard_map/ppermute | solution.py:270
  97.6 29.5 %collective-permute-start.2 = (f32[512,128]{1,0:T(8,128)S(1)}, f32[512,128]{1,0:T(8,128)S(1)}, u32[]{:S(2)}, u32[]{:S(2)}) collective-permute-start(f32[512,128]{1,0:T(8,128)S(1)} %collective-permute-done.1.rest_2_), channel_id=1, source_target_pairs={{0,1},{1,0},{2,3},{3,2},{4,5},{5,4},{6,7},{7,6},{8,9},{9,8},{10,11... | collective-permute-start | bytes 786440 | tf_op jit(solution)/shard_map/ppermute | solution.py:270
  114.3 13.4 %collective-permute-start.4 = (f32[512,128]{1,0:T(8,128)S(1)}, f32[512,128]{1,0:T(8,128)S(1)}, u32[]{:S(2)}, u32[]{:S(2)}) collective-permute-start(f32[512,128]{1,0:T(8,128)S(1)} %collective-permute-done.3.rest_4_), channel_id=1, source_target_pairs={{0,1},{1,0},{2,3},{3,2},{4,5},{5,4},{6,7},{7,6},{8,9},{9,8},{10,11... | collective-permute-start | bytes 786440 | tf_op jit(solution)/shard_map/ppermute | solution.py:270
  119.9 14.3 %collective-permute-start.6 = (f32[512,128]{1,0:T(8,128)S(1)}, f32[512,128]{1,0:T(8,128)S(1)}, u32[]{:S(2)}, u32[]{:S(2)}) collective-permute-start(f32[512,128]{1,0:T(8,128)S(1)} %collective-permute-done.5.rest_6_), channel_id=1, source_target_pairs={{0,1},{1,0},{2,3},{3,2},{4,5},{5,4},{6,7},{7,6},{8,9},{9,8},{10,11... | collective-permute-start | bytes 786440 | tf_op jit(solution)/shard_map/ppermute | solution.py:270
  124.3 9.9 %collective-permute-start.8 = (f32[512,128]{1,0:T(8,128)S(1)}, f32[512,128]{1,0:T(8,128)S(1)}, u32[]{:S(2)}, u32[]{:S(2)}) collective-permute-start(f32[512,128]{1,0:T(8,128)S(1)} %collective-permute-done.7.rest_8_), channel_id=1, source_target_pairs={{0,1},{1,0},{2,3},{3,2},{4,5},{5,4},{6,7},{7,6},{8,9},{9,8},{10,11... | collective-permute-start | bytes 786440 | tf_op jit(solution)/shard_map/ppermute | solution.py:270
  127.2 7.1 %collective-permute-start.10 = (f32[512,128]{1,0:T(8,128)S(1)}, f32[512,128]{1,0:T(8,128)}, u32[]{:S(2)}, u32[]{:S(2)}) collective-permute-start(f32[512,128]{1,0:T(8,128)S(1)} %collective-permute-done.9.rest_10_), channel_id=1, source_target_pairs={{0,1},{1,0},{2,3},{3,2},{4,5},{5,4},{6,7},{7,6},{8,9},{9,8},{10,11... | collective-permute-start | bytes 786440 | tf_op jit(solution)/shard_map/ppermute | solution.py:270
  127.2 7.1 %collective-permute-start.12 = (f32[512,128]{1,0:T(8,128)S(1)}, f32[512,128]{1,0:T(8,128)}, u32[]{:S(2)}, u32[]{:S(2)}) collective-permute-start(f32[512,128]{1,0:T(8,128)S(1)} %collective-permute-done.11.rest_12_), channel_id=1, source_target_pairs={{0,1},{1,0},{2,3},{3,2},{4,5},{5,4},{6,7},{7,6},{8,9},{9,8},{10,11... | collective-permute-start | bytes 786440 | tf_op jit(solution)/shard_map/ppermute | solution.py:270
  127.7 6.6 %collective-permute-start.14 = (f32[512,128]{1,0:T(8,128)S(1)}, f32[512,128]{1,0:T(8,128)}, u32[]{:S(2)}, u32[]{:S(2)}) collective-permute-start(f32[512,128]{1,0:T(8,128)S(1)} %collective-permute-done.13.rest_14_), channel_id=1, source_target_pairs={{0,1},{1,0},{2,3},{3,2},{4,5},{5,4},{6,7},{7,6},{8,9},{9,8},{10,11... | collective-permute-start | bytes 786440 | tf_op jit(solution)/shard_map/ppermute | solution.py:270
  134.3 0.8 copy-start.8
  135.0 0.8 copy-start.9
  135.8 0.8 copy-start.10
  136.6 0.7 copy-start.13
  156.7 1.4 collective-permute-start.15

commit v2 on v1

--- a/solution.py
+++ b/solution.py
@@ -10,7 +10,6 @@
 
 STEPS = 3
 LANES = 128
-FIXED = float(2**30)
 SINE = (3.1415926444, -5.1677100819, 2.5500775297, -0.5982913039, 0.0776576582)
 VMEM = pl.BlockSpec(memory_space=pltpu.VMEM)
 SMEM = pl.BlockSpec(memory_space=pltpu.SMEM)
@@ -31,11 +30,11 @@
 
 
 def lookup(pieces, index):
-    rows = pieces[0].shape[0]
+    rows = pieces[0].shape[1]
     n = index.shape[1]
     hot = lax.broadcasted_iota(jnp.int32, (rows, n), 0) == (index >> 7)
     hot = jnp.where(hot, 1.0, 0.0).astype(jnp.bfloat16)
-    dims = (((0,), (0,)), ((), ()))
+    dims = (((1,), (0,)), ((), ()))
     total = sum(lax.dot_general(p, hot, dims, preferred_element_type=jnp.float32) for p in pieces)
     lane = lax.broadcasted_iota(jnp.int32, (LANES, n), 0) == (index & 127)
     return jnp.sum(jnp.where(lane, total, 0.0), axis=0, keepdims=True)
@@ -65,84 +64,99 @@
     return inj_head, inj_tail
 
 
-def ends_kernel(cols, me_ref, ids_ref, from_ref, to_ref, slot_ref, sus_ref, chg_ref, base_ref, zinv_ref,
-                head_ref, tail_ref, pick_ref, state_ref, cross_ref, tile_s, rows, tiles, sem):
+def addresses(row, width):
+    return (row >> 3) * (8 * width) + (row & 7)
+
+
+def stage(pairs, sem):
+    copies = [pltpu.make_async_copy(src, dst, sem.at[i]) for i, (src, dst) in enumerate(pairs)]
+    for copy in copies:
+        copy.start()
+    return copies
+
+
+def ends_kernel(width, me_ref, ids_ref, from_ref, to_ref, slot_ref, sus_ref, chg_ref, base_ref, zinv_ref,
+                state_ref, pick_ref, rows_h, rows_t, from_v, to_v, slot_v, sus_v, chg_v, base_v, zinv_v,
+                ends_v, ends_s, sem):
     blocks = ids_ref.shape[0]
-    width = cols // LANES
-    first = me_ref[0] * cols
-    f_parts = split(from_ref[...].astype(jnp.float32), 2)
-    t_parts = split(to_ref[...].astype(jnp.float32), 2)
-    s_parts = split(slot_ref[...].astype(jnp.float32), 2)
-    sus_parts = split(sus_ref[...], 3)
-    chg_parts = split(chg_ref[...], 3)
-    base_parts = split(base_ref[...], 3)
+    first = me_ref[0] * width * LANES
+    copies = stage([(from_ref, from_v), (to_ref, to_v), (slot_ref, slot_v), (sus_ref, sus_v),
+                    (chg_ref, chg_v), (base_ref, base_v), (zinv_ref, zinv_v)], sem)
+    for copy in copies[:-1]:
+        copy.wait()
+    f_parts = split(from_v[...].astype(jnp.float32).T, 2)
+    t_parts = split(to_v[...].astype(jnp.float32).T, 2)
+    s_parts = split(slot_v[...].astype(jnp.float32).T, 2)
+    sus_parts = split(sus_v[...].T, 3)
+    chg_parts = split(chg_v[...].T, 3)
+    base_parts = split(base_v[...].T, 3)
+    heads, tails = [], []
     for b in range(blocks):
-        row = pl.ds(b, 1)
+        ids = ids_ref[b:b + 1, :]
+        heads.append(lookup(s_parts, lookup(f_parts, ids).astype(jnp.int32)).astype(jnp.int32))
+        tails.append(lookup(s_parts, lookup(t_parts, ids).astype(jnp.int32)).astype(jnp.int32))
+        ends_v[b:b + 1, :] = addresses(heads[b], width)
+        ends_v[blocks + b:blocks + b + 1, :] = addresses(tails[b], width)
+    copy = pltpu.make_async_copy(ends_v, ends_s, sem.at[0])
+    copy.start()
+    for b in range(blocks):
+        row = slice(b, b + 1)
         ids = ids_ref[row, :]
-        head = lookup(s_parts, lookup(f_parts, ids).astype(jnp.int32)).astype(jnp.int32)
-        tail = lookup(s_parts, lookup(t_parts, ids).astype(jnp.int32)).astype(jnp.int32)
-        head_ref[0, row, :] = head
-        tail_ref[0, row, :] = tail
-        head_ref[1, row, :] = (head >> 3) * (8 * width) + (head & 7)
-        tail_ref[1, row, :] = (tail >> 3) * (8 * width) + (tail & 7)
-        state_ref[0, row, :] = lookup(base_parts, head)
-        state_ref[1, row, :] = lookup(base_parts, tail)
+        state_ref[0, row, :] = lookup(base_parts, heads[b])
+        state_ref[1, row, :] = lookup(base_parts, tails[b])
         state_ref[2, row, :] = lookup(sus_parts, ids)
         state_ref[3, row, :] = lookup(chg_parts, ids)
-        pick_ref[row, :] = tail - first
-        column = jnp.clip((tail - first) >> 7, 0, width - 1)
-        tiles[row, :] = (head >> 3) * (8 * width) + (head & 7) + column * 8
-    copy = pltpu.make_async_copy(tiles, tile_s, sem)
-    copy.start()
+        state_ref[4, row, :] = (heads[b] - first).astype(jnp.float32)
+        state_ref[5, row, :] = (tails[b] - first).astype(jnp.float32)
     copy.wait()
+    copies[-1].wait()
 
     def block(b, carry):
-        for j in range(LANES):
-            rows[pl.ds(j, 1), :] = zinv_ref[pl.ds(tile_s[b, j], 1), :]
-        offset = pick_ref[pl.ds(b, 1), :]
-        inside = (offset >= 0) & (offset < cols)
-        hit = lax.broadcasted_iota(jnp.int32, (LANES, LANES), 0) == jnp.where(inside, offset & 127, -1)
-        entry = jnp.sum(jnp.where(hit, rows[...].T, 0.0), axis=0, keepdims=True)
-        cross_ref[pl.ds(b, 1), :] = jnp.round(entry * FIXED).astype(jnp.int32)
+        def fetch(g, carry):
+            for i in range(16):
+                o = g * 16 + i
+                head = ends_s[b, o]
+                tail = ends_s[blocks + b, o]
+                for t in range(width):
+                    rows_h[b, t, pl.ds(o, 1), :] = zinv_v[pl.ds(head + 8 * t, 1), :]
+                    rows_t[b, t, pl.ds(o, 1), :] = zinv_v[pl.ds(tail + 8 * t, 1), :]
+            return carry
+
+        lax.fori_loop(0, LANES // 16, fetch, 0)
+        square = (LANES, LANES)
+        at_h = jnp.broadcast_to(state_ref[4, pl.ds(b, 1), :], square).T
+        at_t = jnp.broadcast_to(state_ref[5, pl.ds(b, 1), :], square).T
+        lane = lax.broadcasted_iota(jnp.int32, square, 1).astype(jnp.float32)
+        hh = ht = tt = jnp.zeros(square, jnp.float32)
+        for t in range(width):
+            is_h = at_h == lane + float(t * LANES)
+            is_t = at_t == lane + float(t * LANES)
+            hh = jnp.where(is_h, rows_h[b, t], hh)
+            ht = jnp.where(is_t, rows_h[b, t], ht)
+            tt = jnp.where(is_t, rows_t[b, t], tt)
+        for i, pick in enumerate((hh, ht, tt)):
+            pick_ref[pl.ds(i * blocks + b, 1), :] = jnp.sum(pick.T, axis=0, keepdims=True)
         return carry
 
     lax.fori_loop(0, blocks, block, 0)
 
 
-def spread_kernel(me_ref, head_s, tail_s, head_ref, tail_ref, state_ref, cross_ref, diag_ref, base_ref,
-                  zinv_ref, inj_ref, dev_ref, *rest):
-    units, (rows_h, rows_t) = rest[:-2], rest[-2:]
-    blocks, cols = cross_ref.shape[0], units[0].shape[0]
-    tiles = cols // LANES
+def spread_kernel(me_ref, state_ref, pick_ref, base_ref, rows_h, rows_t, inj_ref, dev_ref, *units):
+    blocks, width = rows_h.shape[:2]
     me = me_ref[0]
-    chip = me >> 1
-    d_parts = split(diag_ref[...], 3)
-    self_h = [lookup(d_parts, head_ref[0, pl.ds(b, 1), :]) for b in range(blocks)]
-    self_t = [lookup(d_parts, tail_ref[0, pl.ds(b, 1), :]) for b in range(blocks)]
-    cross = cross_ref[...].astype(jnp.float32) * (1.0 / FIXED)
-    inj_h, inj_t = newton(state_ref[0], state_ref[1], jnp.concatenate(self_h, 0), cross,
-                          jnp.concatenate(self_t, 0), state_ref[2], state_ref[3])
+    inj_h, inj_t = newton(state_ref[0], state_ref[1], pick_ref[:blocks], pick_ref[blocks:2 * blocks],
+                          pick_ref[2 * blocks:], state_ref[2], state_ref[3])
     inj_ref[0] = inj_h
     inj_ref[1] = inj_t
     for d, unit in enumerate(units):
-        blk = chip ^ d
-
-        def fetch(j, carry):
-            for i in range(16):
-                o = j * 16 + i
-                for t in range(tiles):
-                    rows_h[t, pl.ds(o, 1), :] = zinv_ref[pl.ds(head_s[1, blk, o] + 8 * t, 1), :]
-                    rows_t[t, pl.ds(o, 1), :] = zinv_ref[pl.ds(tail_s[1, blk, o] + 8 * t, 1), :]
-            return carry
-
-        lax.fori_loop(0, LANES // 16, fetch, 0)
+        blk = (me >> 1) ^ d
         scale_h = jnp.broadcast_to(inj_ref[0, pl.ds(blk, 1), :], (LANES, LANES)).T
         scale_t = jnp.broadcast_to(inj_ref[1, pl.ds(blk, 1), :], (LANES, LANES)).T
-        for t in range(tiles):
+        for t in range(width):
             at = slice(t * LANES, (t + 1) * LANES)
-            dev = scale_h * rows_h[t] + scale_t * rows_t[t]
+            dev = scale_h * rows_h[blk, t] + scale_t * rows_t[blk, t]
             dev_ref[pl.ds(pl.multiple_of(blk * LANES, LANES), LANES), at] = dev
-            angle = base_ref[pl.ds(me * tiles + t, 1), :] + dev
+            angle = base_ref[pl.ds(me * width + t, 1), :] + dev
             unit[at, :] = (angle * (1.0 / math.pi)).T
 
 
@@ -151,7 +165,7 @@
     me = me_ref[0]
     start = (me & 1) * half
     flip = me * (slot_ref.shape[0] * LANES // me_ref[1])
-    s_parts = split(slot_ref[...].astype(jnp.float32), 2)
+    s_parts = split(slot_ref[...].astype(jnp.float32).T, 2)
 
     def group(g, carry):
         for i in range(8):
@@ -221,34 +235,37 @@
     f32 = lambda *s: jax.ShapeDtypeStruct(s, jnp.float32)
 
     flat = zinv.reshape(buses // 8, 8, cols // LANES, LANES).transpose(0, 2, 1, 3).reshape(-1, LANES)
-    square = lax.dynamic_slice(zinv, (me * cols, 0), (cols, cols))
-    diag = jnp.sum(jnp.where(jnp.eye(cols, dtype=bool), square, 0.0), axis=0)
-    diag = tab(lax.all_gather(diag, "col", tiled=True))
     ids = lax.dynamic_update_slice(jnp.zeros((total,), jnp.int32), outages, (me * own,))
     ids = lax.psum(tab(ids), "col")
 
-    head, tail, _, state, cross = pl.pallas_call(
-        functools.partial(ends_kernel, cols),
+    width = cols // LANES
+    like = lambda a: pltpu.VMEM(a.shape, a.dtype)
+    state, picks, rows_h, rows_t = pl.pallas_call(
+        functools.partial(ends_kernel, width),
         name="ends",
-        out_shape=[i32(2, blocks, LANES), i32(2, blocks, LANES), i32(blocks, LANES),
-                   f32(4, blocks, LANES), i32(blocks, LANES)],
-        in_specs=[SMEM] + [VMEM] * 8,
-        out_specs=[VMEM] * 5,
-        scratch_shapes=[pltpu.SMEM((blocks, LANES), jnp.int32), pltpu.VMEM((LANES, LANES), jnp.float32),
-                        pltpu.VMEM((blocks, LANES), jnp.int32), pltpu.SemaphoreType.DMA],
-        compiler_params=params(24),
+        out_shape=[f32(6, blocks, LANES), f32(3 * blocks, LANES)] + [f32(blocks, width, LANES, LANES)] * 2,
+        in_specs=[SMEM, VMEM] + [ANY] * 7,
+        out_specs=[VMEM] * 4,
+        scratch_shapes=[like(from2), like(to2), like(slot2), like(sus2), like(chg2), like(base2), like(flat),
+                        pltpu.VMEM((2 * blocks, LANES), jnp.int32), pltpu.SMEM((2 * blocks, LANES), jnp.int32),
+                        pltpu.SemaphoreType.DMA((7,))],
+        compiler_params=params(48),
     )(where, ids, from2, to2, slot2, sus2, chg2, base2, flat)
-    cross = lax.psum(cross, "col")
+
+    swap = lambda a, m: lax.ppermute(a, "col", [(i, i ^ m) for i in range(n_col)])
+    step = 1
+    while step < n_col:
+        picks = sum([swap(picks, m * step) for m in range(1, min(4, n_col // step))], picks)
+        step *= 4
 
     injections, deviation, *units = pl.pallas_call(
         spread_kernel,
         name="spread",
         out_shape=[f32(2, blocks, LANES), f32(total, cols)] + [f32(cols, LANES)] * chips,
-        in_specs=[SMEM] * 3 + [VMEM] * 7,
+        in_specs=[SMEM] + [VMEM] * 5,
         out_specs=[VMEM] * (2 + chips),
-        scratch_shapes=[pltpu.VMEM((cols // LANES, LANES, LANES), jnp.float32)] * 2,
         compiler_params=params(32),
-    )(where, head, tail, head, tail, state, cross, diag, base2, flat)
+    )(where, state, picks, base2, rows_h, rows_t)
 
     half = from2.shape[0] // 2
     f_rel, t_rel, ratio = pl.pallas_call(
@@ -263,11 +280,11 @@
     far = sorted(range(1, chips), reverse=True)
     got = {0: units[0]}
     for d in far:
-        got[d] = lax.ppermute(units[d], "col", [(i, i ^ (2 * d)) for i in range(n_col)])
+        got[d] = swap(units[d], 2 * d)
     pieces = []
     for d in range(chips):
         pieces.append(got[d])
-        pieces.append(lax.ppermute(got[d], "col", [(i, i ^ 1) for i in range(n_col)]))
+        pieces.append(swap(got[d], 1))
 
     worst = pl.pallas_call(
         worst_kernel,
@@ -279,7 +296,7 @@
                         pltpu.VMEM((8, LANES), jnp.float32), pltpu.SemaphoreType.DMA((n_col,))],
         compiler_params=params(16),
     )(where, f_rel, t_rel, ratio, ids, *pieces)
-    other = lax.ppermute(worst, "col", [(i, i ^ 1) for i in range(n_col)])
+    other = swap(worst, 1)
     worst = lax.dynamic_slice(jnp.maximum(worst, other)[0], ((me & 1) * own,), (own,))
     inj = lax.dynamic_slice(injections.reshape(2, total), (0, me * own), (2, own))
     return inj, deviation, worst

time: 161 us -> 128 us (0.80)
  blocking collectives: 36.5 us -> 8.75 us
  local copies, waits for them, and re-layouts: 21.7 us -> 9.48 us
  starting transfers between devices: 42.9 us -> 49 us
  waiting for transfers between devices: 9.67 us -> 15.7 us
  Pallas kernels: 45.8 us -> 42.7 us
    all_gather x1 -> x0, blocking collectives: 19.3 us -> none  [per_device(): diag = tab(lax.all_gather(diag, 'col', tiled=True))]
    unnamed x29 -> x23, local copies, waits for them, and re-layouts: 19.6 us -> 7.4 us
    pallas_call x1, Pallas kernels: 11.7 us -> 3.07 us  [per_device(): pl.pallas_call(spread_kernel, name='spread', out_shape=[f32(2, blocks, LA...]
    psum x1 -> x0, blocking collectives: 8.48 us -> none  [per_device(): cross = lax.psum(cross, 'col')]
    ppermute x16 -> x22, waiting for transfers between devices: 9.67 us -> 15.7 us  [per_device(): lax.ppermute(a, 'col', [(i, i ^ m) for i in range(n_col)])]
    ppermute x16 -> x22, starting transfers between devices: 42.9 us -> 49 us  [per_device(): lax.ppermute(a, 'col', [(i, i ^ m) for i in range(n_col)])]
    pallas_call x1, Pallas kernels: 8.2 us -> 14.2 us  [per_device(): pl.pallas_call(functools.partial(ends_kernel, width), name='ends', out_sh...]
  transfers between devices with their start and end apart: 16 -> 22, of which waited for: 2 -> 5; matrix products, arithmetic and copies ran while one was open for 0% -> 1% of each run, Pallas kernels for 4% -> 5%
where the time goes in v2:
time: 128 us; the launch traced here: 126 us
  starting transfers between devices  49 us (38%)
  Pallas kernels  42.7 us (33%)
  waiting for transfers between devices  15.7 us (12%)
  local copies, waits for them, and re-layouts  9.48 us (7%)
  blocking collectives  8.75 us (7%)
    ppermute x22, starting transfers between devices, per_device(): lax.ppermute(a, 'col', [(i, i ^ m) for i in range(n_col)])  49 us
    pallas_call x1, Pallas kernels, per_device(): pl.pallas_call(worst_kernel, name='worst', out_shape=f32(1, LANES), in_sp...  19.4 us
    ppermute x22, waiting for transfers between devices, per_device(): lax.ppermute(a, 'col', [(i, i ^ m) for i in range(n_col)])  15.7 us
    pallas_call x1, Pallas kernels, per_device(): pl.pallas_call(functools.partial(ends_kernel, width), name='ends', out_sh...  14.2 us
    psum x1, blocking collectives, per_device(): ids = lax.psum(tab(ids), 'col')  8.75 us
    unnamed x23, local copies, waits for them, and re-layouts  7.4 us
    pallas_call x1, Pallas kernels, per_device(): pl.pallas_call(prep_kernel, name='prep', out_shape=[i32(half, LANES), i32...  6.13 us
    pallas_call x1, Pallas kernels, per_device(): pl.pallas_call(spread_kernel, name='spread', out_shape=[f32(2, blocks, LA...  3.07 us
  transfers between devices with their start and end apart: 22, of which 5 were waited for; matrix products, arithmetic and copies ran while one was open for 1% of the time, Pallas kernels for 5%

profile of v2, /device:TPU:9, one launch (start us, length us, event | category | flops | bytes accessed | tf_op | source)
XLA Modules:
  0.0 126.5 jit_solution(9301618613448349542)
XLA Ops:
  0.6 0.9 dynamic_update_slice.3
  1.5 8.7 %psum.7.ids_ref = s32[8,128]{1,0:T(8,128)S(1)} all-reduce(s32[8,128]{1,0:T(8,128)S(1)} %bitcast.33), channel_id=1, replica_groups=mesh['parts'=2,'col'=16] {'col'}, use_global_device_ids=true, to_apply=%region_0.0 | all-reduce | flops 1024 | bytes 8192 | tf_op jit(solution)/shard_map/psum | solution.py:239
  10.3 0.1 pad_add_fusion.me_ref
  10.3 0.8 copy-done
  11.1 0.9 copy-done.1
  12.0 0.9 copy-done.2
  12.9 0.9 copy-done.3
  13.8 0.9 copy-done.4
  14.6 0.8 copy-done.8
  15.4 14.2 %ends.1 = (f32[6,8,128]{2,1,0:T(8,128)S(1)}, f32[24,128]{1,0:T(8,128)S(1)}, f32[8,4,128,128]{3,2,1,0:T(8,128)S(1)}, f32[8,4,128,128]{3,2,1,0:T(8,128)S(1)}) custom-call(s32[2]{0:T(128)S(1)} %pad_add_fusion.me_ref, s32[8,128]{1,0:T(8,128)S(1)} %psum.7.ids_ref, s32[160,128]{1,0:T(8,128)S(1)} %bitcast.24, s32[160,128]{1,0:T(8,128)S(1)} %bitcast.26, ...), custom_call_target="tpu_custom_call" | custom-call | tf_op jit(solution)/shard_map/ends/pallas_call | solution.py:243
  29.6 3.2 %collective-permute-start = (f32[24,128]{1,0:T(8,128)S(1)}, f32[24,128]{1,0:T(8,128)S(1)}, u32[]{:S(2)}, u32[]{:S(2)}) collective-permute-start(f32[24,128]{1,0:T(8,128)S(1)} %get-tuple-element.21), channel_id=1, source_target_pairs={{0,1},{1,0},{2,3},{3,2},{4,5},{5,4},{6,7},{7,6},{8,9},{9,8},{10,11... | collective-permute-start | bytes 36872 | tf_op jit(solution)/shard_map/ppermute | solution.py:255
  32.7 0.6 collective-permute-start.1
  33.3 1.1 collective-permute-start.2
  34.4 0.8 collective-permute-done.1
  35.3 1.1 collective-permute-done.2
  36.4 1.3 %collective-permute-start.3 = (f32[24,128]{1,0:T(8,128)S(1)}, f32[24,128]{1,0:T(8,128)S(1)}, u32[]{:S(2)}, u32[]{:S(2)}) collective-permute-start(f32[24,128]{1,0:T(8,128)S(1)} %add_add_fusion.1), channel_id=1, source_target_pairs={{0,4},{1,5},{2,6},{3,7},{4,0},{5,1},{6,2},{7,3},{8,12},{9,13},{10,... | collective-permute-start | bytes 36872 | tf_op jit(solution)/shard_map/ppermute | solution.py:255
  37.7 0.1 collective-permute-start.4
  37.8 1.3 %collective-permute-start.5 = (f32[24,128]{1,0:T(8,128)S(1)}, f32[24,128]{1,0:T(8,128)S(1)}, u32[]{:S(2)}, u32[]{:S(2)}) collective-permute-start(f32[24,128]{1,0:T(8,128)S(1)} %add_add_fusion.1), channel_id=1, source_target_pairs={{0,12},{1,13},{2,14},{3,15},{4,8},{5,9},{6,10},{7,11},{8,4},{9,5},... | collective-permute-start | bytes 36872 | tf_op jit(solution)/shard_map/ppermute | solution.py:255
  39.1 0.0 collective-permute-done.3
  39.1 2.1 %collective-permute-done.4 = f32[24,128]{1,0:T(8,128)S(1)} collective-permute-done((f32[24,128]{1,0:T(8,128)S(1)}, f32[24,128]{1,0:T(8,128)S(1)}, u32[]{:S(2)}, u32[]{:S(2)}) %collective-permute-start.4) | collective-permute-done | bytes 12320 | tf_op jit(solution)/shard_map/ppermute | solution.py:255
  41.2 0.0 collective-permute-done.5
  41.2 3.1 %spread.1 = (f32[2,8,128]{2,1,0:T(8,128)S(1)}, f32[1024,512]{1,0:T(8,128)}, f32[512,128]{1,0:T(8,128)S(1)}, f32[512,128]{1,0:T(8,128)S(1)}, f32[512,128]{1,0:T(8...) custom-call(s32[2]{0:T(128)S(1)} %pad_add_fusion.me_ref, ...), custom_call_target="tpu_custom_call" | custom-call | tf_op jit(solution)/shard_map/spread/pallas_call | solution.py:261
  44.3 1.3 %collective-permute-start.9 = (f32[512,128]{1,0:T(8,128)S(1)}, f32[512,128]{1,0:T(8,128)S(1)}, u32[]{:S(2)}, u32[]{:S(2)}) collective-permute-start(f32[512,128]{1,0:T(8,128)S(1)} %get-tuple-element.31), channel_id=1, source_target_pairs={{0,4},{1,5},{2,6},{3,7},{4,0},{5,1},{6,2},{7,3},{8,12},{9,13},{10,... | collective-permute-start | bytes 786440 | tf_op jit(solution)/shard_map/ppermute | solution.py:255
  45.6 0.7 collective-permute-start.11
  46.3 3.3 %collective-permute-start.13 = (f32[512,128]{1,0:T(8,128)S(1)}, f32[512,128]{1,0:T(8,128)S(1)}, u32[]{:S(2)}, u32[]{:S(2)}) collective-permute-start(f32[512,128]{1,0:T(8,128)S(1)} %get-tuple-element.33), channel_id=1, source_target_pairs={{0,8},{1,9},{2,10},{3,11},{4,12},{5,13},{6,14},{7,15},{8,0},{9,1},... | collective-permute-start | bytes 786440 | tf_op jit(solution)/shard_map/ppermute | solution.py:255
  49.6 0.3 collective-permute-start.15
  49.9 1.2 collective-permute-start.17
  51.1 0.0 collective-permute-done.9.rest_4_
  51.1 1.9 %collective-permute-start.19 = (f32[512,128]{1,0:T(8,128)S(1)}, f32[512,128]{1,0:T(8,128)S(1)}, u32[]{:S(2)}, u32[]{:S(2)}) collective-permute-start(f32[512,128]{1,0:T(8,128)S(1)} %get-tuple-element.36), channel_id=1, source_target_pairs={{0,14},{1,15},{2,12},{3,13},{4,10},{5,11},{6,8},{7,9},{8,6},{9,7},... | collective-permute-start | bytes 786440 | tf_op jit(solution)/shard_map/ppermute | solution.py:255
  53.0 11.2 %collective-permute-done.11.rest_6_ = f32[512,128]{1,0:T(8,128)S(1)} collective-permute-done((f32[512,128]{1,0:T(8,128)S(1)}, f32[512,128]{1,0:T(8,128)S(1)}, u32[]{:S(2)}, u32[]{:S(2)}) %collective-permute-start.11) | collective-permute-done | bytes 262176 | tf_op jit(solution)/shard_map/ppermute | solution.py:255
  64.1 1.0 collective-permute-start.7
  65.2 16.6 %collective-permute-start.6 = (f32[512,128]{1,0:T(8,128)S(1)}, f32[512,128]{1,0:T(8,128)S(1)}, u32[]{:S(2)}, u32[]{:S(2)}) collective-permute-start(f32[512,128]{1,0:T(8,128)S(1)} %get-tuple-element.29.rest_0_), channel_id=1, source_target_pairs={{0,1},{1,0},{2,3},{3,2},{4,5},{5,4},{6,7},{7,6},{8,9},{9,8},{10,11... | collective-permute-start | bytes 786440 | tf_op jit(solution)/shard_map/ppermute | solution.py:255
  81.7 5.6 %collective-permute-start.10 = (f32[512,128]{1,0:T(8,128)S(1)}, f32[512,128]{1,0:T(8,128)S(1)}, u32[]{:S(2)}, u32[]{:S(2)}) collective-permute-start(f32[512,128]{1,0:T(8,128)S(1)} %collective-permute-done.9.rest_4_), channel_id=1, source_target_pairs={{0,1},{1,0},{2,3},{3,2},{4,5},{5,4},{6,7},{7,6},{8,9},{9,8},{10,11... | collective-permute-start | bytes 786440 | tf_op jit(solution)/shard_map/ppermute | solution.py:255
  87.3 5.3 %collective-permute-start.12 = (f32[512,128]{1,0:T(8,128)S(1)}, f32[512,128]{1,0:T(8,128)S(1)}, u32[]{:S(2)}, u32[]{:S(2)}) collective-permute-start(f32[512,128]{1,0:T(8,128)S(1)} %collective-permute-done.11.rest_6_), channel_id=1, source_target_pairs={{0,1},{1,0},{2,3},{3,2},{4,5},{5,4},{6,7},{7,6},{8,9},{9,8},{10,11... | collective-permute-start | bytes 786440 | tf_op jit(solution)/shard_map/ppermute | solution.py:255
  92.7 3.1 %collective-permute-start.14 = (f32[512,128]{1,0:T(8,128)S(1)}, f32[512,128]{1,0:T(8,128)S(1)}, u32[]{:S(2)}, u32[]{:S(2)}) collective-permute-start(f32[512,128]{1,0:T(8,128)S(1)} %collective-permute-done.13.rest_8_), channel_id=1, source_target_pairs={{0,1},{1,0},{2,3},{3,2},{4,5},{5,4},{6,7},{7,6},{8,9},{9,8},{10,11... | collective-permute-start | bytes 786440 | tf_op jit(solution)/shard_map/ppermute | solution.py:255
  95.8 0.0 collective-permute-start.16
  95.8 0.5 collective-permute-start.18
  96.3 0.1 collective-permute-start.20
  96.4 0.4 collective-permute-start.8
  96.8 6.1 %prep.1 = (s32[80,128]{1,0:T(8,128)}, s32[80,128]{1,0:T(8,128)}, f32[80,128]{1,0:T(8,128)}) custom-call(s32[2]{0:T(128)} %copy-done.9, s32[160,128]{1,0:T(8,128)} %bitcast.23, s32[160,128]{1,0:T(8,128)} %bitcast.25, s32[64,128]{1,0:T(8,128)} %bitcast.29, f32[160,128]{1,0:T(8,128)} %bitcast.27, f32[160,128]{1,0:T(8,128)} %bitcast.35), custom_call_target="tpu_custom_call" | custom-call | flops 1000000000 | bytes 1000000 | tf_op jit(solution)/shard_map/prep/pallas_call | solution.py:271
  103.0 0.8 copy-done.5
  103.8 0.8 copy-done.6
  104.6 0.8 copy-done.7
  105.3 19.4 %worst.1 = f32[1,128]{1,0:T(1,128)S(1)} custom-call(s32[2]{0:T(128)S(1)} %copy-done.10, s32[80,128]{1,0:T(8,128)S(1)} %copy-done.5, s32[80,128]{1,0:T(8,128)S(1)} %copy-done.6, f32[80,128]{1,0:T(8,128)S(1)} %copy-done.7, s32[8,128]{1,0:T(8,128)S(1)} %psum.7.ids_ref, f32[512,128]{1,0:T(8,128)S(1)} %get-tuple-element.29.rest_0_, ...), custom_call_target="tpu_custom_call" | custom-call | tf_op jit(solution)/shard_map/worst/pallas_call | solution.py:289
  124.7 0.1 collective-permute-start.21
  124.8 0.6 constant_dynamic-slice_fusion
  125.4 0.5 collective-permute-done.21
  125.9 0.6 dynamic-slice_bitcast_fusion
  (32 shorter events, 0.1 us)
Async XLA Ops:
  10.3 30.9 %copy-start.9 = (s32[2]{0:T(128)}, s32[2]{0:T(128)S(1)}, u32[]{:S(2)}) copy-start(s32[2]{0:T(128)S(1)} %pad_add_fusion.me_ref) | copy-start | bytes 28
  10.3 0.8 copy-start
  11.1 0.9 copy-start.1
  12.0 0.9 copy-start.2
  12.9 0.9 copy-start.3
  13.8 0.9 copy-start.4
  14.6 0.8 copy-start.8
  29.6 4.9 %collective-permute-start = (f32[24,128]{1,0:T(8,128)S(1)}, f32[24,128]{1,0:T(8,128)S(1)}, u32[]{:S(2)}, u32[]{:S(2)}) collective-permute-start(f32[24,128]{1,0:T(8,128)S(1)} %get-tuple-element.21), channel_id=1, source_target_pairs={{0,1},{1,0},{2,3},{3,2},{4,5},{5,4},{6,7},{7,6},{8,9},{9,8},{10,11... | collective-permute-start | bytes 36872 | tf_op jit(solution)/shard_map/ppermute | solution.py:255
  32.7 2.6 %collective-permute-start.1 = (f32[24,128]{1,0:T(8,128)S(1)}, f32[24,128]{1,0:T(8,128)S(1)}, u32[]{:S(2)}, u32[]{:S(2)}) collective-permute-start(f32[24,128]{1,0:T(8,128)S(1)} %get-tuple-element.21), channel_id=1, source_target_pairs={{0,2},{1,3},{2,0},{3,1},{4,6},{5,7},{6,4},{7,5},{8,10},{9,11},{10,... | collective-permute-start | bytes 36872 | tf_op jit(solution)/shard_map/ppermute | solution.py:255
  33.3 3.1 %collective-permute-start.2 = (f32[24,128]{1,0:T(8,128)S(1)}, f32[24,128]{1,0:T(8,128)S(1)}, u32[]{:S(2)}, u32[]{:S(2)}) collective-permute-start(f32[24,128]{1,0:T(8,128)S(1)} %get-tuple-element.21), channel_id=1, source_target_pairs={{0,3},{1,2},{2,1},{3,0},{4,7},{5,6},{6,5},{7,4},{8,11},{9,10},{10,... | collective-permute-start | bytes 36872 | tf_op jit(solution)/shard_map/ppermute | solution.py:255
  36.4 2.7 %collective-permute-start.3 = (f32[24,128]{1,0:T(8,128)S(1)}, f32[24,128]{1,0:T(8,128)S(1)}, u32[]{:S(2)}, u32[]{:S(2)}) collective-permute-start(f32[24,128]{1,0:T(8,128)S(1)} %add_add_fusion.1), channel_id=1, source_target_pairs={{0,4},{1,5},{2,6},{3,7},{4,0},{5,1},{6,2},{7,3},{8,12},{9,13},{10,... | collective-permute-start | bytes 36872 | tf_op jit(solution)/shard_map/ppermute | solution.py:255
  37.7 3.4 %collective-permute-start.4 = (f32[24,128]{1,0:T(8,128)S(1)}, f32[24,128]{1,0:T(8,128)S(1)}, u32[]{:S(2)}, u32[]{:S(2)}) collective-permute-start(f32[24,128]{1,0:T(8,128)S(1)} %add_add_fusion.1), channel_id=1, source_target_pairs={{0,8},{1,9},{2,10},{3,11},{4,12},{5,13},{6,14},{7,15},{8,0},{9,1},... | collective-permute-start | bytes 36872 | tf_op jit(solution)/shard_map/ppermute | solution.py:255
  37.8 3.4 %collective-permute-start.5 = (f32[24,128]{1,0:T(8,128)S(1)}, f32[24,128]{1,0:T(8,128)S(1)}, u32[]{:S(2)}, u32[]{:S(2)}) collective-permute-start(f32[24,128]{1,0:T(8,128)S(1)} %add_add_fusion.1), channel_id=1, source_target_pairs={{0,12},{1,13},{2,14},{3,15},{4,8},{5,9},{6,10},{7,11},{8,4},{9,5},... | collective-permute-start | bytes 36872 | tf_op jit(solution)/shard_map/ppermute | solution.py:255
  44.3 58.7 %copy-start.10 = (s32[2]{0:T(128)S(1)}, s32[2]{0:T(128)}, u32[]{:S(2)}) copy-start(s32[2]{0:T(128)} %copy-done.9) | copy-start | bytes 28
  44.3 6.8 %collective-permute-start.9 = (f32[512,128]{1,0:T(8,128)S(1)}, f32[512,128]{1,0:T(8,128)S(1)}, u32[]{:S(2)}, u32[]{:S(2)}) collective-permute-start(f32[512,128]{1,0:T(8,128)S(1)} %get-tuple-element.31), channel_id=1, source_target_pairs={{0,4},{1,5},{2,6},{3,7},{4,0},{5,1},{6,2},{7,3},{8,12},{9,13},{10,... | collective-permute-start | bytes 786440 | tf_op jit(solution)/shard_map/ppermute | solution.py:255
  45.6 18.5 %collective-permute-start.11 = (f32[512,128]{1,0:T(8,128)S(1)}, f32[512,128]{1,0:T(8,128)S(1)}, u32[]{:S(2)}, u32[]{:S(2)}) collective-permute-start(f32[512,128]{1,0:T(8,128)S(1)} %get-tuple-element.32), channel_id=1, source_target_pairs={{0,6},{1,7},{2,4},{3,5},{4,2},{5,3},{6,0},{7,1},{8,14},{9,15},{10,... | collective-permute-start | bytes 786440 | tf_op jit(solution)/shard_map/ppermute | solution.py:255
  46.3 18.8 %collective-permute-start.13 = (f32[512,128]{1,0:T(8,128)S(1)}, f32[512,128]{1,0:T(8,128)S(1)}, u32[]{:S(2)}, u32[]{:S(2)}) collective-permute-start(f32[512,128]{1,0:T(8,128)S(1)} %get-tuple-element.33), channel_id=1, source_target_pairs={{0,8},{1,9},{2,10},{3,11},{4,12},{5,13},{6,14},{7,15},{8,0},{9,1},... | collective-permute-start | bytes 786440 | tf_op jit(solution)/shard_map/ppermute | solution.py:255
  49.6 32.1 %collective-permute-start.15 = (f32[512,128]{1,0:T(8,128)S(1)}, f32[512,128]{1,0:T(8,128)S(1)}, u32[]{:S(2)}, u32[]{:S(2)}) collective-permute-start(f32[512,128]{1,0:T(8,128)S(1)} %get-tuple-element.34), channel_id=1, source_target_pairs={{0,10},{1,11},{2,8},{3,9},{4,14},{5,15},{6,12},{7,13},{8,2},{9,3},... | collective-permute-start | bytes 786440 | tf_op jit(solution)/shard_map/ppermute | solution.py:255
  49.9 37.4 %collective-permute-start.17 = (f32[512,128]{1,0:T(8,128)S(1)}, f32[512,128]{1,0:T(8,128)S(1)}, u32[]{:S(2)}, u32[]{:S(2)}) collective-permute-start(f32[512,128]{1,0:T(8,128)S(1)} %get-tuple-element.35), channel_id=1, source_target_pairs={{0,12},{1,13},{2,14},{3,15},{4,8},{5,9},{6,10},{7,11},{8,4},{9,5},... | collective-permute-start | bytes 786440 | tf_op jit(solution)/shard_map/ppermute | solution.py:255
  51.1 41.6 %collective-permute-start.19 = (f32[512,128]{1,0:T(8,128)S(1)}, f32[512,128]{1,0:T(8,128)S(1)}, u32[]{:S(2)}, u32[]{:S(2)}) collective-permute-start(f32[512,128]{1,0:T(8,128)S(1)} %get-tuple-element.36), channel_id=1, source_target_pairs={{0,14},{1,15},{2,12},{3,13},{4,10},{5,11},{6,8},{7,9},{8,6},{9,7},... | collective-permute-start | bytes 786440 | tf_op jit(solution)/shard_map/ppermute | solution.py:255
  64.1 31.6 %collective-permute-start.7 = (f32[512,128]{1,0:T(8,128)S(1)}, f32[512,128]{1,0:T(8,128)S(1)}, u32[]{:S(2)}, u32[]{:S(2)}) collective-permute-start(f32[512,128]{1,0:T(8,128)S(1)} %get-tuple-element.30), channel_id=1, source_target_pairs={{0,2},{1,3},{2,0},{3,1},{4,6},{5,7},{6,4},{7,5},{8,10},{9,11},{10,... | collective-permute-start | bytes 786440 | tf_op jit(solution)/shard_map/ppermute | solution.py:255
  65.2 30.6 %collective-permute-start.6 = (f32[512,128]{1,0:T(8,128)S(1)}, f32[512,128]{1,0:T(8,128)S(1)}, u32[]{:S(2)}, u32[]{:S(2)}) collective-permute-start(f32[512,128]{1,0:T(8,128)S(1)} %get-tuple-element.29.rest_0_), channel_id=1, source_target_pairs={{0,1},{1,0},{2,3},{3,2},{4,5},{5,4},{6,7},{7,6},{8,9},{9,8},{10,11... | collective-permute-start | bytes 786440 | tf_op jit(solution)/shard_map/ppermute | solution.py:255
  81.7 14.6 %collective-permute-start.10 = (f32[512,128]{1,0:T(8,128)S(1)}, f32[512,128]{1,0:T(8,128)S(1)}, u32[]{:S(2)}, u32[]{:S(2)}) collective-permute-start(f32[512,128]{1,0:T(8,128)S(1)} %collective-permute-done.9.rest_4_), channel_id=1, source_target_pairs={{0,1},{1,0},{2,3},{3,2},{4,5},{5,4},{6,7},{7,6},{8,9},{9,8},{10,11... | collective-permute-start | bytes 786440 | tf_op jit(solution)/shard_map/ppermute | solution.py:255
  87.3 9.0 %collective-permute-start.12 = (f32[512,128]{1,0:T(8,128)S(1)}, f32[512,128]{1,0:T(8,128)S(1)}, u32[]{:S(2)}, u32[]{:S(2)}) collective-permute-start(f32[512,128]{1,0:T(8,128)S(1)} %collective-permute-done.11.rest_6_), channel_id=1, source_target_pairs={{0,1},{1,0},{2,3},{3,2},{4,5},{5,4},{6,7},{7,6},{8,9},{9,8},{10,11... | collective-permute-start | bytes 786440 | tf_op jit(solution)/shard_map/ppermute | solution.py:255
  92.7 10.3 %collective-permute-start.14 = (f32[512,128]{1,0:T(8,128)S(1)}, f32[512,128]{1,0:T(8,128)S(1)}, u32[]{:S(2)}, u32[]{:S(2)}) collective-permute-start(f32[512,128]{1,0:T(8,128)S(1)} %collective-permute-done.13.rest_8_), channel_id=1, source_target_pairs={{0,1},{1,0},{2,3},{3,2},{4,5},{5,4},{6,7},{7,6},{8,9},{9,8},{10,11... | collective-permute-start | bytes 786440 | tf_op jit(solution)/shard_map/ppermute | solution.py:255
  95.8 7.2 %collective-permute-start.16 = (f32[512,128]{1,0:T(8,128)S(1)}, f32[512,128]{1,0:T(8,128)S(1)}, u32[]{:S(2)}, u32[]{:S(2)}) collective-permute-start(f32[512,128]{1,0:T(8,128)S(1)} %collective-permute-done.15.rest_10_), channel_id=1, source_target_pairs={{0,1},{1,0},{2,3},{3,2},{4,5},{5,4},{6,7},{7,6},{8,9},{9,8},{10,11... | collective-permute-start | bytes 786440 | tf_op jit(solution)/shard_map/ppermute | solution.py:255
  95.8 7.2 %collective-permute-start.18 = (f32[512,128]{1,0:T(8,128)S(1)}, f32[512,128]{1,0:T(8,128)}, u32[]{:S(2)}, u32[]{:S(2)}) collective-permute-start(f32[512,128]{1,0:T(8,128)S(1)} %collective-permute-done.17.rest_12_), channel_id=1, source_target_pairs={{0,1},{1,0},{2,3},{3,2},{4,5},{5,4},{6,7},{7,6},{8,9},{9,8},{10,11... | collective-permute-start | bytes 786440 | tf_op jit(solution)/shard_map/ppermute | solution.py:255
  96.3 6.7 %collective-permute-start.20 = (f32[512,128]{1,0:T(8,128)S(1)}, f32[512,128]{1,0:T(8,128)}, u32[]{:S(2)}, u32[]{:S(2)}) collective-permute-start(f32[512,128]{1,0:T(8,128)S(1)} %collective-permute-done.19.rest_14_), channel_id=1, source_target_pairs={{0,1},{1,0},{2,3},{3,2},{4,5},{5,4},{6,7},{7,6},{8,9},{9,8},{10,11... | collective-permute-start | bytes 786440 | tf_op jit(solution)/shard_map/ppermute | solution.py:255
  96.4 6.6 %collective-permute-start.8 = (f32[512,128]{1,0:T(8,128)S(1)}, f32[512,128]{1,0:T(8,128)}, u32[]{:S(2)}, u32[]{:S(2)}) collective-permute-start(f32[512,128]{1,0:T(8,128)S(1)} %collective-permute-done.7.rest_2_), channel_id=1, source_target_pairs={{0,1},{1,0},{2,3},{3,2},{4,5},{5,4},{6,7},{7,6},{8,9},{9,8},{10,11... | collective-permute-start | bytes 786440 | tf_op jit(solution)/shard_map/ppermute | solution.py:255
  103.0 0.8 copy-start.5
  103.8 0.8 copy-start.6
  104.6 0.8 copy-start.7
  124.7 1.2 collective-permute-start.21

commit v3 on v2

--- a/solution.py
+++ b/solution.py
@@ -10,10 +10,16 @@
 
 STEPS = 3
 LANES = 128
+GROUP = 4
 SINE = (3.1415926444, -5.1677100819, 2.5500775297, -0.5982913039, 0.0776576582)
 VMEM = pl.BlockSpec(memory_space=pltpu.VMEM)
 SMEM = pl.BlockSpec(memory_space=pltpu.SMEM)
 ANY = pl.BlockSpec(memory_space=pl.ANY)
+HBM = pl.BlockSpec(memory_space=pltpu.HBM)
+
+
+def cost(micros):
+    return pl.CostEstimate(flops=micros * 10**9, bytes_accessed=10**6, transcendentals=0)
 
 
 def params(mib):
@@ -160,40 +166,104 @@
             unit[at, :] = (angle * (1.0 / math.pi)).T
 
 
-def prep_kernel(me_ref, from_ref, to_ref, slot_ref, sus_ref, rate_ref, f_ref, t_ref, ratio_ref):
+def prep_kernel(unit, mid, last, me_ref, from_ref, to_ref, slot_ref, sus_ref, rate_ref,
+                f_ref, t_ref, ratio_ref, k_ref, cnt_ref, from_v, to_v, slot_v, sus_v, rate_v, sem):
+    copies = stage([(from_ref, from_v), (to_ref, to_v), (slot_ref, slot_v), (sus_ref, sus_v),
+                    (rate_ref, rate_v)], sem)
+    for copy in copies:
+        copy.wait()
     half = f_ref.shape[0]
     me = me_ref[0]
     start = (me & 1) * half
-    flip = me * (slot_ref.shape[0] * LANES // me_ref[1])
-    s_parts = split(slot_ref[...].astype(jnp.float32).T, 2)
+    flip = me * unit
+    shift = (2 * unit).bit_length() - 1
+    s_parts = split(slot_v[...].astype(jnp.float32).T, 2)
+    square = (LANES, LANES)
+    before = lax.broadcasted_iota(jnp.int32, square, 0) < lax.broadcasted_iota(jnp.int32, square, 1)
+    before = jnp.where(before, 1.0, 0.0).astype(jnp.bfloat16)
+    lane = lax.broadcasted_iota(jnp.int32, (1, LANES), 1).astype(jnp.float32)
+    slots = lax.broadcasted_iota(jnp.int32, (GROUP * LANES, LANES), 0).astype(jnp.float32)
 
     def group(g, carry):
-        for i in range(8):
-            row = pl.ds(start + g * 8 + i, 1)
-            out = pl.ds(g * 8 + i, 1)
-            f_ref[out, :] = lookup(s_parts, from_ref[row, :]).astype(jnp.int32) ^ flip
-            t_ref[out, :] = lookup(s_parts, to_ref[row, :]).astype(jnp.int32) ^ flip
-            ratio_ref[out, :] = sus_ref[row, :] / rate_ref[row, :]
+        fs, ts, ratios, first, second = [], [], [], [], []
+        for i in range(GROUP):
+            row = pl.ds(start + g * GROUP + i, 1)
+            f = lookup(s_parts, from_v[row, :]).astype(jnp.int32) ^ flip
+            t = lookup(s_parts, to_v[row, :]).astype(jnp.int32) ^ flip
+            fs.append(f)
+            ts.append(t)
+            ratios.append(sus_v[row, :] / rate_v[row, :])
+            f_chip, t_chip = f >> shift, t >> shift
+            late = (f_chip == last) | (t_chip == last)
+            middle = ((f_chip == mid) | (t_chip == mid)) & jnp.logical_not(late)
+            first.append(jnp.where(late | middle, 0.0, 1.0))
+            second.append(jnp.where(middle, 1.0, 0.0))
+        flags = jnp.concatenate(first + second, 0)
+        ahead = jnp.dot(flags.astype(jnp.bfloat16), before, preferred_element_type=jnp.float32)
+        sums = jnp.sum(flags, axis=1, keepdims=True)
+        n_first = sum(sums[i:i + 1] for i in range(GROUP))
+        n_second = sum(sums[GROUP + i:GROUP + i + 1] for i in range(GROUP))
+        off_first = off_second = jnp.zeros((1, 1), jnp.float32)
+        total = jnp.zeros((16, GROUP * LANES), jnp.float32)
+        for i in range(GROUP):
+            c_first = off_first + ahead[i:i + 1]
+            c_second = off_second + ahead[GROUP + i:GROUP + i + 1]
+            rest = n_first + n_second + (lane + float(i * LANES)) - c_first - c_second
+            place = jnp.where(first[i] > 0.5, c_first, jnp.where(second[i] > 0.5, n_first + c_second, rest))
+            off_first = off_first + sums[i:i + 1]
+            off_second = off_second + sums[GROUP + i:GROUP + i + 1]
+            hot = jnp.where(slots == place, 1.0, 0.0).astype(jnp.bfloat16)
+            high, low = fs[i] >> 7, fs[i] & 127
+            rows = [high, low, ts[i] >> 7, ts[i] & 127]
+            rows = [r.astype(jnp.float32) for r in rows]
+            rows += [p.astype(jnp.float32) for p in split(ratios[i], 3)]
+            rows += [jnp.full((1, LANES), float(i)), lane] + [jnp.zeros((1, LANES), jnp.float32)] * 7
+            values = jnp.concatenate(rows, 0).astype(jnp.bfloat16)
+            total += lax.dot_general(values, hot, (((1,), (1,)), ((), ())), preferred_element_type=jnp.float32)
+        for i in range(GROUP):
+            out = pl.ds(g * GROUP + i, 1)
+            part = total[:, i * LANES:(i + 1) * LANES]
+            f_ref[out, :] = (part[0:1] * 128.0 + part[1:2]).astype(jnp.int32)
+            t_ref[out, :] = (part[2:3] * 128.0 + part[3:4]).astype(jnp.int32)
+            ratio_ref[out, :] = part[4:5] + part[5:6] + part[6:7]
+            origin = ((start + g * GROUP) * LANES).astype(jnp.float32)
+            k_ref[out, :] = part[7:8] * 128.0 + part[8:9] + origin
+        wide = lambda a: jnp.broadcast_to(a, (1, LANES)).astype(jnp.int32) >> 7
+        cnt_ref[0, pl.ds(g, 1), :] = wide(n_first)
+        cnt_ref[1, pl.ds(g, 1), :] = wide(n_first + n_second)
         return carry
 
-    lax.fori_loop(0, half // 8, group, 0)
-
-
-def worst_kernel(me_ref, f_s, t_s, ratio_ref, ids_ref, *rest):
-    pieces, (out_ref, table, diff, best, sem) = rest[:-5], rest[-5:]
-    unit = pieces[0].shape[0]
-    copies = []
-    for i, piece in enumerate(pieces):
-        copy = pltpu.make_async_copy(piece, table.at[pl.ds(i * unit, unit)], sem.at[i])
-        copy.start()
-        copies.append(copy)
+    lax.fori_loop(0, half // GROUP, group, 0)
+
+
+def gate_kernel(*refs):
+    pass
+
+
+def gate(value, *after):
+    return pl.pallas_call(
+        gate_kernel,
+        name="gate",
+        out_shape=jax.ShapeDtypeStruct(value.shape, value.dtype),
+        in_specs=[ANY] * (1 + len(after)),
+        out_specs=ANY,
+        input_output_aliases={0: 0},
+    )(value, *after)
+
+
+def worst_kernel(level, places, me_ref, f_ref, t_ref, cnt_ref, ratio_ref, k_ref, ids_ref, *rest):
+    if level:
+        best_in, _, *rest = rest
+    n = len(places)
+    pieces, (best, table, f_s, t_s, cnt_s, diff, sem) = rest[:n], rest[n:]
+    pairs = [(f_ref, f_s), (t_ref, t_s), (cnt_ref, cnt_s)]
+    pairs += [(p, table.at[pl.ds(i * p.shape[0], p.shape[0])]) for p, i in zip(pieces, places)]
+    copies = stage(pairs, sem)
+    half = f_ref.shape[0]
+    ids = ids_ref[pl.ds(me_ref[0] >> 1, 1), :].astype(jnp.float32)
+    best[...] = best_in[...] if level else jnp.zeros_like(best)
     for copy in copies:
         copy.wait()
-    half = f_s.shape[0]
-    me = me_ref[0]
-    ids = ids_ref[pl.ds(me >> 1, 1), :]
-    start = (me & 1) * half
-    best[...] = jnp.zeros_like(best)
 
     def block(b, carry):
         for j in range(LANES):
@@ -205,14 +275,19 @@
         for c in SINE[3::-1]:
             poly = poly * square + c
         ratio = jnp.broadcast_to(ratio_ref[pl.ds(b, 1), :], (LANES, LANES)).T
-        load = jnp.abs(turn * poly) * ratio
-        branch = lax.broadcasted_iota(jnp.int32, (LANES, LANES), 0) + (start + b) * LANES
-        load = jnp.where(branch == ids, 0.0, load)
+        branch = jnp.broadcast_to(k_ref[pl.ds(b, 1), :], (LANES, LANES)).T
+        load = jnp.where(branch == ids, 0.0, jnp.abs(turn * poly) * ratio)
         best[...] = jnp.maximum(best[...], jnp.max(load.reshape(LANES // 8, 8, LANES), axis=0))
         return carry
 
-    lax.fori_loop(0, half, block, 0)
-    out_ref[...] = jnp.max(best[...], axis=0, keepdims=True)
+    def group(g, carry):
+        low = 0 if level == 0 else cnt_s[level - 1, g, 0]
+        high = GROUP if level == 2 else cnt_s[level, g, 0]
+        return lax.fori_loop(g * GROUP + low, g * GROUP + high, block, carry)
+
+    lax.fori_loop(0, half // GROUP, group, 0)
+    if level == 2:
+        best[...] = jnp.broadcast_to(jnp.max(best[...], axis=0, keepdims=True), best.shape)
 
 
 def per_device(
@@ -244,7 +319,7 @@
         functools.partial(ends_kernel, width),
         name="ends",
         out_shape=[f32(6, blocks, LANES), f32(3 * blocks, LANES)] + [f32(blocks, width, LANES, LANES)] * 2,
-        in_specs=[SMEM, VMEM] + [ANY] * 7,
+        in_specs=[SMEM, VMEM] + [HBM] * 7,
         out_specs=[VMEM] * 4,
         scratch_shapes=[like(from2), like(to2), like(slot2), like(sus2), like(chg2), like(base2), like(flat),
                         pltpu.VMEM((2 * blocks, LANES), jnp.int32), pltpu.SMEM((2 * blocks, LANES), jnp.int32),
@@ -268,36 +343,51 @@
     )(where, state, picks, base2, rows_h, rows_t)
 
     half = from2.shape[0] // 2
-    f_rel, t_rel, ratio = pl.pallas_call(
-        prep_kernel,
+    near = list(range(1, chips // 2))
+    *far, mid, last = range(chips // 2, chips)
+    f_rel, t_rel, ratio, k_rel, counts = pl.pallas_call(
+        functools.partial(prep_kernel, cols, mid, last),
         name="prep",
-        out_shape=[i32(half, LANES), i32(half, LANES), f32(half, LANES)],
-        in_specs=[SMEM] + [VMEM] * 5,
-        out_specs=[VMEM] * 3,
-        cost_estimate=pl.CostEstimate(flops=10**9, bytes_accessed=10**6, transcendentals=0),
+        out_shape=[i32(half, LANES), i32(half, LANES), f32(half, LANES), f32(half, LANES),
+                   i32(2, half // GROUP, LANES)],
+        in_specs=[SMEM] + [HBM] * 5,
+        out_specs=[VMEM] * 5,
+        scratch_shapes=[like(from2), like(to2), like(slot2), like(sus2), like(rate2),
+                        pltpu.SemaphoreType.DMA((5,))],
+        compiler_params=params(16),
+        cost_estimate=cost(12),
     )(where, from2, to2, slot2, sus2, rate2)
 
-    far = sorted(range(1, chips), reverse=True)
     got = {0: units[0]}
-    for d in far:
+    for d in far + near:
         got[d] = swap(units[d], 2 * d)
-    pieces = []
-    for d in range(chips):
-        pieces.append(got[d])
-        pieces.append(swap(got[d], 1))
-
-    worst = pl.pallas_call(
-        worst_kernel,
-        name="worst",
-        out_shape=f32(1, LANES),
-        in_specs=[SMEM] * 3 + [VMEM] * 2 + [ANY] * n_col,
-        out_specs=VMEM,
-        scratch_shapes=[pltpu.VMEM((buses, LANES), jnp.float32), pltpu.VMEM((LANES, LANES), jnp.float32),
-                        pltpu.VMEM((8, LANES), jnp.float32), pltpu.SemaphoreType.DMA((n_col,))],
-        compiler_params=params(16),
-    )(where, f_rel, t_rel, ratio, ids, *pieces)
-    other = swap(worst, 1)
-    worst = lax.dynamic_slice(jnp.maximum(worst, other)[0], ((me & 1) * own,), (own,))
+    between = swap(gate(units[mid], got[far[0]], counts), 2 * mid)
+    arrived = swap(gate(units[last], got[far[-1]]), 2 * last)
+
+    def worst_stage(level, ds, *carried):
+        places = [2 * d + e for d in ds for e in (0, 1)]
+        pieces = [p for d in ds for p in (got[d], swap(got[d], 1))]
+        return pl.pallas_call(
+            functools.partial(worst_kernel, level, places),
+            name=f"worst{level}",
+            out_shape=[f32(8, LANES), f32(buses, LANES)],
+            in_specs=[SMEM] + [HBM] * 3 + [VMEM] * (3 + len(carried)) + [ANY] * len(pieces),
+            out_specs=[VMEM] * 2,
+            scratch_shapes=[pltpu.SMEM(f_rel.shape, jnp.int32), pltpu.SMEM(t_rel.shape, jnp.int32),
+                            pltpu.SMEM(counts.shape, jnp.int32), pltpu.VMEM((LANES, LANES), jnp.float32),
+                            pltpu.SemaphoreType.DMA((3 + len(pieces),))],
+            input_output_aliases={7 + i: i for i in range(len(carried))},
+            compiler_params=params(16),
+            cost_estimate=cost((9, 4, 4)[level]),
+        )(where, f_rel, t_rel, counts, ratio, k_rel, ids, *carried, *pieces)
+
+    best, table = worst_stage(0, [0] + near + far)
+    got[mid] = gate(between, best)
+    best, table = worst_stage(1, [mid], best, table)
+    got[last] = gate(arrived, best)
+    best, _ = worst_stage(2, [last], best, table)
+    worst = lax.slice(best, (0, 0), (1, LANES))
+    worst = lax.dynamic_slice(jnp.maximum(worst, swap(worst, 1))[0], ((me & 1) * own,), (own,))
     inj = lax.dynamic_slice(injections.reshape(2, total), (0, me * own), (2, own))
     return inj, deviation, worst
 

time: 128 us -> 146 us (1.14)
  the two profiles are of different devices: /device:TPU:9 before, /device:TPU:0 now
where the time goes in v3:
time: 146 us; the launch traced here: 145 us
  Pallas kernels  57.8 us (40%)
  local copies, waits for them, and re-layouts  27.4 us (19%)
  waiting for transfers between devices  26.4 us (18%)
  starting transfers between devices  19 us (13%)
  blocking collectives  13.7 us (9%)
    ppermute x22, waiting for transfers between devices, per_device(): lax.ppermute(a, 'col', [(i, i ^ m) for i in range(n_col)])  26.4 us
    unnamed x71, local copies, waits for them, and re-layouts  25.3 us
    pallas_call x3, Pallas kernels, worst_stage(): pl.pallas_call(functools.partial(worst_kernel, level, places), name=f'wor...  24.9 us
    ppermute x22, starting transfers between devices, per_device(): lax.ppermute(a, 'col', [(i, i ^ m) for i in range(n_col)])  19 us
    pallas_call x1, Pallas kernels, per_device(): pl.pallas_call(functools.partial(prep_kernel, cols, mid, last), name='pre...  15.7 us
    pallas_call x1, Pallas kernels, per_device(): pl.pallas_call(functools.partial(ends_kernel, width), name='ends', out_sh...  14.1 us
    psum x1, blocking collectives, per_device(): ids = lax.psum(tab(ids), 'col')  13.7 us
    pallas_call x1, Pallas kernels, per_device(): pl.pallas_call(spread_kernel, name='spread', out_shape=[f32(2, blocks, LA...  3.05 us
  transfers between devices with their start and end apart: 22, of which 10 were waited for; matrix products, arithmetic and copies ran while one was open for 0% of the time, Pallas kernels for 22%

profile of v3, /device:TPU:0, one launch (start us, length us, event | category | flops | bytes accessed | tf_op | source)
XLA Modules:
  0.0 145.3 jit_solution(17850495730812006560)
XLA Ops:
  0.6 0.9 dynamic_update_slice.3
  1.5 13.7 %psum.7.ids_ref = s32[8,128]{1,0:T(8,128)S(1)} all-reduce(s32[8,128]{1,0:T(8,128)S(1)} %bitcast.34), channel_id=1, replica_groups=mesh['parts'=2,'col'=16] {'col'}, use_global_device_ids=true, to_apply=%region_0.0 | all-reduce | flops 1024 | bytes 8192 | tf_op jit(solution)/shard_map/psum | solution.py:314
  15.3 0.8 copy-done.9
  16.1 0.9 copy-done.10
  17.0 0.9 copy-done.11
  17.9 0.9 copy-done.12
  18.7 0.9 copy-done.13
  19.6 0.8 copy-done.14
  20.4 14.1 %ends.1 = (f32[6,8,128]{2,1,0:T(8,128)S(1)}, f32[24,128]{1,0:T(8,128)S(1)}, f32[8,4,128,128]{3,2,1,0:T(8,128)S(1)}, f32[8,4,128,128]{3,2,1,0:T(8,128)S(1)}) custom-call(s32[2]{0:T(128)S(1)} %pad_add_fusion.me_ref, s32[8,128]{1,0:T(8,128)S(1)} %psum.7.ids_ref, s32[160,128]{1,0:T(8,128)S(1)} %bitcast.23, s32[160,128]{1,0:T(8,128)S(1)} %bitcast.25, ...), custom_call_target="tpu_custom_call" | custom-call | tf_op jit(solution)/shard_map/ends/pallas_call | solution.py:318
  34.6 0.9 collective-permute-start.1
  35.5 0.9 collective-permute-start
  36.5 1.3 collective-permute-done.2
  37.7 0.7 collective-permute-done.1
  38.7 1.7 %collective-permute-start.4 = (f32[24,128]{1,0:T(8,128)S(1)}, f32[24,128]{1,0:T(8,128)S(1)}, u32[]{:S(2)}, u32[]{:S(2)}) collective-permute-start(f32[24,128]{1,0:T(8,128)S(1)} %add_add_fusion.1), channel_id=1, source_target_pairs={{0,8},{1,9},{2,10},{3,11},{4,12},{5,13},{6,14},{7,15},{8,0},{9,1},... | collective-permute-start | bytes 36872 | tf_op jit(solution)/shard_map/ppermute | solution.py:330
  40.4 2.5 %collective-permute-start.3 = (f32[24,128]{1,0:T(8,128)S(1)}, f32[24,128]{1,0:T(8,128)S(1)}, u32[]{:S(2)}, u32[]{:S(2)}) collective-permute-start(f32[24,128]{1,0:T(8,128)S(1)} %add_add_fusion.1), channel_id=1, source_target_pairs={{0,4},{1,5},{2,6},{3,7},{4,0},{5,1},{6,2},{7,3},{8,12},{9,13},{10,... | collective-permute-start | bytes 36872 | tf_op jit(solution)/shard_map/ppermute | solution.py:330
  42.9 1.1 collective-permute-done.5
  44.6 3.0 %spread.1 = (f32[2,8,128]{2,1,0:T(8,128)S(1)}, f32[1024,512]{1,0:T(8,128)}, f32[512,128]{1,0:T(8,128)S(1)}, f32[512,128]{1,0:T(8,128)S(1)}, f32[512,128]{1,0:T(8...) custom-call(s32[2]{0:T(128)S(1)} %pad_add_fusion.me_ref, ...), custom_call_target="tpu_custom_call" | custom-call | tf_op jit(solution)/shard_map/spread/pallas_call | solution.py:336
  47.6 0.8 collective-permute-start.7
  48.4 2.0 %collective-permute-start.9 = (f32[512,128]{1,0:T(8,128)S(1)}, f32[512,128]{1,0:T(8,128)S(1)}, u32[]{:S(2)}, u32[]{:S(2)}) collective-permute-start(f32[512,128]{1,0:T(8,128)S(1)} %get-tuple-element.40), channel_id=1, source_target_pairs={{0,4},{1,5},{2,6},{3,7},{4,0},{5,1},{6,2},{7,3},{8,12},{9,13},{10,... | collective-permute-start | bytes 786440 | tf_op jit(solution)/shard_map/ppermute | solution.py:330
  50.5 0.7 collective-permute-start.11
  51.1 0.9 collective-permute-start.13
  52.0 2.3 %collective-permute-start.15 = (f32[512,128]{1,0:T(8,128)S(1)}, f32[512,128]{1,0:T(8,128)S(1)}, u32[]{:S(2)}, u32[]{:S(2)}) collective-permute-start(f32[512,128]{1,0:T(8,128)S(1)} %get-tuple-element.43), channel_id=1, source_target_pairs={{0,10},{1,11},{2,8},{3,9},{4,14},{5,15},{6,12},{7,13},{8,2},{9,3},... | collective-permute-start | bytes 786440 | tf_op jit(solution)/shard_map/ppermute | solution.py:330
  54.9 11.4 %collective-permute-done.9.rest_4_ = f32[512,128]{1,0:T(8,128)S(1)} collective-permute-done((f32[512,128]{1,0:T(8,128)S(1)}, f32[512,128]{1,0:T(8,128)S(1)}, u32[]{:S(2)}, u32[]{:S(2)}) %collective-permute-start.9) | collective-permute-done | bytes 262176 | tf_op jit(solution)/shard_map/ppermute | solution.py:330
  66.3 4.2 %collective-permute-done.11.rest_6_ = f32[512,128]{1,0:T(8,128)S(1)} collective-permute-done((f32[512,128]{1,0:T(8,128)S(1)}, f32[512,128]{1,0:T(8,128)S(1)}, u32[]{:S(2)}, u32[]{:S(2)}) %collective-permute-start.11) | collective-permute-done | bytes 262176 | tf_op jit(solution)/shard_map/ppermute | solution.py:330
  71.0 4.6 %collective-permute-done.15.rest_10_.refs_1_ = f32[512,128]{1,0:T(8,128)S(1)} collective-permute-done((f32[512,128]{1,0:T(8,128)S(1)}, f32[512,128]{1,0:T(8,128)S(1)}, u32[]{:S(2)}, u32[]{:S(2)}) %collective-permute-start.15) | collective-permute-done | bytes 262176 | tf_op jit(solution)/shard_map/ppermute | solution.py:330
  76.1 15.7 %prep.1 = (s32[80,128]{1,0:T(8,128)S(1)}, s32[80,128]{1,0:T(8,128)S(1)}, f32[80,128]{1,0:T(8,128)S(1)}, f32[80,128]{1,0:T(8,128)S(1)}, s32[2,20,128]{2,1,0:T(8,128)S(1)}) custom-call(s32[2]{0:T(128)S(1)} %pad_add_fusion.me_ref, s32[160,128]{1,0:T(8,128)S(1)} %bitcast.24, s32[160,128]{1,0:T(8,128)S(1)} %bitcast.26, s32[64,128]{1,0:T(8,128)S(1)} %bitcast.30, ...), custom_call_target="tpu_custom_call" | custom-call | flops 12000000000 | bytes 1000000 | tf_op jit(solution)/shard_map/prep/pallas_call | solution.py:348
  93.1 2.0 %collective-permute-start.17 = (f32[512,128]{1,0:T(8,128)}, f32[512,128]{1,0:T(8,128)S(1)}, u32[]{:S(2)}, u32[]{:S(2)}) collective-permute-start(f32[512,128]{1,0:T(8,128)} %gate.4), channel_id=1, source_target_pairs={{0,12},{1,13},{2,14},{3,15},{4,8},{5,9},{6,10},{7,11},{8,4},{9,5},... | collective-permute-start | bytes 786440 | tf_op jit(solution)/shard_map/ppermute | solution.py:330
  95.2 0.9 copy-done.3
  96.1 0.7 copy-done.16
  96.8 0.8 copy-done.28
  97.6 0.8 copy-done.32
  98.4 11.0 %worst0.1 = (f32[8,128]{1,0:T(8,128)S(1)}, f32[8192,128]{1,0:T(8,128)S(1)}) custom-call(s32[2]{0:T(128)S(1)} %pad_add_fusion.me_ref, s32[80,128]{1,0:T(8,128)S(1)} %get-tuple-element.33.f_ref, s32[80,128]{1,0:T(8,128)S(1)} %get-tuple-element.34.t_ref, s32[2,20,128]{2,1,0:T(8,128)S(1)} %copy-done.16, f32[80,128]{1,0:T(8,128)S(1)} %copy-done.28, ...), custom_call_target="tpu_custom_call" | custom-call | flops 8999999488 | bytes 1000000 | tf_op jit(solution)/shard_map/worst0/pallas_call | solution.py:370
  110.0 2.0 %copy-done.23 = f32[8192,128]{1,0:T(8,128)} copy-done((f32[8192,128]{1,0:T(8,128)}, f32[8192,128]{1,0:T(8,128)S(1)}, u32[]{:S(2)}) %copy-start.23) | copy-done | bytes 4194328
  112.0 0.7 copy-done.5
  112.7 2.4 %collective-permute-start.19 = (f32[512,128]{1,0:T(8,128)}, f32[512,128]{1,0:T(8,128)S(1)}, u32[]{:S(2)}, u32[]{:S(2)}) collective-permute-start(f32[512,128]{1,0:T(8,128)} %gate.6), channel_id=1, source_target_pairs={{0,14},{1,15},{2,12},{3,13},{4,10},{5,11},{6,8},{7,9},{8,6},{9,7},... | collective-permute-start | bytes 786440 | tf_op jit(solution)/shard_map/ppermute | solution.py:330
  115.1 0.9 copy-done.6
  116.1 0.7 copy-done.19
  116.8 2.2 %copy-done.24 = f32[8192,128]{1,0:T(8,128)S(1)} copy-done((f32[8192,128]{1,0:T(8,128)S(1)}, f32[8192,128]{1,0:T(8,128)}, u32[]{:S(2)}) %copy-start.24) | copy-done | bytes 4194328
  119.0 0.8 copy-done.29
  119.7 0.8 copy-done.33
  120.5 6.0 %worst1.1 = (f32[8,128]{1,0:T(8,128)S(1)}, f32[8192,128]{1,0:T(8,128)S(1)}) custom-call(s32[2]{0:T(128)S(1)} %pad_add_fusion.me_ref, s32[80,128]{1,0:T(8,128)S(1)} %get-tuple-element.33.f_ref, s32[80,128]{1,0:T(8,128)S(1)} %get-tuple-element.34.t_ref, s32[2,20,128]{2,1,0:T(8,128)S(1)} %copy-done.17, ...), custom_call_target="tpu_custom_call", output_to_operand_aliasing={{0}: (7, {}), {1}: (8, {})} | custom-call | flops 4000000000 | bytes 1000000 | tf_op jit(solution)/shard_map/worst1/pallas_call | solution.py:370
  127.1 2.0 %copy-done.25 = f32[8192,128]{1,0:T(8,128)} copy-done((f32[8192,128]{1,0:T(8,128)}, f32[8192,128]{1,0:T(8,128)S(1)}, u32[]{:S(2)}) %copy-start.25) | copy-done | bytes 4194328
  129.1 0.7 copy-done.7
  129.8 1.7 %collective-permute-done.20.rest_3_ = f32[512,128]{1,0:T(8,128)S(1)} collective-permute-done((f32[512,128]{1,0:T(8,128)}, f32[512,128]{1,0:T(8,128)S(1)}, u32[]{:S(2)}, u32[]{:S(2)}) %collective-permute-start.20) | collective-permute-done | bytes 262176 | tf_op jit(solution)/shard_map/ppermute | solution.py:330
  131.6 0.9 copy-done.8
  132.5 0.7 copy-done.21
  133.2 2.2 %copy-done.26 = f32[8192,128]{1,0:T(8,128)S(1)} copy-done((f32[8192,128]{1,0:T(8,128)S(1)}, f32[8192,128]{1,0:T(8,128)}, u32[]{:S(2)}) %copy-start.26) | copy-done | bytes 4194328
  135.4 7.9 %worst2.1 = (f32[8,128]{1,0:T(8,128)S(1)}, f32[8192,128]{1,0:T(8,128)S(1)}) custom-call(s32[2]{0:T(128)S(1)} %pad_add_fusion.me_ref, s32[80,128]{1,0:T(8,128)S(1)} %get-tuple-element.33.f_ref, s32[80,128]{1,0:T(8,128)S(1)} %get-tuple-element.34.t_ref, s32[2,20,128]{2,1,0:T(8,128)S(1)} %copy-done.17, ...), custom_call_target="tpu_custom_call", output_to_operand_aliasing={{0}: (7, {}), {1}: (8, {})} | custom-call | flops 4000000000 | bytes 1000000 | tf_op jit(solution)/shard_map/worst2/pallas_call | solution.py:370
  (87 shorter events, 7.1 us)
Async XLA Ops:
  15.3 0.8 copy-start.9
  16.1 0.9 copy-start.10
  17.0 0.9 copy-start.11
  17.9 0.9 copy-start.12
  18.7 0.9 copy-start.13
  19.6 0.8 copy-start.14
  34.5 41.6 %copy-start.22 = (f32[20480]{0:T(1024)S(1)}, f32[20480]{0:T(1024)}, u32[]{:S(2)}) copy-start(f32[20480]{0:T(1024)} %param.15) | copy-start | bytes 245764
  34.5 3.2 %collective-permute-start.2 = (f32[24,128]{1,0:T(8,128)S(1)}, f32[24,128]{1,0:T(8,128)S(1)}, u32[]{:S(2)}, u32[]{:S(2)}) collective-permute-start(f32[24,128]{1,0:T(8,128)S(1)} %get-tuple-element.28), channel_id=1, source_target_pairs={{0,3},{1,2},{2,1},{3,0},{4,7},{5,6},{6,5},{7,4},{8,11},{9,10},{10,... | collective-permute-start | bytes 36872 | tf_op jit(solution)/shard_map/ppermute | solution.py:330
  34.6 3.8 %collective-permute-start.1 = (f32[24,128]{1,0:T(8,128)S(1)}, f32[24,128]{1,0:T(8,128)S(1)}, u32[]{:S(2)}, u32[]{:S(2)}) collective-permute-start(f32[24,128]{1,0:T(8,128)S(1)} %get-tuple-element.28), channel_id=1, source_target_pairs={{0,2},{1,3},{2,0},{3,1},{4,6},{5,7},{6,4},{7,5},{8,10},{9,11},{10,... | collective-permute-start | bytes 36872 | tf_op jit(solution)/shard_map/ppermute | solution.py:330
  35.5 2.9 %collective-permute-start = (f32[24,128]{1,0:T(8,128)S(1)}, f32[24,128]{1,0:T(8,128)S(1)}, u32[]{:S(2)}, u32[]{:S(2)}) collective-permute-start(f32[24,128]{1,0:T(8,128)S(1)} %get-tuple-element.28), channel_id=1, source_target_pairs={{0,1},{1,0},{2,3},{3,2},{4,5},{5,4},{6,7},{7,6},{8,9},{9,8},{10,11... | collective-permute-start | bytes 36872 | tf_op jit(solution)/shard_map/ppermute | solution.py:330
  38.4 5.6 %collective-permute-start.5 = (f32[24,128]{1,0:T(8,128)S(1)}, f32[24,128]{1,0:T(8,128)S(1)}, u32[]{:S(2)}, u32[]{:S(2)}) collective-permute-start(f32[24,128]{1,0:T(8,128)S(1)} %add_add_fusion.1), channel_id=1, source_target_pairs={{0,12},{1,13},{2,14},{3,15},{4,8},{5,9},{6,10},{7,11},{8,4},{9,5},... | collective-permute-start | bytes 36872 | tf_op jit(solution)/shard_map/ppermute | solution.py:330
  38.7 5.3 %collective-permute-start.4 = (f32[24,128]{1,0:T(8,128)S(1)}, f32[24,128]{1,0:T(8,128)S(1)}, u32[]{:S(2)}, u32[]{:S(2)}) collective-permute-start(f32[24,128]{1,0:T(8,128)S(1)} %add_add_fusion.1), channel_id=1, source_target_pairs={{0,8},{1,9},{2,10},{3,11},{4,12},{5,13},{6,14},{7,15},{8,0},{9,1},... | collective-permute-start | bytes 36872 | tf_op jit(solution)/shard_map/ppermute | solution.py:330
  40.4 4.1 %collective-permute-start.3 = (f32[24,128]{1,0:T(8,128)S(1)}, f32[24,128]{1,0:T(8,128)S(1)}, u32[]{:S(2)}, u32[]{:S(2)}) collective-permute-start(f32[24,128]{1,0:T(8,128)S(1)} %add_add_fusion.1), channel_id=1, source_target_pairs={{0,4},{1,5},{2,6},{3,7},{4,0},{5,1},{6,2},{7,3},{8,12},{9,13},{10,... | collective-permute-start | bytes 36872 | tf_op jit(solution)/shard_map/ppermute | solution.py:330
  47.6 44.3 %copy-start = (f32[512,128]{1,0:T(8,128)}, f32[512,128]{1,0:T(8,128)S(1)}, u32[]{:S(2)}) copy-start(f32[512,128]{1,0:T(8,128)S(1)} %get-tuple-element.49.refs_0_) | copy-start | bytes 786436
  47.6 44.3 %copy-start.4 = (f32[512,128]{1,0:T(8,128)}, f32[512,128]{1,0:T(8,128)S(1)}, u32[]{:S(2)}) copy-start(f32[512,128]{1,0:T(8,128)S(1)} %get-tuple-element.46.refs_0_) | copy-start | bytes 786436
  47.6 7.2 %collective-permute-start.7 = (f32[512,128]{1,0:T(8,128)S(1)}, f32[512,128]{1,0:T(8,128)S(1)}, u32[]{:S(2)}, u32[]{:S(2)}) collective-permute-start(f32[512,128]{1,0:T(8,128)S(1)} %get-tuple-element.39), channel_id=1, source_target_pairs={{0,2},{1,3},{2,0},{3,1},{4,6},{5,7},{6,4},{7,5},{8,10},{9,11},{10,... | collective-permute-start | bytes 786440 | tf_op jit(solution)/shard_map/ppermute | solution.py:330
  48.4 17.8 %collective-permute-start.9 = (f32[512,128]{1,0:T(8,128)S(1)}, f32[512,128]{1,0:T(8,128)S(1)}, u32[]{:S(2)}, u32[]{:S(2)}) collective-permute-start(f32[512,128]{1,0:T(8,128)S(1)} %get-tuple-element.40), channel_id=1, source_target_pairs={{0,4},{1,5},{2,6},{3,7},{4,0},{5,1},{6,2},{7,3},{8,12},{9,13},{10,... | collective-permute-start | bytes 786440 | tf_op jit(solution)/shard_map/ppermute | solution.py:330
  50.5 20.0 %collective-permute-start.11 = (f32[512,128]{1,0:T(8,128)S(1)}, f32[512,128]{1,0:T(8,128)S(1)}, u32[]{:S(2)}, u32[]{:S(2)}) collective-permute-start(f32[512,128]{1,0:T(8,128)S(1)} %get-tuple-element.41), channel_id=1, source_target_pairs={{0,6},{1,7},{2,4},{3,5},{4,2},{5,3},{6,0},{7,1},{8,14},{9,15},{10,... | collective-permute-start | bytes 786440 | tf_op jit(solution)/shard_map/ppermute | solution.py:330
  51.1 19.4 %collective-permute-start.13 = (f32[512,128]{1,0:T(8,128)S(1)}, f32[512,128]{1,0:T(8,128)S(1)}, u32[]{:S(2)}, u32[]{:S(2)}) collective-permute-start(f32[512,128]{1,0:T(8,128)S(1)} %get-tuple-element.42), channel_id=1, source_target_pairs={{0,8},{1,9},{2,10},{3,11},{4,12},{5,13},{6,14},{7,15},{8,0},{9,1},... | collective-permute-start | bytes 786440 | tf_op jit(solution)/shard_map/ppermute | solution.py:330
  52.0 23.6 %collective-permute-start.15 = (f32[512,128]{1,0:T(8,128)S(1)}, f32[512,128]{1,0:T(8,128)S(1)}, u32[]{:S(2)}, u32[]{:S(2)}) collective-permute-start(f32[512,128]{1,0:T(8,128)S(1)} %get-tuple-element.43), channel_id=1, source_target_pairs={{0,10},{1,11},{2,8},{3,9},{4,14},{5,15},{6,12},{7,13},{8,2},{9,3},... | collective-permute-start | bytes 786440 | tf_op jit(solution)/shard_map/ppermute | solution.py:330
  54.8 20.8 %collective-permute-start.6 = (f32[512,128]{1,0:T(8,128)S(1)}, f32[512,128]{1,0:T(8,128)S(1)}, u32[]{:S(2)}, u32[]{:S(2)}) collective-permute-start(f32[512,128]{1,0:T(8,128)S(1)} %get-tuple-element.38.rest_0_), channel_id=1, source_target_pairs={{0,1},{1,0},{2,3},{3,2},{4,5},{5,4},{6,7},{7,6},{8,9},{9,8},{10,11... | collective-permute-start | bytes 786440 | tf_op jit(solution)/shard_map/ppermute | solution.py:330
  66.3 26.9 %collective-permute-start.8 = (f32[512,128]{1,0:T(8,128)S(1)}, f32[512,128]{1,0:T(8,128)S(1)}, u32[]{:S(2)}, u32[]{:S(2)}) collective-permute-start(f32[512,128]{1,0:T(8,128)S(1)} %collective-permute-done.7.rest_2_), channel_id=1, source_target_pairs={{0,1},{1,0},{2,3},{3,2},{4,5},{5,4},{6,7},{7,6},{8,9},{9,8},{10,11... | collective-permute-start | bytes 786440 | tf_op jit(solution)/shard_map/ppermute | solution.py:330
  70.5 24.6 %collective-permute-start.10 = (f32[512,128]{1,0:T(8,128)S(1)}, f32[512,128]{1,0:T(8,128)S(1)}, u32[]{:S(2)}, u32[]{:S(2)}) collective-permute-start(f32[512,128]{1,0:T(8,128)S(1)} %collective-permute-done.9.rest_4_), channel_id=1, source_target_pairs={{0,1},{1,0},{2,3},{3,2},{4,5},{5,4},{6,7},{7,6},{8,9},{9,8},{10,11... | collective-permute-start | bytes 786440 | tf_op jit(solution)/shard_map/ppermute | solution.py:330
  70.5 21.4 %copy-start.2 = (f32[512,128]{1,0:T(8,128)}, f32[512,128]{1,0:T(8,128)S(1)}, u32[]{:S(2)}) copy-start(f32[512,128]{1,0:T(8,128)S(1)} %collective-permute-done.13.rest_8_.refs_1_) | copy-start | bytes 786436
  70.5 24.6 %collective-permute-start.12 = (f32[512,128]{1,0:T(8,128)S(1)}, f32[512,128]{1,0:T(8,128)S(1)}, u32[]{:S(2)}, u32[]{:S(2)}) collective-permute-start(f32[512,128]{1,0:T(8,128)S(1)} %collective-permute-done.11.rest_6_), channel_id=1, source_target_pairs={{0,1},{1,0},{2,3},{3,2},{4,5},{5,4},{6,7},{7,6},{8,9},{9,8},{10,11... | collective-permute-start | bytes 786440 | tf_op jit(solution)/shard_map/ppermute | solution.py:330
  75.6 19.5 %copy-start.1 = (f32[512,128]{1,0:T(8,128)}, f32[512,128]{1,0:T(8,128)S(1)}, u32[]{:S(2)}) copy-start(f32[512,128]{1,0:T(8,128)S(1)} %collective-permute-done.15.rest_10_.refs_1_) | copy-start | bytes 786436
  75.6 19.5 %collective-permute-start.14 = (f32[512,128]{1,0:T(8,128)S(1)}, f32[512,128]{1,0:T(8,128)S(1)}, u32[]{:S(2)}, u32[]{:S(2)}) collective-permute-start(f32[512,128]{1,0:T(8,128)S(1)} %collective-permute-done.13.rest_8_.refs_1_), channel_id=1, source_target_pairs={{0,1},{1,0},{2,3},{3,2},{4,5},{5,4},{6,7},{7,6},{8,9},{9,8},{10,11... | collective-permute-start | bytes 786440 | tf_op jit(solution)/shard_map/ppermute | solution.py:330
  75.6 19.5 %collective-permute-start.16 = (f32[512,128]{1,0:T(8,128)S(1)}, f32[512,128]{1,0:T(8,128)S(1)}, u32[]{:S(2)}, u32[]{:S(2)}) collective-permute-start(f32[512,128]{1,0:T(8,128)S(1)} %collective-permute-done.15.rest_10_.refs_1_), channel_id=1, source_target_pairs={{0,1},{1,0},{2,3},{3,2},{4,5},{5,4},{6,7},{7,6},{8,9},{9,8},{10,11... | collective-permute-start | bytes 786440 | tf_op jit(solution)/shard_map/ppermute | solution.py:330
  93.1 18.8 %collective-permute-start.17 = (f32[512,128]{1,0:T(8,128)}, f32[512,128]{1,0:T(8,128)S(1)}, u32[]{:S(2)}, u32[]{:S(2)}) collective-permute-start(f32[512,128]{1,0:T(8,128)} %gate.4), channel_id=1, source_target_pairs={{0,12},{1,13},{2,14},{3,15},{4,8},{5,9},{6,10},{7,11},{8,4},{9,5},... | collective-permute-start | bytes 786440 | tf_op jit(solution)/shard_map/ppermute | solution.py:330
  95.2 1.0 copy-start.3
  96.1 0.7 copy-start.16
  96.8 0.8 copy-start.28
  97.6 0.8 copy-start.32
  98.4 16.7 %copy-start.17 = (s32[2,20,128]{2,1,0:T(8,128)S(1)}, s32[2,20,128]{2,1,0:T(8,128)}, u32[]{:S(2)}) copy-start(s32[2,20,128]{2,1,0:T(8,128)} %copy-done.15) | copy-start | bytes 61444
  110.0 2.0 %copy-start.23 = (f32[8192,128]{1,0:T(8,128)}, f32[8192,128]{1,0:T(8,128)S(1)}, u32[]{:S(2)}) copy-start(f32[8192,128]{1,0:T(8,128)S(1)} %get-tuple-element.45.rest_1_) | copy-start | bytes 12582916
  112.7 2.4 %collective-permute-start.18 = (f32[512,128]{1,0:T(8,128)}, f32[512,128]{1,0:T(8,128)S(1)}, u32[]{:S(2)}, u32[]{:S(2)}) collective-permute-start(f32[512,128]{1,0:T(8,128)} %gate.5.rest_2_), channel_id=1, source_target_pairs={{0,1},{1,0},{2,3},{3,2},{4,5},{5,4},{6,7},{7,6},{8,9},{9,8},{10,11... | collective-permute-start | bytes 786440 | tf_op jit(solution)/shard_map/ppermute | solution.py:330
  112.7 16.4 %collective-permute-start.19 = (f32[512,128]{1,0:T(8,128)}, f32[512,128]{1,0:T(8,128)S(1)}, u32[]{:S(2)}, u32[]{:S(2)}) collective-permute-start(f32[512,128]{1,0:T(8,128)} %gate.6), channel_id=1, source_target_pairs={{0,14},{1,15},{2,12},{3,13},{4,10},{5,11},{6,8},{7,9},{8,6},{9,7},... | collective-permute-start | bytes 786440 | tf_op jit(solution)/shard_map/ppermute | solution.py:330
  115.1 1.0 copy-start.6
  116.8 2.2 %copy-start.24 = (f32[8192,128]{1,0:T(8,128)S(1)}, f32[8192,128]{1,0:T(8,128)}, u32[]{:S(2)}) copy-start(f32[8192,128]{1,0:T(8,128)} %copy-done.23) | copy-start | bytes 12582916
  119.0 0.8 copy-start.29
  119.7 0.8 copy-start.33
  120.5 11.0 %copy-start.30 = (f32[80,128]{1,0:T(8,128)S(1)}, f32[80,128]{1,0:T(8,128)}, u32[]{:S(2)}) copy-start(f32[80,128]{1,0:T(8,128)} %copy-done.27) | copy-start | bytes 122884
  120.5 11.0 %copy-start.34 = (f32[80,128]{1,0:T(8,128)S(1)}, f32[80,128]{1,0:T(8,128)}, u32[]{:S(2)}) copy-start(f32[80,128]{1,0:T(8,128)} %copy-done.31) | copy-start | bytes 122884
  127.1 2.0 %copy-start.25 = (f32[8192,128]{1,0:T(8,128)}, f32[8192,128]{1,0:T(8,128)S(1)}, u32[]{:S(2)}) copy-start(f32[8192,128]{1,0:T(8,128)S(1)} %get-tuple-element.48.rest_1_) | copy-start | bytes 12582916
  129.8 1.7 %collective-permute-start.20 = (f32[512,128]{1,0:T(8,128)}, f32[512,128]{1,0:T(8,128)S(1)}, u32[]{:S(2)}, u32[]{:S(2)}) collective-permute-start(f32[512,128]{1,0:T(8,128)} %gate.7.rest_2_), channel_id=1, source_target_pairs={{0,1},{1,0},{2,3},{3,2},{4,5},{5,4},{6,7},{7,6},{8,9},{9,8},{10,11... | collective-permute-start | bytes 786440 | tf_op jit(solution)/shard_map/ppermute | solution.py:330
  131.6 1.0 copy-start.8
  133.2 2.2 %copy-start.26 = (f32[8192,128]{1,0:T(8,128)S(1)}, f32[8192,128]{1,0:T(8,128)}, u32[]{:S(2)}) copy-start(f32[8192,128]{1,0:T(8,128)} %copy-done.25) | copy-start | bytes 12582916
  143.3 1.4 collective-permute-start.21
  (9 other events, 5.8 us)

commit v4 on v3

v4 whole, which is shorter than its diff:
```python
import functools
import math

import jax
import jax.numpy as jnp
from jax import lax
from jax.experimental import pallas as pl
from jax.experimental.pallas import tpu as pltpu
from jax.sharding import PartitionSpec as P

STEPS = 3
LANES = 128
GROUP = 4
SINE = (3.1415926444, -5.1677100819, 2.5500775297, -0.5982913039, 0.0776576582)
VMEM = pl.BlockSpec(memory_space=pltpu.VMEM)
SMEM = pl.BlockSpec(memory_space=pltpu.SMEM)
ANY = pl.BlockSpec(memory_space=pl.ANY)


def params(mib):
    return pltpu.CompilerParams(vmem_limit_bytes=mib * 2**20)


def split(table, parts):
    out = []
    for _ in range(parts):
        piece = table.astype(jnp.bfloat16)
        out.append(piece)
        table = table - piece.astype(jnp.float32)
    return out


def columns(tables):
    return jnp.concatenate([jnp.concatenate(split(t.T, 3), 1) for t in tables], 0)


def lookup(turned, index):
    rows = turned.shape[1] // 3
    n = index.shape[1]
    hot = lax.broadcasted_iota(jnp.int32, (rows, n), 0) == (index >> 7)
    hot = jnp.where(hot, 1.0, 0.0).astype(jnp.bfloat16)
    picked = jnp.dot(turned, jnp.concatenate([hot] * 3, 0), preferred_element_type=jnp.float32)
    lane = lax.broadcasted_iota(jnp.int32, (LANES, n), 0) == (index & 127)
    return [jnp.sum(jnp.where(lane, picked[i:i + LANES], 0.0), axis=0, keepdims=True)
            for i in range(0, turned.shape[0], LANES)]


def newton(a_head, a_tail, self_head, cross, self_tail, bsus, hchg):
    inj_head = jnp.zeros_like(a_head)
    inj_tail = jnp.zeros_like(a_head)
    for step in range(1, STEPS + 1):
        level = step / STEPS
        end_head = a_head + self_head * inj_head + cross * inj_tail
        end_tail = a_tail + cross * inj_head + self_tail * inj_tail
        spread = end_head - end_tail
        sine_val = jnp.sin(spread)
        cosine_val = jnp.cos(spread)
        resid_head = inj_head - level * (bsus * sine_val + hchg * end_head)
        resid_tail = inj_tail - level * (-bsus * sine_val + hchg * end_tail)
        diag_term = bsus * cosine_val + hchg
        cross_term = -bsus * cosine_val
        jac_one = 1.0 - level * (diag_term * self_head + cross_term * cross)
        jac_two = -level * (diag_term * cross + cross_term * self_tail)
        jac_three = -level * (cross_term * self_head + diag_term * cross)
        jac_four = 1.0 - level * (cross_term * cross + diag_term * self_tail)
        determinant = jac_one * jac_four - jac_two * jac_three
        inj_head = inj_head - (jac_four * resid_head - jac_two * resid_tail) / determinant
        inj_tail = inj_tail - (jac_one * resid_tail - jac_three * resid_head) / determinant
    return inj_head, inj_tail


def addresses(row, width):
    return (row >> 3) * (8 * width) + (row & 7)


def stage(pairs, sem):
    copies = [pltpu.make_async_copy(src, dst, sem.at[i]) for i, (src, dst) in enumerate(pairs)]
    for copy in copies:
        copy.start()
    return copies


def ends_kernel(width, me_ref, ids_ref, from_ref, to_ref, slot_ref, sus_ref, chg_ref, base_ref, zinv_ref,
                state_ref, pick_ref, own_base_ref, rows_ref, from_v, to_v, slot_v, sus_v, chg_v, base_v,
                zinv_v, ends_v, ends_s, rows, sem, out_sem):
    total = ids_ref.shape[1]
    blocks = total // LANES
    first = me_ref[0] * width * LANES
    copies = stage([(from_ref, from_v), (to_ref, to_v), (slot_ref, slot_v), (sus_ref, sus_v),
                    (chg_ref, chg_v), (base_ref, base_v), (zinv_ref, zinv_v)], sem)
    for copy in copies[:-1]:
        copy.wait()
    branch = columns([from_v[...].astype(jnp.float32), to_v[...].astype(jnp.float32), sus_v[...], chg_v[...]])
    slot = columns([slot_v[...].astype(jnp.float32)])
    base = columns([base_v[...]])
    wide = min(total, 8 * LANES)
    for c in range(0, total, wide):
        ids = ids_ref[:, c:c + wide]
        f, t, sus, chg = lookup(branch, ids)
        ends, = lookup(slot, jnp.concatenate([f, t], 1).astype(jnp.int32))
        ends = ends.astype(jnp.int32)
        angle, = lookup(base, ends)
        place = addresses(ends, width)
        local = (ends - first).astype(jnp.float32)
        known = (angle[:, :wide], angle[:, wide:], sus, chg, local[:, :wide], local[:, wide:],
                 ids.astype(jnp.float32))
        for b in range(wide // LANES):
            row = slice(c // LANES + b, c // LANES + b + 1)
            at = slice(b * LANES, (b + 1) * LANES)
            ends_v[row, :] = place[:, at]
            ends_v[slice(blocks + row.start, blocks + row.stop), :] = place[:, b * LANES + wide:(b + 1) * LANES + wide]
            for i, value in enumerate(known):
                state_ref[i, row, :] = value[:, at]
    copy = pltpu.make_async_copy(ends_v, ends_s, sem.at[0])
    copy.start()
    for t in range(width):
        own_base_ref[t:t + 1, :] = base_v[pl.ds(me_ref[0] * width + t, 1), :]
    copy.wait()
    copies[-1].wait()

    def block(b, slot):
        def fetch(g, carry):
            for i in range(32):
                o = g * 32 + i
                head = ends_s[b, o]
                tail = ends_s[blocks + b, o]
                for t in range(width):
                    rows[slot, 0, t, pl.ds(o, 1), :] = zinv_v[pl.ds(head + 8 * t, 1), :]
                    rows[slot, 1, t, pl.ds(o, 1), :] = zinv_v[pl.ds(tail + 8 * t, 1), :]
            return carry

        lax.fori_loop(0, LANES // 32, fetch, 0)
        pltpu.make_async_copy(rows.at[slot], rows_ref.at[b], out_sem.at[slot]).start()
        square = (LANES, LANES)
        at_h = jnp.broadcast_to(state_ref[4, pl.ds(b, 1), :], square).T
        at_t = jnp.broadcast_to(state_ref[5, pl.ds(b, 1), :], square).T
        lane = lax.broadcasted_iota(jnp.int32, square, 1).astype(jnp.float32)
        hh = ht = tt = jnp.zeros(square, jnp.float32)
        for t in range(width):
            is_h = at_h == lane + float(t * LANES)
            is_t = at_t == lane + float(t * LANES)
            hh = jnp.where(is_h, rows[slot, 0, t], hh)
            ht = jnp.where(is_t, rows[slot, 0, t], ht)
            tt = jnp.where(is_t, rows[slot, 1, t], tt)
        for i, pick in enumerate((hh, ht, tt)):
            pick_ref[pl.ds(i * blocks + b, 1), :] = jnp.sum(pick.T, axis=0, keepdims=True)

    def pair(i, carry):
        for slot in (0, 1):
            @pl.when(i > 0)
            def _():
                pltpu.make_async_copy(rows.at[slot], rows_ref.at[2 * i - 2 + slot], out_sem.at[slot]).wait()

            block(2 * i + slot, slot)
        return carry

    lax.fori_loop(0, blocks // 2, pair, 0)
    for slot in (0, 1):
        pltpu.make_async_copy(rows.at[slot], rows_ref.at[blocks - 2 + slot], out_sem.at[slot]).wait()


def spread_kernel(chips, me_ref, state_ref, pick_ref, base_ref, rows_ref, inj_ref, dev_ref, *rest):
    units, (state, pick, base, inj, rows, dev, unit, in_sem, row_sem, out_sem) = rest[:chips], rest[chips:]
    blocks, _, width = rows.shape[:3]
    me = me_ref[0]
    small = stage([(state_ref, state), (pick_ref, pick), (base_ref, base)], in_sem)
    whole = [pltpu.make_async_copy(rows_ref.at[(me >> 1) ^ d], rows.at[d], row_sem.at[d]) for d in range(chips)]
    for copy in whole:
        copy.start()
    for copy in small:
        copy.wait()
    inj_h, inj_t = newton(state[0], state[1], pick[:blocks], pick[blocks:2 * blocks], pick[2 * blocks:],
                          state[2], state[3])
    inj[0] = inj_h
    inj[1] = inj_t
    outs = [pltpu.make_async_copy(inj, inj_ref, in_sem.at[0])]
    outs[0].start()
    order = list(range(chips // 2, chips)) + list(range(chips // 2))
    pending = [None, None]
    for i, d in enumerate(order):
        slot = i % 2
        blk = (me >> 1) ^ d
        scale_h = jnp.broadcast_to(inj[0, pl.ds(blk, 1), :], (LANES, LANES)).T
        scale_t = jnp.broadcast_to(inj[1, pl.ds(blk, 1), :], (LANES, LANES)).T
        whole[d].wait()
        for copy in pending[slot] or ():
            copy.wait()
        for t in range(width):
            at = slice(t * LANES, (t + 1) * LANES)
            value = scale_h * rows[d, 0, t] + scale_t * rows[d, 1, t]
            dev[slot, :, at] = value
            unit[slot, at, :] = ((base[t:t + 1, :] + value) * (1.0 / math.pi)).T
        goal = dev_ref.at[pl.ds(pl.multiple_of(blk * LANES, LANES), LANES)]
        pending[slot] = stage([(dev.at[slot], goal), (unit.at[slot], units[d])], out_sem.at[slot])
    for copy in pending[0] + pending[1] + outs:
        copy.wait()


def prep_kernel(unit, chips, me_ref, from_ref, to_ref, slot_ref, sus_ref, rate_ref,
                f_ref, t_ref, ratio_ref, k_ref, cnt_ref):
    half = f_ref.shape[0]
    me = me_ref[0]
    start = (me & 1) * half
    flip = me * unit
    bits = unit.bit_length() - 1
    slot = columns([slot_ref[...].astype(jnp.float32)])

    square = (LANES, LANES)
    before = lax.broadcasted_iota(jnp.int32, square, 0) < lax.broadcasted_iota(jnp.int32, square, 1)
    before = jnp.where(before, 1.0, 0.0).astype(jnp.bfloat16)
    lane = lax.broadcasted_iota(jnp.int32, (1, LANES), 1).astype(jnp.float32)
    slots = lax.broadcasted_iota(jnp.int32, (GROUP * LANES, LANES), 0).astype(jnp.float32)

    def place(bus_ref, row):
        bus = jnp.concatenate([bus_ref[pl.ds(row + i, 1), :] for i in range(GROUP)], 1)
        rel = lookup(slot, bus)[0].astype(jnp.int32) ^ flip
        chip = rel >> (bits + 1)
        core = (rel >> bits) & 1
        return chip, (rel & (unit - 1)) + (core * chips + chip) * unit

    def group(g, carry):
        f_chip, f = place(from_ref, start + g * GROUP)
        t_chip, t = place(to_ref, start + g * GROUP)
        chip = jnp.maximum(f_chip, t_chip)
        first = jnp.where(chip < chips - 2, 1.0, 0.0)
        second = jnp.where(chip == chips - 2, 1.0, 0.0)
        tile = lambda a, i: a[:, i * LANES:(i + 1) * LANES]
        flags = jnp.concatenate([tile(a, i) for a in (first, second) for i in range(GROUP)], 0)
        ahead = jnp.dot(flags.astype(jnp.bfloat16), before, preferred_element_type=jnp.float32)
        sums = jnp.sum(flags, axis=1, keepdims=True)
        n_first = sum(sums[i:i + 1] for i in range(GROUP))
        n_second = sum(sums[GROUP + i:GROUP + i + 1] for i in range(GROUP))
        off_first = off_second = jnp.zeros((1, 1), jnp.float32)
        total = jnp.zeros((16, GROUP * LANES), jnp.float32)
        for i in range(GROUP):
            c_first = off_first + ahead[i:i + 1]
            c_second = off_second + ahead[GROUP + i:GROUP + i + 1]
            rest = n_first + n_second + (lane + float(i * LANES)) - c_first - c_second
            goal = jnp.where(tile(first, i) > 0.5, c_first,
                             jnp.where(tile(second, i) > 0.5, n_first + c_second, rest))
            off_first = off_first + sums[i:i + 1]
            off_second = off_second + sums[GROUP + i:GROUP + i + 1]
            hot = jnp.where(slots == goal, 1.0, 0.0).astype(jnp.bfloat16)
            row = pl.ds(start + g * GROUP + i, 1)
            rows = [tile(f, i) >> 7, tile(f, i) & 127, tile(t, i) >> 7, tile(t, i) & 127]
            rows = [r.astype(jnp.float32) for r in rows]
            rows += [p.astype(jnp.float32) for p in split(sus_ref[row, :] / rate_ref[row, :], 3)]
            rows += [jnp.full((1, LANES), float(i)), lane] + [jnp.zeros((1, LANES), jnp.float32)] * 7
            values = jnp.concatenate(rows, 0).astype(jnp.bfloat16)
            total += lax.dot_general(values, hot, (((1,), (1,)), ((), ())), preferred_element_type=jnp.float32)
        for i in range(GROUP):
            out = pl.ds(g * GROUP + i, 1)
            part = total[:, i * LANES:(i + 1) * LANES]
            f_ref[out, :] = (part[0:1] * 128.0 + part[1:2]).astype(jnp.int32)
            t_ref[out, :] = (part[2:3] * 128.0 + part[3:4]).astype(jnp.int32)
            ratio_ref[out, :] = part[4:5] + part[5:6] + part[6:7]
            origin = ((start + g * GROUP) * LANES).astype(jnp.float32)
            k_ref[out, :] = part[7:8] * 128.0 + part[8:9] + origin
        wide = lambda a: jnp.broadcast_to(a, (1, LANES)).astype(jnp.int32) >> 7
        cnt_ref[0, pl.ds(g, 1), :] = wide(n_first)
        cnt_ref[1, pl.ds(g, 1), :] = wide(n_first + n_second)
        return carry

    lax.fori_loop(0, half // GROUP, group, 0)


def join_kernel(_, *refs):
    pieces, (out_ref, sem) = refs[:-2], refs[-2:]
    unit = pieces[0].shape[0]
    for copy in stage([(p, out_ref.at[pl.ds(i * unit, unit)]) for i, p in enumerate(pieces)], sem):
        copy.wait()


def worst_kernel(level, me_ref, f_ref, t_ref, cnt_ref, ratio_ref, k_ref, state_ref, *rest):
    n = 2 * level + 2
    if level:
        best_in, *rest = rest
    pieces, (best, table, f_s, t_s, cnt_s, diff, sem) = rest[:n], rest[n:]
    pairs = [(f_ref, f_s), (t_ref, t_s), (cnt_ref, cnt_s)]
    row = 0
    for own, other in zip(pieces[::2], pieces[1::2]):
        size = own.shape[0]
        pairs += [(own, table.at[pl.ds(row, size)]),
                  (other, table.at[pl.ds(table.shape[0] // 2 + row, size)])]
        row += size
    copies = stage(pairs, sem)
    half = f_ref.shape[0]
    ids = state_ref[6, pl.ds(me_ref[0] >> 1, 1), :]
    best[...] = best_in[...] if level else jnp.zeros_like(best)
    for copy in copies:
        copy.wait()

    def block(b, carry):
        for j in range(LANES):
            diff[pl.ds(j, 1), :] = table[pl.ds(f_s[b, j], 1), :] - table[pl.ds(t_s[b, j], 1), :]
        turn = diff[...]
        turn = turn - jnp.round(turn)
        square = turn * turn
        poly = SINE[4]
        for c in SINE[3::-1]:
            poly = poly * square + c
        ratio = jnp.broadcast_to(ratio_ref[pl.ds(b, 1), :], (LANES, LANES)).T
        branch = jnp.broadcast_to(k_ref[pl.ds(b, 1), :], (LANES, LANES)).T
        load = jnp.where(branch == ids, 0.0, jnp.abs(turn * poly) * ratio)
        best[...] = jnp.maximum(best[...], jnp.max(load.reshape(LANES // 8, 8, LANES), axis=0))
        return carry

    def group(g, carry):
        low = cnt_s[level - 1, g, 0] if level else 0
        high = GROUP if level == 2 else cnt_s[level, g, 0]
        return lax.fori_loop(g * GROUP + low, g * GROUP + high, block, carry)

    lax.fori_loop(0, half // GROUP, group, 0)
    if level == 2:
        best[...] = jnp.broadcast_to(jnp.max(best[...], axis=0, keepdims=True), best.shape)


def per_device(
    outages, branch_from, branch_to, bus_slot, susceptance, charging, rating, base_angles, zinv
):
    n_col = lax.axis_size("col")
    buses, cols = zinv.shape
    own = outages.shape[0]
    total = own * n_col
    blocks = total // LANES
    chips = n_col // 2
    assert own * 2 == LANES and chips & (chips - 1) == 0 and chips > 2
    me = lax.axis_index("col")
    where = jnp.stack([me, jnp.int32(n_col)])
    tab = lambda a: a.reshape(-1, LANES)
    from2, to2, slot2, sus2, chg2, rate2, base2 = map(
        tab, (branch_from, branch_to, bus_slot, susceptance, charging, rating, base_angles)
    )
    i32 = lambda *s: jax.ShapeDtypeStruct(s, jnp.int32)
    f32 = lambda *s: jax.ShapeDtypeStruct(s, jnp.float32)

    flat = zinv.reshape(buses // 8, 8, cols // LANES, LANES).transpose(0, 2, 1, 3).reshape(-1, LANES)
    ids = lax.dynamic_update_slice(jnp.zeros((total,), jnp.int32), outages, (me * own,))
    ids = lax.psum(ids[None], "col")

    width = cols // LANES
    like = lambda a: pltpu.VMEM(a.shape, a.dtype)
    row_shape = (2, width, LANES, LANES)
    state, picks, own_base, rows = pl.pallas_call(
        functools.partial(ends_kernel, width),
        name="ends",
        out_shape=[f32(7, blocks, LANES), f32(3 * blocks, LANES), f32(width, LANES), f32(blocks, *row_shape)],
        in_specs=[SMEM, VMEM] + [ANY] * 7,
        out_specs=[VMEM] * 3 + [ANY],
        scratch_shapes=[like(from2), like(to2), like(slot2), like(sus2), like(chg2), like(base2), like(flat),
                        pltpu.VMEM((2 * blocks, LANES), jnp.int32), pltpu.SMEM((2 * blocks, LANES), jnp.int32),
                        pltpu.VMEM((2,) + row_shape, jnp.float32), pltpu.SemaphoreType.DMA((7,)),
                        pltpu.SemaphoreType.DMA((2,))],
        compiler_params=params(60),
    )(where, ids, from2, to2, slot2, sus2, chg2, base2, flat)

    swap = lambda a, m: lax.ppermute(a, "col", [(i, i ^ m) for i in range(n_col)])
    step = 1
    while step < n_col:
        picks = sum([swap(picks, m * step) for m in range(1, min(4, n_col // step))], picks)
        step *= 4

    injections, deviation, *units = pl.pallas_call(
        functools.partial(spread_kernel, chips),
        name="spread",
        out_shape=[f32(2, blocks, LANES), f32(total, cols)] + [f32(cols, LANES)] * chips,
        in_specs=[SMEM] + [ANY] * 4,
        out_specs=[ANY] * (2 + chips),
        scratch_shapes=[like(state), like(picks), like(own_base), pltpu.VMEM((2, blocks, LANES), jnp.float32),
                        like(rows), pltpu.VMEM((2, LANES, cols), jnp.float32),
                        pltpu.VMEM((2, cols, LANES), jnp.float32), pltpu.SemaphoreType.DMA((3,)),
                        pltpu.SemaphoreType.DMA((chips,)), pltpu.SemaphoreType.DMA((2, 2))],
        compiler_params=params(60),
    )(where, state, picks, own_base, rows)

    half = branch_from.shape[0] // LANES // 2
    f_rel, t_rel, ratio, k_rel, counts = pl.pallas_call(
        functools.partial(prep_kernel, cols, chips),
        name="prep",
        out_shape=[i32(half, LANES), i32(half, LANES), f32(half, LANES), f32(half, LANES),
                   i32(2, half // GROUP, LANES)],
        in_specs=[SMEM] + [VMEM] * 5,
        out_specs=[VMEM] * 5,
        compiler_params=params(16),
    )(where, from2, to2, slot2, sus2, rate2)

    got = [units[0]] + [swap(units[d], 2 * d) for d in range(1, chips)]

    def join(after, pieces):
        packed = pl.pallas_call(
            join_kernel,
            name="join",
            out_shape=f32(len(pieces) * cols, LANES),
            in_specs=[ANY] * (1 + len(pieces)),
            out_specs=VMEM,
            scratch_shapes=[pltpu.SemaphoreType.DMA((len(pieces),))],
            compiler_params=params(16),
        )(after, *pieces)
        return [packed, swap(packed, 1)]

    def worst_of(level, *operands):
        return pl.pallas_call(
            functools.partial(worst_kernel, level),
            name=f"worst{level}",
            out_shape=f32(8, LANES),
            in_specs=[SMEM] + [ANY] * 3 + [VMEM] * (3 + min(level, 1)) + [ANY] * (2 * level + 2),
            out_specs=VMEM,
            scratch_shapes=[pltpu.VMEM((buses, LANES), jnp.float32)]
            + [pltpu.SMEM(a.shape, a.dtype) for a in (f_rel, t_rel, counts)]
            + [pltpu.VMEM((LANES, LANES), jnp.float32), pltpu.SemaphoreType.DMA((2 * level + 5,))],
            compiler_params=params(16),
        )(where, f_rel, t_rel, counts, ratio, k_rel, state, *operands)

    early = join(counts, got[:-2])
    best = worst_of(0, *early)
    middle, late = join(best, got[-2:-1]), join(best, got[-1:])
    best = worst_of(1, best, *early, *middle)
    best = worst_of(2, best, *early, *middle, *late)
    worst = lax.slice(best, (0, 0), (1, LANES))
    worst = lax.dynamic_slice(jnp.maximum(worst, swap(worst, 1))[0], ((me & 1) * own,), (own,))
    inj = lax.dynamic_slice(injections.reshape(2, total), (0, me * own), (2, own))
    return inj, deviation, worst


def solution(mesh):
    return jax.shard_map(
        per_device,
        mesh=mesh,
        in_specs=(P(("parts", "col")), P(), P(), P(), P(), P(), P(), P("parts"), P(None, "col")),
        out_specs=(P(None, ("parts", "col")), P("parts", "col"), P(("parts", "col"))),
        check_vma=False,
    )
```

time: 146 us -> 121 us (0.83)
  the two profiles are of different devices: /device:TPU:0 before, /device:TPU:9 now
where the time goes in v4:
time: 121 us; the launch traced here: 120 us
  Pallas kernels  62.5 us (52%)
  starting transfers between devices  23.4 us (19%)
  waiting for transfers between devices  17.1 us (14%)
  blocking collectives  9.24 us (8%)
  local copies, waits for them, and re-layouts  5.36 us (4%)
  other arithmetic  1.9 us (2%)
    pallas_call x3, Pallas kernels, worst_of(): pl.pallas_call(functools.partial(worst_kernel, level), name=f'worst{level...  25.3 us
    ppermute x17, starting transfers between devices, per_device(): lax.ppermute(a, 'col', [(i, i ^ m) for i in range(n_col)])  23.4 us
    ppermute x17, waiting for transfers between devices, per_device(): lax.ppermute(a, 'col', [(i, i ^ m) for i in range(n_col)])  17.1 us
    pallas_call x1, Pallas kernels, per_device(): pl.pallas_call(functools.partial(ends_kernel, width), name='ends', out_sh...  15.1 us
    pallas_call x1, Pallas kernels, per_device(): pl.pallas_call(functools.partial(prep_kernel, cols, chips), name='prep',...  14.6 us
    psum x1, blocking collectives, per_device(): ids = lax.psum(ids[None], 'col')  9.24 us
    pallas_call x1, Pallas kernels, per_device(): pl.pallas_call(functools.partial(spread_kernel, chips), name='spread', ou...  6.62 us
    unnamed x29, local copies, waits for them, and re-layouts  3.25 us
  transfers between devices with their start and end apart: 17, of which 8 were waited for; matrix products, arithmetic and copies ran while one was open for 1% of the time, Pallas kernels for 27%

profile of v4, /device:TPU:9, one launch (start us, length us, event | category | flops | bytes accessed | tf_op | source)
XLA Modules:
  0.0 120.4 jit_solution(17891510947491486784)
XLA Ops:
  0.6 0.9 dynamic_update_slice.4
  1.5 9.2 %psum.7.ids_ref = s32[1,1024]{1,0:T(1,128)} all-reduce(s32[1,1024]{1,0:T(1,128)S(1)} %dynamic_update_slice.4), channel_id=1, replica_groups=mesh['parts'=2,'col'=16] {'col'}, use_global_device_ids=true, to_apply=%region_0.0 | all-reduce | flops 1024 | bytes 8192 | tf_op jit(solution)/shard_map/psum | solution.py:339
  10.8 0.6 pad_add_fusion.me_ref
  11.3 15.1 %ends.1 = (f32[7,8,128]{2,1,0:T(8,128)}, f32[24,128]{1,0:T(8,128)}, f32[4,128]{1,0:T(4,128)}, f32[8,2,4,128,128]{4,3,2,1,0:T(8,128)}) custom-call(s32[2]{0:T(128)} %pad_add_fusion.me_ref, s32[1,1024]{1,0:T(1,128)} %psum.7.ids_ref, s32[160,128]{1,0:T(8,128)} %bitcast.20, s32[160,128]{1,0:T(8,128)} %bitcast.22, s32[64,128]{1,0:T(8,128)} %bitcast.26, ...), custom_call_target="tpu_custom_call" | custom-call | tf_op jit(solution)/shard_map/ends/pallas_call | solution.py:344
  26.5 3.2 %collective-permute-start = (f32[24,128]{1,0:T(8,128)}, f32[24,128]{1,0:T(8,128)S(1)}, u32[]{:S(2)}, u32[]{:S(2)}) collective-permute-start(f32[24,128]{1,0:T(8,128)} %get-tuple-element.23), channel_id=1, source_target_pairs={{0,1},{1,0},{2,3},{3,2},{4,5},{5,4},{6,7},{7,6},{8,9},{9,8},{10,11... | collective-permute-start | bytes 36872 | tf_op jit(solution)/shard_map/ppermute | solution.py:357
  29.6 0.6 collective-permute-start.1
  30.2 1.1 collective-permute-start.2
  31.4 1.1 collective-permute-done.1
  32.4 1.1 collective-permute-done.2
  33.6 0.7 add_add_fusion.1
  34.3 1.3 %collective-permute-start.3 = (f32[24,128]{1,0:T(8,128)S(1)}, f32[24,128]{1,0:T(8,128)S(1)}, u32[]{:S(2)}, u32[]{:S(2)}) collective-permute-start(f32[24,128]{1,0:T(8,128)S(1)} %add_add_fusion.1), channel_id=1, source_target_pairs={{0,4},{1,5},{2,6},{3,7},{4,0},{5,1},{6,2},{7,3},{8,12},{9,13},{10,... | collective-permute-start | bytes 36872 | tf_op jit(solution)/shard_map/ppermute | solution.py:357
  35.6 0.1 collective-permute-start.4
  35.6 1.3 %collective-permute-start.5 = (f32[24,128]{1,0:T(8,128)S(1)}, f32[24,128]{1,0:T(8,128)S(1)}, u32[]{:S(2)}, u32[]{:S(2)}) collective-permute-start(f32[24,128]{1,0:T(8,128)S(1)} %add_add_fusion.1), channel_id=1, source_target_pairs={{0,12},{1,13},{2,14},{3,15},{4,8},{5,9},{6,10},{7,11},{8,4},{9,5},... | collective-permute-start | bytes 36872 | tf_op jit(solution)/shard_map/ppermute | solution.py:357
  36.9 0.0 collective-permute-done.3
  36.9 2.1 %collective-permute-done.4 = f32[24,128]{1,0:T(8,128)S(1)} collective-permute-done((f32[24,128]{1,0:T(8,128)S(1)}, f32[24,128]{1,0:T(8,128)S(1)}, u32[]{:S(2)}, u32[]{:S(2)}) %collective-permute-start.4) | collective-permute-done | bytes 12320 | tf_op jit(solution)/shard_map/ppermute | solution.py:357
  39.0 0.0 collective-permute-done.5
  39.0 0.6 add_add_fusion.pick_ref
  39.6 0.0 copy-start.10
  39.6 0.0 copy-start.11
  39.6 6.6 %spread.1 = (f32[2,8,128]{2,1,0:T(8,128)}, f32[1024,512]{1,0:T(8,128)}, f32[512,128]{1,0:T(8,128)}, f32[512,128]{1,0:T(8,128)}, f32[512,128]{1,0:T(8,128)}, /*in...) custom-call(s32[2]{0:T(128)} %pad_add_fusion.me_ref, ...), custom_call_target="tpu_custom_call" | custom-call | tf_op jit(solution)/shard_map/spread/pallas_call | solution.py:363
  46.3 3.9 %collective-permute-start.10 = (f32[512,128]{1,0:T(8,128)}, f32[512,128]{1,0:T(8,128)S(1)}, u32[]{:S(2)}, u32[]{:S(2)}) collective-permute-start(f32[512,128]{1,0:T(8,128)} %get-tuple-element.38), channel_id=1, source_target_pairs={{0,10},{1,11},{2,8},{3,9},{4,14},{5,15},{6,12},{7,13},{8,2},{9,3},... | collective-permute-start | bytes 786440 | tf_op jit(solution)/shard_map/ppermute | solution.py:357
  50.2 0.6 collective-permute-start.6
  50.8 2.1 %collective-permute-start.8 = (f32[512,128]{1,0:T(8,128)}, f32[512,128]{1,0:T(8,128)S(1)}, u32[]{:S(2)}, u32[]{:S(2)}) collective-permute-start(f32[512,128]{1,0:T(8,128)} %get-tuple-element.36), channel_id=1, source_target_pairs={{0,6},{1,7},{2,4},{3,5},{4,2},{5,3},{6,0},{7,1},{8,14},{9,15},{10,... | collective-permute-start | bytes 786440 | tf_op jit(solution)/shard_map/ppermute | solution.py:357
  52.9 14.6 %prep.1 = (s32[80,128]{1,0:T(8,128)S(1)}, s32[80,128]{1,0:T(8,128)S(1)}, f32[80,128]{1,0:T(8,128)S(1)}, f32[80,128]{1,0:T(8,128)S(1)}, s32[2,20,128]{2,1,0:T(8,128)S(1)}) custom-call(s32[2]{0:T(128)S(1)} %copy-done.11, s32[160,128]{1,0:T(8,128)S(1)} %bitcast.21, s32[160,128]{1,0:T(8,128)S(1)} %bitcast.23, s32[64,128]{1,0:T(8,128)S(1)} %bitcast.27, ...), custom_call_target="tpu_custom_call" | custom-call | tf_op jit(solution)/shard_map/prep/pallas_call | solution.py:377
  67.5 0.0 collective-permute-done.10.refs_5_
  67.5 0.0 collective-permute-done.6.refs_1_
  67.5 3.8 %collective-permute-done.8.refs_3_ = f32[512,128]{1,0:T(8,128)S(1)} collective-permute-done((f32[512,128]{1,0:T(8,128)}, f32[512,128]{1,0:T(8,128)S(1)}, u32[]{:S(2)}, u32[]{:S(2)}) %collective-permute-start.8) | collective-permute-done | bytes 262176 | tf_op jit(solution)/shard_map/ppermute | solution.py:357
  71.4 0.9 copy-done.8
  72.3 0.2 join.3.rest_0_.rest_1_
  72.5 2.9 %collective-permute-start.11 = (f32[3072,128]{1,0:T(8,128)S(1)}, f32[3072,128]{1,0:T(8,128)S(1)}, u32[]{:S(2)}, u32[]{:S(2)}) collective-permute-start(f32[3072,128]{1,0:T(8,128)S(1)} %join.3.rest_0_.rest_1_), channel_id=1, source_target_pairs={{0,1},{1,0},{2,3},{3,2},{4,5},{5,4},{6,7},{7,6},{8,9},{9,8},{10,11... | collective-permute-start | bytes 4718600 | tf_op jit(solution)/shard_map/ppermute | solution.py:357
  75.4 0.3 collective-permute-start.12
  75.8 1.5 %collective-permute-start.14 = (f32[512,128]{1,0:T(8,128)S(1)}, f32[512,128]{1,0:T(8,128)S(1)}, u32[]{:S(2)}, u32[]{:S(2)}) collective-permute-start(f32[512,128]{1,0:T(8,128)S(1)} %copy-done.12), channel_id=1, source_target_pairs={{0,14},{1,15},{2,12},{3,13},{4,10},{5,11},{6,8},{7,9},{8,6},{9,7},... | collective-permute-start | bytes 786440 | tf_op jit(solution)/shard_map/ppermute | solution.py:357
  77.3 1.2 %collective-permute-done.11.rest_1_.rest_2_ = f32[3072,128]{1,0:T(8,128)S(1)} collective-permute-done((f32[3072,128]{1,0:T(8,128)S(1)}, f32[3072,128]{1,0:T(8,128)S(1)}, u32[]{:S(2)}, u32[]{:S(2)}) %collective-permute-start.11) | collective-permute-done | bytes 1572896 | tf_op jit(solution)/shard_map/ppermute | solution.py:357
  78.5 11.1 %worst0.1._.rest_0_ = f32[8,128]{1,0:T(8,128)S(1)} custom-call(s32[2]{0:T(128)S(1)} %copy-done.11, s32[80,128]{1,0:T(8,128)S(1)} %get-tuple-element.28.f_ref, s32[80,128]{1,0:T(8,128)S(1)} %get-tuple-element.29.t_ref, s32[2,20,128]{2,1,0:T(8,128)S(1)} %get-tuple-element.30._.cnt_ref, f32[80,128]{1,0:T(8,128)S(1)} %get-tuple-element.31.ratio_ref, ...), custom_call_target="tpu_custom_call" | custom-call | tf_op jit(solution)/shard_map/worst0/pallas_call | solution.py:402
  89.6 4.2 %collective-permute-done.12.refs_0_ = f32[512,128]{1,0:T(8,128)S(1)} collective-permute-done((f32[512,128]{1,0:T(8,128)S(1)}, f32[512,128]{1,0:T(8,128)S(1)}, u32[]{:S(2)}, u32[]{:S(2)}) %collective-permute-start.12) | collective-permute-done | bytes 262176 | tf_op jit(solution)/shard_map/ppermute | solution.py:357
  93.9 2.8 %collective-permute-start.13 = (f32[512,128]{1,0:T(8,128)S(1)}, f32[512,128]{1,0:T(8,128)}, u32[]{:S(2)}, u32[]{:S(2)}) collective-permute-start(f32[512,128]{1,0:T(8,128)S(1)} %join.4.rest_3_), channel_id=1, source_target_pairs={{0,1},{1,0},{2,3},{3,2},{4,5},{5,4},{6,7},{7,6},{8,9},{9,8},{10,11... | collective-permute-start | bytes 786440 | tf_op jit(solution)/shard_map/ppermute | solution.py:357
  96.7 3.1 %collective-permute-done.14.refs_0_ = f32[512,128]{1,0:T(8,128)S(1)} collective-permute-done((f32[512,128]{1,0:T(8,128)S(1)}, f32[512,128]{1,0:T(8,128)S(1)}, u32[]{:S(2)}, u32[]{:S(2)}) %collective-permute-start.14) | collective-permute-done | bytes 262176 | tf_op jit(solution)/shard_map/ppermute | solution.py:357
  99.8 0.7 join.5.rest_5_
  100.5 1.6 %collective-permute-start.15 = (f32[512,128]{1,0:T(8,128)}, f32[512,128]{1,0:T(8,128)}, u32[]{:S(2)}, u32[]{:S(2)}) collective-permute-start(f32[512,128]{1,0:T(8,128)} %join.5.rest_5_), channel_id=1, source_target_pairs={{0,1},{1,0},{2,3},{3,2},{4,5},{5,4},{6,7},{7,6},{8,9},{9,8},{10,11... | collective-permute-start | bytes 786440 | tf_op jit(solution)/shard_map/ppermute | solution.py:357
  102.2 0.7 copy.14
  102.9 0.8 copy-done.2
  103.7 0.8 copy-done.4
  104.4 5.9 %worst1.1.rest_0_ = f32[8,128]{1,0:T(8,128)S(1)} custom-call(s32[2]{0:T(128)S(1)} %copy-done.11, s32[80,128]{1,0:T(8,128)S(1)} %get-tuple-element.28.f_ref, s32[80,128]{1,0:T(8,128)S(1)} %get-tuple-element.29.t_ref, s32[2,20,128]{2,1,0:T(8,128)S(1)} %get-tuple-element.30._.cnt_ref, f32[80,128]{1,0:T(8,128)S(1)} %copy-done.2, f32[80,128]{1,0:T(8,128)S(1)} %copy-done.4, ...), custom_call_target="tpu_custom_call" | custom-call | tf_op jit(solution)/shard_map/worst1/pallas_call | solution.py:402
  110.3 8.3 %worst2.1 = f32[8,128]{1,0:T(8,128)S(1)} custom-call(s32[2]{0:T(128)S(1)} %copy-done.11, s32[80,128]{1,0:T(8,128)S(1)} %get-tuple-element.28.f_ref, s32[80,128]{1,0:T(8,128)S(1)} %get-tuple-element.29.t_ref, s32[2,20,128]{2,1,0:T(8,128)S(1)} %get-tuple-element.30._.cnt_ref, f32[80,128]{1,0:T(8,128)S(1)} %copy-done.2, f32[80,128]{1,0:T(8,128)S(1)} %copy-done.4, ...), custom_call_target="tpu_custom_call" | custom-call | tf_op jit(solution)/shard_map/worst2/pallas_call | solution.py:402
  118.6 0.1 collective-permute-start.16
  118.7 0.6 constant_dynamic-slice_fusion
  119.4 0.5 collective-permute-done.16
  119.8 0.6 dynamic-slice_bitcast_fusion
  (34 shorter events, 0.1 us)
Async XLA Ops:
  26.5 4.9 %collective-permute-start = (f32[24,128]{1,0:T(8,128)}, f32[24,128]{1,0:T(8,128)S(1)}, u32[]{:S(2)}, u32[]{:S(2)}) collective-permute-start(f32[24,128]{1,0:T(8,128)} %get-tuple-element.23), channel_id=1, source_target_pairs={{0,1},{1,0},{2,3},{3,2},{4,5},{5,4},{6,7},{7,6},{8,9},{9,8},{10,11... | collective-permute-start | bytes 36872 | tf_op jit(solution)/shard_map/ppermute | solution.py:357
  29.6 2.8 %collective-permute-start.1 = (f32[24,128]{1,0:T(8,128)}, f32[24,128]{1,0:T(8,128)S(1)}, u32[]{:S(2)}, u32[]{:S(2)}) collective-permute-start(f32[24,128]{1,0:T(8,128)} %get-tuple-element.23), channel_id=1, source_target_pairs={{0,2},{1,3},{2,0},{3,1},{4,6},{5,7},{6,4},{7,5},{8,10},{9,11},{10,... | collective-permute-start | bytes 36872 | tf_op jit(solution)/shard_map/ppermute | solution.py:357
  30.2 3.3 %collective-permute-start.2 = (f32[24,128]{1,0:T(8,128)}, f32[24,128]{1,0:T(8,128)S(1)}, u32[]{:S(2)}, u32[]{:S(2)}) collective-permute-start(f32[24,128]{1,0:T(8,128)} %get-tuple-element.23), channel_id=1, source_target_pairs={{0,3},{1,2},{2,1},{3,0},{4,7},{5,6},{6,5},{7,4},{8,11},{9,10},{10,... | collective-permute-start | bytes 36872 | tf_op jit(solution)/shard_map/ppermute | solution.py:357
  34.3 2.7 %collective-permute-start.3 = (f32[24,128]{1,0:T(8,128)S(1)}, f32[24,128]{1,0:T(8,128)S(1)}, u32[]{:S(2)}, u32[]{:S(2)}) collective-permute-start(f32[24,128]{1,0:T(8,128)S(1)} %add_add_fusion.1), channel_id=1, source_target_pairs={{0,4},{1,5},{2,6},{3,7},{4,0},{5,1},{6,2},{7,3},{8,12},{9,13},{10,... | collective-permute-start | bytes 36872 | tf_op jit(solution)/shard_map/ppermute | solution.py:357
  35.6 3.4 %collective-permute-start.4 = (f32[24,128]{1,0:T(8,128)S(1)}, f32[24,128]{1,0:T(8,128)S(1)}, u32[]{:S(2)}, u32[]{:S(2)}) collective-permute-start(f32[24,128]{1,0:T(8,128)S(1)} %add_add_fusion.1), channel_id=1, source_target_pairs={{0,8},{1,9},{2,10},{3,11},{4,12},{5,13},{6,14},{7,15},{8,0},{9,1},... | collective-permute-start | bytes 36872 | tf_op jit(solution)/shard_map/ppermute | solution.py:357
  35.6 3.4 %collective-permute-start.5 = (f32[24,128]{1,0:T(8,128)S(1)}, f32[24,128]{1,0:T(8,128)S(1)}, u32[]{:S(2)}, u32[]{:S(2)}) collective-permute-start(f32[24,128]{1,0:T(8,128)S(1)} %add_add_fusion.1), channel_id=1, source_target_pairs={{0,12},{1,13},{2,14},{3,15},{4,8},{5,9},{6,10},{7,11},{8,4},{9,5},... | collective-permute-start | bytes 36872 | tf_op jit(solution)/shard_map/ppermute | solution.py:357
  39.6 13.3 %copy-start.5 = (s32[20480]{0:T(1024)S(1)}, s32[20480]{0:T(1024)}, u32[]{:S(2)}) copy-start(s32[20480]{0:T(1024)} %param.10) | copy-start | bytes 245764
  39.6 13.3 %copy-start.6 = (s32[20480]{0:T(1024)S(1)}, s32[20480]{0:T(1024)}, u32[]{:S(2)}) copy-start(s32[20480]{0:T(1024)} %param.11) | copy-start | bytes 245764
  39.6 13.3 %copy-start.7 = (f32[20480]{0:T(1024)S(1)}, f32[20480]{0:T(1024)}, u32[]{:S(2)}) copy-start(f32[20480]{0:T(1024)} %param.13) | copy-start | bytes 245764
  39.6 13.3 %copy-start.9 = (s32[8192]{0:T(1024)S(1)}, s32[8192]{0:T(1024)}, u32[]{:S(2)}) copy-start(s32[8192]{0:T(1024)} %param.12) | copy-start | bytes 98308
  39.6 13.3 %copy-start.10 = (f32[20480]{0:T(1024)S(1)}, f32[20480]{0:T(1024)}, u32[]{:S(2)}) copy-start(f32[20480]{0:T(1024)} %param.15) | copy-start | bytes 245764
  39.6 13.3 %copy-start.11 = (s32[2]{0:T(128)S(1)}, s32[2]{0:T(128)}, u32[]{:S(2)}) copy-start(s32[2]{0:T(128)} %pad_add_fusion.me_ref) | copy-start | bytes 28
  46.3 29.5 %copy-start.12 = (f32[512,128]{1,0:T(8,128)S(1)}, f32[512,128]{1,0:T(8,128)}, u32[]{:S(2)}) copy-start(f32[512,128]{1,0:T(8,128)} %get-tuple-element.40) | copy-start | bytes 786436
  46.3 32.2 %copy-start = (f32[7,8,128]{2,1,0:T(8,128)S(1)}, f32[7,8,128]{2,1,0:T(8,128)}, u32[]{:S(2)}) copy-start(f32[7,8,128]{2,1,0:T(8,128)} %get-tuple-element.22.state_ref) | copy-start | bytes 86020
  46.3 21.2 %collective-permute-start.10 = (f32[512,128]{1,0:T(8,128)}, f32[512,128]{1,0:T(8,128)S(1)}, u32[]{:S(2)}, u32[]{:S(2)}) collective-permute-start(f32[512,128]{1,0:T(8,128)} %get-tuple-element.38), channel_id=1, source_target_pairs={{0,10},{1,11},{2,8},{3,9},{4,14},{5,15},{6,12},{7,13},{8,2},{9,3},... | collective-permute-start | bytes 786440 | tf_op jit(solution)/shard_map/ppermute | solution.py:357
  50.2 17.3 %collective-permute-start.6 = (f32[512,128]{1,0:T(8,128)}, f32[512,128]{1,0:T(8,128)S(1)}, u32[]{:S(2)}, u32[]{:S(2)}) collective-permute-start(f32[512,128]{1,0:T(8,128)} %get-tuple-element.34), channel_id=1, source_target_pairs={{0,2},{1,3},{2,0},{3,1},{4,6},{5,7},{6,4},{7,5},{8,10},{9,11},{10,... | collective-permute-start | bytes 786440 | tf_op jit(solution)/shard_map/ppermute | solution.py:357
  50.8 16.7 %collective-permute-start.7 = (f32[512,128]{1,0:T(8,128)}, f32[512,128]{1,0:T(8,128)S(1)}, u32[]{:S(2)}, u32[]{:S(2)}) collective-permute-start(f32[512,128]{1,0:T(8,128)} %get-tuple-element.35), channel_id=1, source_target_pairs={{0,4},{1,5},{2,6},{3,7},{4,0},{5,1},{6,2},{7,3},{8,12},{9,13},{10,... | collective-permute-start | bytes 786440 | tf_op jit(solution)/shard_map/ppermute | solution.py:357
  50.8 20.6 %collective-permute-start.8 = (f32[512,128]{1,0:T(8,128)}, f32[512,128]{1,0:T(8,128)S(1)}, u32[]{:S(2)}, u32[]{:S(2)}) collective-permute-start(f32[512,128]{1,0:T(8,128)} %get-tuple-element.36), channel_id=1, source_target_pairs={{0,6},{1,7},{2,4},{3,5},{4,2},{5,3},{6,0},{7,1},{8,14},{9,15},{10,... | collective-permute-start | bytes 786440 | tf_op jit(solution)/shard_map/ppermute | solution.py:357
  52.9 18.5 %collective-permute-start.9 = (f32[512,128]{1,0:T(8,128)}, f32[512,128]{1,0:T(8,128)S(1)}, u32[]{:S(2)}, u32[]{:S(2)}) collective-permute-start(f32[512,128]{1,0:T(8,128)} %get-tuple-element.37), channel_id=1, source_target_pairs={{0,8},{1,9},{2,10},{3,11},{4,12},{5,13},{6,14},{7,15},{8,0},{9,1},... | collective-permute-start | bytes 786440 | tf_op jit(solution)/shard_map/ppermute | solution.py:357
  67.5 22.1 %copy-start.1 = (f32[80,128]{1,0:T(8,128)}, f32[80,128]{1,0:T(8,128)S(1)}, u32[]{:S(2)}) copy-start(f32[80,128]{1,0:T(8,128)S(1)} %get-tuple-element.31.ratio_ref) | copy-start | bytes 122884
  67.5 22.1 %copy-start.3 = (f32[80,128]{1,0:T(8,128)}, f32[80,128]{1,0:T(8,128)S(1)}, u32[]{:S(2)}) copy-start(f32[80,128]{1,0:T(8,128)S(1)} %get-tuple-element.32.k_ref) | copy-start | bytes 122884
  71.4 1.0 copy-start.8
  72.3 3.1 %copy-start.13 = (f32[512,128]{1,0:T(8,128)S(1)}, f32[512,128]{1,0:T(8,128)}, u32[]{:S(2)}) copy-start(f32[512,128]{1,0:T(8,128)} %get-tuple-element.39) | copy-start | bytes 786436
  72.5 6.0 %collective-permute-start.11 = (f32[3072,128]{1,0:T(8,128)S(1)}, f32[3072,128]{1,0:T(8,128)S(1)}, u32[]{:S(2)}, u32[]{:S(2)}) collective-permute-start(f32[3072,128]{1,0:T(8,128)S(1)} %join.3.rest_0_.rest_1_), channel_id=1, source_target_pairs={{0,1},{1,0},{2,3},{3,2},{4,5},{5,4},{6,7},{7,6},{8,9},{9,8},{10,11... | collective-permute-start | bytes 4718600 | tf_op jit(solution)/shard_map/ppermute | solution.py:357
  75.4 18.4 %collective-permute-start.12 = (f32[512,128]{1,0:T(8,128)S(1)}, f32[512,128]{1,0:T(8,128)S(1)}, u32[]{:S(2)}, u32[]{:S(2)}) collective-permute-start(f32[512,128]{1,0:T(8,128)S(1)} %copy-done.13), channel_id=1, source_target_pairs={{0,12},{1,13},{2,14},{3,15},{4,8},{5,9},{6,10},{7,11},{8,4},{9,5},... | collective-permute-start | bytes 786440 | tf_op jit(solution)/shard_map/ppermute | solution.py:357
  75.8 24.0 %collective-permute-start.14 = (f32[512,128]{1,0:T(8,128)S(1)}, f32[512,128]{1,0:T(8,128)S(1)}, u32[]{:S(2)}, u32[]{:S(2)}) collective-permute-start(f32[512,128]{1,0:T(8,128)S(1)} %copy-done.12), channel_id=1, source_target_pairs={{0,14},{1,15},{2,12},{3,13},{4,10},{5,11},{6,8},{7,9},{8,6},{9,7},... | collective-permute-start | bytes 786440 | tf_op jit(solution)/shard_map/ppermute | solution.py:357
  93.9 9.0 %collective-permute-start.13 = (f32[512,128]{1,0:T(8,128)S(1)}, f32[512,128]{1,0:T(8,128)}, u32[]{:S(2)}, u32[]{:S(2)}) collective-permute-start(f32[512,128]{1,0:T(8,128)S(1)} %join.4.rest_3_), channel_id=1, source_target_pairs={{0,1},{1,0},{2,3},{3,2},{4,5},{5,4},{6,7},{7,6},{8,9},{9,8},{10,11... | collective-permute-start | bytes 786440 | tf_op jit(solution)/shard_map/ppermute | solution.py:357
  100.5 9.8 %collective-permute-start.15 = (f32[512,128]{1,0:T(8,128)}, f32[512,128]{1,0:T(8,128)}, u32[]{:S(2)}, u32[]{:S(2)}) collective-permute-start(f32[512,128]{1,0:T(8,128)} %join.5.rest_5_), channel_id=1, source_target_pairs={{0,1},{1,0},{2,3},{3,2},{4,5},{5,4},{6,7},{7,6},{8,9},{9,8},{10,11... | collective-permute-start | bytes 786440 | tf_op jit(solution)/shard_map/ppermute | solution.py:357
  102.9 0.8 copy-start.2
  103.7 0.8 copy-start.4
  118.6 1.2 collective-permute-start.16

commit v5 on v4

--- a/solution.py
+++ b/solution.py
@@ -10,6 +10,8 @@
 
 STEPS = 3
 LANES = 128
+LATE = 2
+CHUNKS = 1
 GROUP = 4
 SINE = (3.1415926444, -5.1677100819, 2.5500775297, -0.5982913039, 0.0776576582)
 VMEM = pl.BlockSpec(memory_space=pltpu.VMEM)
@@ -82,13 +84,16 @@
 
 def ends_kernel(width, me_ref, ids_ref, from_ref, to_ref, slot_ref, sus_ref, chg_ref, base_ref, zinv_ref,
                 state_ref, pick_ref, own_base_ref, rows_ref, from_v, to_v, slot_v, sus_v, chg_v, base_v,
-                zinv_v, ends_v, ends_s, rows, sem, out_sem):
+                zinv_v, ends_v, ends_s, rows, sem, out_sem, zinv_sem):
     total = ids_ref.shape[1]
     blocks = total // LANES
     first = me_ref[0] * width * LANES
     copies = stage([(from_ref, from_v), (to_ref, to_v), (slot_ref, slot_v), (sus_ref, sus_v),
-                    (chg_ref, chg_v), (base_ref, base_v), (zinv_ref, zinv_v)], sem)
-    for copy in copies[:-1]:
+                    (chg_ref, chg_v), (base_ref, base_v)], sem)
+    part = zinv_v.shape[0] // CHUNKS
+    cuts = [pl.ds(i * part, part) for i in range(CHUNKS)]
+    zinv_copies = stage([(zinv_ref.at[c], zinv_v.at[c]) for c in cuts], zinv_sem)
+    for copy in copies:
         copy.wait()
     branch = columns([from_v[...].astype(jnp.float32), to_v[...].astype(jnp.float32), sus_v[...], chg_v[...]])
     slot = columns([slot_v[...].astype(jnp.float32)])
@@ -116,7 +121,8 @@
     for t in range(width):
         own_base_ref[t:t + 1, :] = base_v[pl.ds(me_ref[0] * width + t, 1), :]
     copy.wait()
-    copies[-1].wait()
+    for copy in zinv_copies:
+        copy.wait()
 
     def block(b, slot):
         def fetch(g, carry):
@@ -198,7 +204,8 @@
 
 def prep_kernel(unit, chips, me_ref, from_ref, to_ref, slot_ref, sus_ref, rate_ref,
                 f_ref, t_ref, ratio_ref, k_ref, cnt_ref):
-    half = f_ref.shape[0]
+    half = ratio_ref.shape[0]
+    groups = half // GROUP
     me = me_ref[0]
     start = (me & 1) * half
     flip = me * unit
@@ -210,6 +217,7 @@
     before = jnp.where(before, 1.0, 0.0).astype(jnp.bfloat16)
     lane = lax.broadcasted_iota(jnp.int32, (1, LANES), 1).astype(jnp.float32)
     slots = lax.broadcasted_iota(jnp.int32, (GROUP * LANES, LANES), 0).astype(jnp.float32)
+    cnt_ref[...] = jnp.zeros_like(cnt_ref)
 
     def place(bus_ref, row):
         bus = jnp.concatenate([bus_ref[pl.ds(row + i, 1), :] for i in range(GROUP)], 1)
@@ -221,25 +229,20 @@
     def group(g, carry):
         f_chip, f = place(from_ref, start + g * GROUP)
         t_chip, t = place(to_ref, start + g * GROUP)
-        chip = jnp.maximum(f_chip, t_chip)
-        first = jnp.where(chip < chips - 2, 1.0, 0.0)
-        second = jnp.where(chip == chips - 2, 1.0, 0.0)
+        first = jnp.where(jnp.maximum(f_chip, t_chip) < chips - LATE, 1.0, 0.0)
         tile = lambda a, i: a[:, i * LANES:(i + 1) * LANES]
-        flags = jnp.concatenate([tile(a, i) for a in (first, second) for i in range(GROUP)], 0)
+        flags = jnp.concatenate([tile(first, i) for i in range(GROUP)]
+                                + [jnp.zeros((8 - GROUP, LANES), jnp.float32)], 0)
         ahead = jnp.dot(flags.astype(jnp.bfloat16), before, preferred_element_type=jnp.float32)
         sums = jnp.sum(flags, axis=1, keepdims=True)
-        n_first = sum(sums[i:i + 1] for i in range(GROUP))
-        n_second = sum(sums[GROUP + i:GROUP + i + 1] for i in range(GROUP))
-        off_first = off_second = jnp.zeros((1, 1), jnp.float32)
+        count = sum(sums[i:i + 1] for i in range(GROUP))
+        offset = jnp.zeros((1, 1), jnp.float32)
         total = jnp.zeros((16, GROUP * LANES), jnp.float32)
         for i in range(GROUP):
-            c_first = off_first + ahead[i:i + 1]
-            c_second = off_second + ahead[GROUP + i:GROUP + i + 1]
-            rest = n_first + n_second + (lane + float(i * LANES)) - c_first - c_second
-            goal = jnp.where(tile(first, i) > 0.5, c_first,
-                             jnp.where(tile(second, i) > 0.5, n_first + c_second, rest))
-            off_first = off_first + sums[i:i + 1]
-            off_second = off_second + sums[GROUP + i:GROUP + i + 1]
+            front = offset + ahead[i:i + 1]
+            rest = count + (lane + float(i * LANES)) - front
+            goal = jnp.where(tile(first, i) > 0.5, front, rest)
+            offset = offset + sums[i:i + 1]
             hot = jnp.where(slots == goal, 1.0, 0.0).astype(jnp.bfloat16)
             row = pl.ds(start + g * GROUP + i, 1)
             rows = [tile(f, i) >> 7, tile(f, i) & 127, tile(t, i) >> 7, tile(t, i) & 127]
@@ -249,16 +252,15 @@
             values = jnp.concatenate(rows, 0).astype(jnp.bfloat16)
             total += lax.dot_general(values, hot, (((1,), (1,)), ((), ())), preferred_element_type=jnp.float32)
         for i in range(GROUP):
-            out = pl.ds(g * GROUP + i, 1)
+            out = pl.ds(i * groups + g, 1)
             part = total[:, i * LANES:(i + 1) * LANES]
             f_ref[out, :] = (part[0:1] * 128.0 + part[1:2]).astype(jnp.int32)
             t_ref[out, :] = (part[2:3] * 128.0 + part[3:4]).astype(jnp.int32)
             ratio_ref[out, :] = part[4:5] + part[5:6] + part[6:7]
             origin = ((start + g * GROUP) * LANES).astype(jnp.float32)
             k_ref[out, :] = part[7:8] * 128.0 + part[8:9] + origin
-        wide = lambda a: jnp.broadcast_to(a, (1, LANES)).astype(jnp.int32) >> 7
-        cnt_ref[0, pl.ds(g, 1), :] = wide(n_first)
-        cnt_ref[1, pl.ds(g, 1), :] = wide(n_first + n_second)
+        blocks = jnp.broadcast_to(count, (1, LANES)).astype(jnp.int32) >> 7
+        cnt_ref[...] = jnp.where(lane == g.astype(jnp.float32), blocks, cnt_ref[...])
         return carry
 
     lax.fori_loop(0, half // GROUP, group, 0)
@@ -271,12 +273,15 @@
         copy.wait()
 
 
-def worst_kernel(level, me_ref, f_ref, t_ref, cnt_ref, ratio_ref, k_ref, state_ref, *rest):
-    n = 2 * level + 2
-    if level:
-        best_in, *rest = rest
-    pieces, (best, table, f_s, t_s, cnt_s, diff, sem) = rest[:n], rest[n:]
-    pairs = [(f_ref, f_s), (t_ref, t_s), (cnt_ref, cnt_s)]
+def worst_kernel(late, me_ref, f_ref, t_ref, cnt_ref, ratio_ref, k_ref, state_ref, *rest):
+    if late:
+        best_ref, *rest = rest
+    pieces, (out_ref, table, f_s, t_s, cnt_s, best, diff, sem) = rest[:2 * late + 2], rest[2 * late + 2:]
+    half = f_ref.shape[0]
+    groups = half // GROUP
+    side = [pl.ds(0, half // 2), pl.ds(half // 2, half // 2)]
+    main, spare = side[late], side[1 - late]
+    pairs = [(cnt_ref, cnt_s), (f_ref.at[main], f_s.at[main]), (t_ref.at[main], t_s.at[main])]
     row = 0
     for own, other in zip(pieces[::2], pieces[1::2]):
         size = own.shape[0]
@@ -284,35 +289,40 @@
                   (other, table.at[pl.ds(table.shape[0] // 2 + row, size)])]
         row += size
     copies = stage(pairs, sem)
-    half = f_ref.shape[0]
     ids = state_ref[6, pl.ds(me_ref[0] >> 1, 1), :]
-    best[...] = best_in[...] if level else jnp.zeros_like(best)
+    best[...] = best_ref[...] if late else jnp.zeros_like(best)
     for copy in copies:
         copy.wait()
-
-    def block(b, carry):
-        for j in range(LANES):
-            diff[pl.ds(j, 1), :] = table[pl.ds(f_s[b, j], 1), :] - table[pl.ds(t_s[b, j], 1), :]
-        turn = diff[...]
-        turn = turn - jnp.round(turn)
-        square = turn * turn
-        poly = SINE[4]
-        for c in SINE[3::-1]:
-            poly = poly * square + c
-        ratio = jnp.broadcast_to(ratio_ref[pl.ds(b, 1), :], (LANES, LANES)).T
-        branch = jnp.broadcast_to(k_ref[pl.ds(b, 1), :], (LANES, LANES)).T
-        load = jnp.where(branch == ids, 0.0, jnp.abs(turn * poly) * ratio)
-        best[...] = jnp.maximum(best[...], jnp.max(load.reshape(LANES // 8, 8, LANES), axis=0))
-        return carry
+    bound = cnt_s[0, 0]
+    for g in range(1, groups):
+        bound = jnp.minimum(bound, cnt_s[0, g]) if late else jnp.maximum(bound, cnt_s[0, g])
+
+    @pl.when(bound < GROUP // 2 if late else bound > GROUP // 2)
+    def _():
+        for copy in stage([(f_ref.at[spare], f_s.at[spare]), (t_ref.at[spare], t_s.at[spare])], sem):
+            copy.wait()
 
     def group(g, carry):
-        low = cnt_s[level - 1, g, 0] if level else 0
-        high = GROUP if level == 2 else cnt_s[level, g, 0]
-        return lax.fori_loop(g * GROUP + low, g * GROUP + high, block, carry)
-
-    lax.fori_loop(0, half // GROUP, group, 0)
-    if level == 2:
-        best[...] = jnp.broadcast_to(jnp.max(best[...], axis=0, keepdims=True), best.shape)
+        def block(i, carry):
+            b = i * groups + g
+            for j in range(LANES):
+                diff[pl.ds(j, 1), :] = table[pl.ds(f_s[b, j], 1), :] - table[pl.ds(t_s[b, j], 1), :]
+            turn = diff[...]
+            turn = turn - jnp.round(turn)
+            square = turn * turn
+            poly = SINE[4]
+            for c in SINE[3::-1]:
+                poly = poly * square + c
+            scale = jnp.broadcast_to(ratio_ref[pl.ds(b, 1), :], (LANES, LANES)).T
+            branch = jnp.broadcast_to(k_ref[pl.ds(b, 1), :], (LANES, LANES)).T
+            load = jnp.where(branch == ids, 0.0, jnp.abs(turn * poly) * scale)
+            best[...] = jnp.maximum(best[...], jnp.max(load.reshape(LANES // 8, 8, LANES), axis=0))
+            return carry
+
+        return lax.fori_loop(cnt_s[0, g] if late else 0, GROUP if late else cnt_s[0, g], block, carry)
+
+    lax.fori_loop(0, groups, group, 0)
+    out_ref[...] = jnp.max(best[...], axis=0, keepdims=True) if late else best[...]
 
 
 def per_device(
@@ -326,7 +336,7 @@
     chips = n_col // 2
     assert own * 2 == LANES and chips & (chips - 1) == 0 and chips > 2
     me = lax.axis_index("col")
-    where = jnp.stack([me, jnp.int32(n_col)])
+    where = me[None]
     tab = lambda a: a.reshape(-1, LANES)
     from2, to2, slot2, sus2, chg2, rate2, base2 = map(
         tab, (branch_from, branch_to, bus_slot, susceptance, charging, rating, base_angles)
@@ -349,8 +359,8 @@
         out_specs=[VMEM] * 3 + [ANY],
         scratch_shapes=[like(from2), like(to2), like(slot2), like(sus2), like(chg2), like(base2), like(flat),
                         pltpu.VMEM((2 * blocks, LANES), jnp.int32), pltpu.SMEM((2 * blocks, LANES), jnp.int32),
-                        pltpu.VMEM((2,) + row_shape, jnp.float32), pltpu.SemaphoreType.DMA((7,)),
-                        pltpu.SemaphoreType.DMA((2,))],
+                        pltpu.VMEM((2,) + row_shape, jnp.float32), pltpu.SemaphoreType.DMA((6,)),
+                        pltpu.SemaphoreType.DMA((2,)), pltpu.SemaphoreType.DMA((CHUNKS,))],
         compiler_params=params(60),
     )(where, ids, from2, to2, slot2, sus2, chg2, base2, flat)
 
@@ -378,7 +388,7 @@
         functools.partial(prep_kernel, cols, chips),
         name="prep",
         out_shape=[i32(half, LANES), i32(half, LANES), f32(half, LANES), f32(half, LANES),
-                   i32(2, half // GROUP, LANES)],
+                   i32(1, LANES)],
         in_specs=[SMEM] + [VMEM] * 5,
         out_specs=[VMEM] * 5,
         compiler_params=params(16),
@@ -402,23 +412,22 @@
         return pl.pallas_call(
             functools.partial(worst_kernel, level),
             name=f"worst{level}",
-            out_shape=f32(8, LANES),
-            in_specs=[SMEM] + [ANY] * 3 + [VMEM] * (3 + min(level, 1)) + [ANY] * (2 * level + 2),
+            out_shape=f32(1 if level else 8, LANES),
+            in_specs=[SMEM] + [ANY] * 3 + [VMEM] * (3 + level) + [ANY] * (len(operands) - level),
             out_specs=VMEM,
-            scratch_shapes=[pltpu.VMEM((buses, LANES), jnp.float32)]
-            + [pltpu.SMEM(a.shape, a.dtype) for a in (f_rel, t_rel, counts)]
-            + [pltpu.VMEM((LANES, LANES), jnp.float32), pltpu.SemaphoreType.DMA((2 * level + 5,))],
+            scratch_shapes=[pltpu.VMEM((buses, LANES), jnp.float32), pltpu.SMEM(f_rel.shape, jnp.int32),
+                            pltpu.SMEM(t_rel.shape, jnp.int32), pltpu.SMEM(counts.shape, jnp.int32),
+                            pltpu.VMEM((8, LANES), jnp.float32), pltpu.VMEM((LANES, LANES), jnp.float32),
+                            pltpu.SemaphoreType.DMA((3 + len(operands),))],
             compiler_params=params(16),
         )(where, f_rel, t_rel, counts, ratio, k_rel, state, *operands)
 
-    early = join(counts, got[:-2])
+    early = join(counts, got[:-LATE])
     best = worst_of(0, *early)
-    middle, late = join(best, got[-2:-1]), join(best, got[-1:])
-    best = worst_of(1, best, *early, *middle)
-    best = worst_of(2, best, *early, *middle, *late)
-    worst = lax.slice(best, (0, 0), (1, LANES))
-    worst = lax.dynamic_slice(jnp.maximum(worst, swap(worst, 1))[0], ((me & 1) * own,), (own,))
-    inj = lax.dynamic_slice(injections.reshape(2, total), (0, me * own), (2, own))
+    worst = worst_of(1, best, *early, *join(best, got[-LATE:]))
+    mine = lambda a, b: lax.dynamic_slice(a, (jnp.int32(0),) * (a.ndim - len(b)) + b, a.shape[:1] + (1,) * (a.ndim - 2) + (own,))
+    worst = jnp.maximum(mine(worst, ((me & 1) * own,)), mine(swap(worst, 1), ((me & 1) * own,))).reshape(own)
+    inj = mine(injections, (me >> 1, (me & 1) * own)).reshape(2, own)
     return inj, deviation, worst
 
 

time: 121 us -> 115 us (0.950)
  Pallas kernels: 62.5 us -> 55.1 us
  waiting for transfers between devices: 17.1 us -> 23.7 us
  starting transfers between devices: 23.4 us -> 20.9 us
  local copies, waits for them, and re-layouts: 5.36 us -> 3.19 us
    ppermute x17 -> x16, waiting for transfers between devices: 17.1 us -> 23.7 us  [per_device(): lax.ppermute(a, 'col', [(i, i ^ m) for i in range(n_col)])]
    pallas_call x3 -> x2, Pallas kernels: 25.3 us -> 19.2 us  [worst_of(): pl.pallas_call(functools.partial(worst_kernel, level), name=f'worst{level...]
    ppermute x17 -> x16, starting transfers between devices: 23.4 us -> 20.9 us  [per_device(): lax.ppermute(a, 'col', [(i, i ^ m) for i in range(n_col)])]
    unnamed x29 -> x18, local copies, waits for them, and re-layouts: 3.25 us -> 0.98 us
  transfers between devices with their start and end apart: 17 -> 16, of which waited for: 8 -> 9; matrix products, arithmetic and copies ran while one was open for 1% -> 1% of each run, Pallas kernels for 27% -> 20%
where the time goes in v5:
time: 115 us
  Pallas kernels  55.1 us (48%)
  waiting for transfers between devices  23.7 us (21%)
  starting transfers between devices  20.9 us (18%)
  blocking collectives  9.25 us (8%)
  local copies, waits for them, and re-layouts  3.19 us (3%)
  other arithmetic  1.9 us (2%)
    ppermute x16, waiting for transfers between devices, per_device(): lax.ppermute(a, 'col', [(i, i ^ m) for i in range(n_col)])  23.7 us
    ppermute x16, starting transfers between devices, per_device(): lax.ppermute(a, 'col', [(i, i ^ m) for i in range(n_col)])  20.9 us
    pallas_call x2, Pallas kernels, worst_of(): pl.pallas_call(functools.partial(worst_kernel, level), name=f'worst{level...  19.2 us
    pallas_call x1, Pallas kernels, per_device(): pl.pallas_call(functools.partial(ends_kernel, width), name='ends', out_sh...  15.1 us
    pallas_call x1, Pallas kernels, per_device(): pl.pallas_call(functools.partial(prep_kernel, cols, chips), name='prep',...  13.9 us
    psum x1, blocking collectives, per_device(): ids = lax.psum(ids[None], 'col')  9.25 us
    pallas_call x1, Pallas kernels, per_device(): pl.pallas_call(functools.partial(spread_kernel, chips), name='spread', ou...  5.8 us
  transfers between devices with their start and end apart: 16, of which 9 were waited for; matrix products, arithmetic and copies ran while one was open for 1% of the time, Pallas kernels for 20%

profile of v5, /device:TPU:9, one launch (start us, length us, event | category | flops | bytes accessed | tf_op | source)
XLA Modules:
  0.0 114.8 jit_solution(3210532662638880102)
XLA Ops:
  0.6 0.9 dynamic_update_slice.4
  1.5 9.3 %psum.7.ids_ref = s32[1,1024]{1,0:T(1,128)} all-reduce(s32[1,1024]{1,0:T(1,128)S(1)} %dynamic_update_slice.4), channel_id=1, replica_groups=mesh['parts'=2,'col'=16] {'col'}, use_global_device_ids=true, to_apply=%region_0.0 | all-reduce | flops 1024 | bytes 8192 | tf_op jit(solution)/shard_map/psum | solution.py:349
  10.8 15.1 %ends.1 = (f32[7,8,128]{2,1,0:T(8,128)}, f32[24,128]{1,0:T(8,128)}, f32[4,128]{1,0:T(4,128)}, f32[8,2,4,128,128]{4,3,2,1,0:T(8,128)}) custom-call(s32[1]{0:T(128)} %bitcast.me_ref, s32[1,1024]{1,0:T(1,128)} %psum.7.ids_ref, s32[160,128]{1,0:T(8,128)} %bitcast.17, s32[160,128]{1,0:T(8,128)} %bitcast.19, s32[64,128]{1,0:T(8,128)} %bitcast.23, ...), custom_call_target="tpu_custom_call" | custom-call | tf_op jit(solution)/shard_map/ends/pallas_call | solution.py:354
  25.9 3.2 %collective-permute-start = (f32[24,128]{1,0:T(8,128)}, f32[24,128]{1,0:T(8,128)S(1)}, u32[]{:S(2)}, u32[]{:S(2)}) collective-permute-start(f32[24,128]{1,0:T(8,128)} %get-tuple-element.23), channel_id=1, source_target_pairs={{0,1},{1,0},{2,3},{3,2},{4,5},{5,4},{6,7},{7,6},{8,9},{9,8},{10,11... | collective-permute-start | bytes 36872 | tf_op jit(solution)/shard_map/ppermute | solution.py:367
  29.1 0.6 collective-permute-start.1
  29.7 1.1 collective-permute-start.2
  30.8 0.0 collective-permute-done
  30.8 1.1 collective-permute-done.1
  31.8 1.1 %collective-permute-done.2 = f32[24,128]{1,0:T(8,128)S(1)} collective-permute-done((f32[24,128]{1,0:T(8,128)}, f32[24,128]{1,0:T(8,128)S(1)}, u32[]{:S(2)}, u32[]{:S(2)}) %collective-permute-start.2) | collective-permute-done | bytes 12320 | tf_op jit(solution)/shard_map/ppermute | solution.py:367
  33.0 0.7 add_add_fusion.1
  33.7 1.3 %collective-permute-start.3 = (f32[24,128]{1,0:T(8,128)S(1)}, f32[24,128]{1,0:T(8,128)S(1)}, u32[]{:S(2)}, u32[]{:S(2)}) collective-permute-start(f32[24,128]{1,0:T(8,128)S(1)} %add_add_fusion.1), channel_id=1, source_target_pairs={{0,4},{1,5},{2,6},{3,7},{4,0},{5,1},{6,2},{7,3},{8,12},{9,13},{10,... | collective-permute-start | bytes 36872 | tf_op jit(solution)/shard_map/ppermute | solution.py:367
  35.0 0.1 collective-permute-start.4
  35.0 1.3 %collective-permute-start.5 = (f32[24,128]{1,0:T(8,128)S(1)}, f32[24,128]{1,0:T(8,128)S(1)}, u32[]{:S(2)}, u32[]{:S(2)}) collective-permute-start(f32[24,128]{1,0:T(8,128)S(1)} %add_add_fusion.1), channel_id=1, source_target_pairs={{0,12},{1,13},{2,14},{3,15},{4,8},{5,9},{6,10},{7,11},{8,4},{9,5},... | collective-permute-start | bytes 36872 | tf_op jit(solution)/shard_map/ppermute | solution.py:367
  36.3 0.0 collective-permute-done.3
  36.4 2.1 %collective-permute-done.4 = f32[24,128]{1,0:T(8,128)S(1)} collective-permute-done((f32[24,128]{1,0:T(8,128)S(1)}, f32[24,128]{1,0:T(8,128)S(1)}, u32[]{:S(2)}, u32[]{:S(2)}) %collective-permute-start.4) | collective-permute-done | bytes 12320 | tf_op jit(solution)/shard_map/ppermute | solution.py:367
  38.4 0.0 collective-permute-done.5
  38.4 0.6 add_add_fusion.pick_ref
  39.0 0.0 copy-start.6
  39.1 5.8 %spread.1 = (f32[2,8,128]{2,1,0:T(8,128)}, f32[1024,512]{1,0:T(8,128)}, f32[512,128]{1,0:T(8,128)}, f32[512,128]{1,0:T(8,128)}, f32[512,128]{1,0:T(8,128)}, /*in...) custom-call(s32[1]{0:T(128)} %bitcast.me_ref, ...), custom_call_target="tpu_custom_call" | custom-call | tf_op jit(solution)/shard_map/spread/pallas_call | solution.py:373
  44.9 3.9 %collective-permute-start.10 = (f32[512,128]{1,0:T(8,128)}, f32[512,128]{1,0:T(8,128)S(1)}, u32[]{:S(2)}, u32[]{:S(2)}) collective-permute-start(f32[512,128]{1,0:T(8,128)} %get-tuple-element.38), channel_id=1, source_target_pairs={{0,10},{1,11},{2,8},{3,9},{4,14},{5,15},{6,12},{7,13},{8,2},{9,3},... | collective-permute-start | bytes 786440 | tf_op jit(solution)/shard_map/ppermute | solution.py:367
  48.8 0.6 collective-permute-start.6
  49.4 0.0 collective-permute-start.7
  49.4 2.1 %collective-permute-start.8 = (f32[512,128]{1,0:T(8,128)}, f32[512,128]{1,0:T(8,128)S(1)}, u32[]{:S(2)}, u32[]{:S(2)}) collective-permute-start(f32[512,128]{1,0:T(8,128)} %get-tuple-element.36), channel_id=1, source_target_pairs={{0,6},{1,7},{2,4},{3,5},{4,2},{5,3},{6,0},{7,1},{8,14},{9,15},{10,... | collective-permute-start | bytes 786440 | tf_op jit(solution)/shard_map/ppermute | solution.py:367
  51.5 0.0 collective-permute-start.9
  51.5 0.0 copy-done.1
  51.5 13.9 %prep.1 = (s32[80,128]{1,0:T(8,128)S(1)}, s32[80,128]{1,0:T(8,128)S(1)}, f32[80,128]{1,0:T(8,128)S(1)}, f32[80,128]{1,0:T(8,128)S(1)}, s32[1,128]{1,0:T(1,128)S(1)}) custom-call(s32[1]{0:T(128)} %bitcast.me_ref, s32[160,128]{1,0:T(8,128)S(1)} %bitcast.18, s32[160,128]{1,0:T(8,128)S(1)} %bitcast.20, s32[64,128]{1,0:T(8,128)S(1)} %bitcast.24, ...), custom_call_target="tpu_custom_call" | custom-call | tf_op jit(solution)/shard_map/prep/pallas_call | solution.py:387
  65.4 0.0 collective-permute-done.10.refs_5_
  65.5 0.7 collective-permute-done.6.refs_1_
  66.1 0.0 collective-permute-done.7.refs_2_
  66.1 3.8 %collective-permute-done.8.refs_3_ = f32[512,128]{1,0:T(8,128)S(1)} collective-permute-done((f32[512,128]{1,0:T(8,128)}, f32[512,128]{1,0:T(8,128)S(1)}, u32[]{:S(2)}, u32[]{:S(2)}) %collective-permute-start.8) | collective-permute-done | bytes 262176 | tf_op jit(solution)/shard_map/ppermute | solution.py:367
  70.0 0.0 collective-permute-done.9.refs_4_
  70.0 0.9 copy-done.3
  70.9 0.2 join.2.rest_0_.rest_1_
  71.1 2.9 %collective-permute-start.11 = (f32[3072,128]{1,0:T(8,128)S(1)}, f32[3072,128]{1,0:T(8,128)S(1)}, u32[]{:S(2)}, u32[]{:S(2)}) collective-permute-start(f32[3072,128]{1,0:T(8,128)S(1)} %join.2.rest_0_.rest_1_), channel_id=1, source_target_pairs={{0,1},{1,0},{2,3},{3,2},{4,5},{5,4},{6,7},{7,6},{8,9},{9,8},{10,11... | collective-permute-start | bytes 4718600 | tf_op jit(solution)/shard_map/ppermute | solution.py:367
  74.0 0.3 collective-permute-start.12
  74.4 1.5 %collective-permute-start.13 = (f32[512,128]{1,0:T(8,128)S(1)}, f32[512,128]{1,0:T(8,128)S(1)}, u32[]{:S(2)}, u32[]{:S(2)}) collective-permute-start(f32[512,128]{1,0:T(8,128)S(1)} %copy-done.7), channel_id=1, source_target_pairs={{0,14},{1,15},{2,12},{3,13},{4,10},{5,11},{6,8},{7,9},{8,6},{9,7},... | collective-permute-start | bytes 786440 | tf_op jit(solution)/shard_map/ppermute | solution.py:367
  75.9 1.2 %collective-permute-done.11.rest_1_.rest_2_ = f32[3072,128]{1,0:T(8,128)S(1)} collective-permute-done((f32[3072,128]{1,0:T(8,128)S(1)}, f32[3072,128]{1,0:T(8,128)S(1)}, u32[]{:S(2)}, u32[]{:S(2)}) %collective-permute-start.11) | collective-permute-done | bytes 1572896 | tf_op jit(solution)/shard_map/ppermute | solution.py:367
  77.1 9.5 %worst0.1._.rest_0_ = f32[8,128]{1,0:T(8,128)S(1)} custom-call(s32[1]{0:T(128)} %bitcast.me_ref, s32[80,128]{1,0:T(8,128)S(1)} %get-tuple-element.28.f_ref, s32[80,128]{1,0:T(8,128)S(1)} %get-tuple-element.29.t_ref, s32[1,128]{1,0:T(1,128)S(1)} %get-tuple-element.30._.cnt_ref, f32[80,128]{1,0:T(8,128)S(1)} %get-tuple-element.31.ratio_ref, ...), custom_call_target="tpu_custom_call" | custom-call | tf_op jit(solution)/shard_map/worst0/pallas_call | solution.py:412
  86.6 5.8 %collective-permute-done.12.refs_0_ = f32[512,128]{1,0:T(8,128)S(1)} collective-permute-done((f32[512,128]{1,0:T(8,128)S(1)}, f32[512,128]{1,0:T(8,128)S(1)}, u32[]{:S(2)}, u32[]{:S(2)}) %collective-permute-start.12) | collective-permute-done | bytes 262176 | tf_op jit(solution)/shard_map/ppermute | solution.py:367
  92.4 6.0 %collective-permute-done.13.refs_1_ = f32[512,128]{1,0:T(8,128)S(1)} collective-permute-done((f32[512,128]{1,0:T(8,128)S(1)}, f32[512,128]{1,0:T(8,128)S(1)}, u32[]{:S(2)}, u32[]{:S(2)}) %collective-permute-start.13) | collective-permute-done | bytes 262176 | tf_op jit(solution)/shard_map/ppermute | solution.py:367
  98.4 0.9 join.3.rest_3_
  99.3 1.6 %collective-permute-start.14 = (f32[1024,128]{1,0:T(8,128)}, f32[1024,128]{1,0:T(8,128)}, u32[]{:S(2)}, u32[]{:S(2)}) collective-permute-start(f32[1024,128]{1,0:T(8,128)} %join.3.rest_3_), channel_id=1, source_target_pairs={{0,1},{1,0},{2,3},{3,2},{4,5},{5,4},{6,7},{7,6},{8,9},{9,8},{10,11... | collective-permute-start | bytes 1572872 | tf_op jit(solution)/shard_map/ppermute | solution.py:367
  100.9 1.9 %collective-permute-done.14.rest_4_ = f32[1024,128]{1,0:T(8,128)} collective-permute-done((f32[1024,128]{1,0:T(8,128)}, f32[1024,128]{1,0:T(8,128)}, u32[]{:S(2)}, u32[]{:S(2)}) %collective-permute-start.14) | collective-permute-done | bytes 524320 | tf_op jit(solution)/shard_map/ppermute | solution.py:367
  102.8 9.7 %worst1.1 = f32[1,128]{1,0:T(1,128)S(1)} custom-call(s32[1]{0:T(128)} %bitcast.me_ref, s32[80,128]{1,0:T(8,128)S(1)} %get-tuple-element.28.f_ref, s32[80,128]{1,0:T(8,128)S(1)} %get-tuple-element.29.t_ref, s32[1,128]{1,0:T(1,128)S(1)} %get-tuple-element.30._.cnt_ref, f32[80,128]{1,0:T(8,128)S(1)} %get-tuple-element.31.ratio_ref, ...), custom_call_target="tpu_custom_call" | custom-call | tf_op jit(solution)/shard_map/worst1/pallas_call | solution.py:412
  112.5 0.4 collective-permute-start.15
  112.9 1.3 %constant_dynamic-slice_fusion.2 = f32[2,1,64]{2,1,0:T(1,128)} fusion(f32[2,8,128]{2,1,0:T(8,128)} %get-tuple-element.26, s32[]{:T(128)S(6)} %select_n.12, s32[]{:T(128)S(6)} %select_n.13), kind=kLoop, calls=%fused_computation.4 | loop fusion | bytes 1032 | tf_op jit(solution)/shard_map/dynamic_slice | solution.py:428
  114.2 0.0 collective-permute-done.15
  114.3 0.6 fusion.1
  (16 shorter events, 0.0 us)
Async XLA Ops:
  25.9 4.9 %collective-permute-start = (f32[24,128]{1,0:T(8,128)}, f32[24,128]{1,0:T(8,128)S(1)}, u32[]{:S(2)}, u32[]{:S(2)}) collective-permute-start(f32[24,128]{1,0:T(8,128)} %get-tuple-element.23), channel_id=1, source_target_pairs={{0,1},{1,0},{2,3},{3,2},{4,5},{5,4},{6,7},{7,6},{8,9},{9,8},{10,11... | collective-permute-start | bytes 36872 | tf_op jit(solution)/shard_map/ppermute | solution.py:367
  29.1 2.8 %collective-permute-start.1 = (f32[24,128]{1,0:T(8,128)}, f32[24,128]{1,0:T(8,128)S(1)}, u32[]{:S(2)}, u32[]{:S(2)}) collective-permute-start(f32[24,128]{1,0:T(8,128)} %get-tuple-element.23), channel_id=1, source_target_pairs={{0,2},{1,3},{2,0},{3,1},{4,6},{5,7},{6,4},{7,5},{8,10},{9,11},{10,... | collective-permute-start | bytes 36872 | tf_op jit(solution)/shard_map/ppermute | solution.py:367
  29.7 3.3 %collective-permute-start.2 = (f32[24,128]{1,0:T(8,128)}, f32[24,128]{1,0:T(8,128)S(1)}, u32[]{:S(2)}, u32[]{:S(2)}) collective-permute-start(f32[24,128]{1,0:T(8,128)} %get-tuple-element.23), channel_id=1, source_target_pairs={{0,3},{1,2},{2,1},{3,0},{4,7},{5,6},{6,5},{7,4},{8,11},{9,10},{10,... | collective-permute-start | bytes 36872 | tf_op jit(solution)/shard_map/ppermute | solution.py:367
  33.7 2.7 %collective-permute-start.3 = (f32[24,128]{1,0:T(8,128)S(1)}, f32[24,128]{1,0:T(8,128)S(1)}, u32[]{:S(2)}, u32[]{:S(2)}) collective-permute-start(f32[24,128]{1,0:T(8,128)S(1)} %add_add_fusion.1), channel_id=1, source_target_pairs={{0,4},{1,5},{2,6},{3,7},{4,0},{5,1},{6,2},{7,3},{8,12},{9,13},{10,... | collective-permute-start | bytes 36872 | tf_op jit(solution)/shard_map/ppermute | solution.py:367
  35.0 3.4 %collective-permute-start.4 = (f32[24,128]{1,0:T(8,128)S(1)}, f32[24,128]{1,0:T(8,128)S(1)}, u32[]{:S(2)}, u32[]{:S(2)}) collective-permute-start(f32[24,128]{1,0:T(8,128)S(1)} %add_add_fusion.1), channel_id=1, source_target_pairs={{0,8},{1,9},{2,10},{3,11},{4,12},{5,13},{6,14},{7,15},{8,0},{9,1},... | collective-permute-start | bytes 36872 | tf_op jit(solution)/shard_map/ppermute | solution.py:367
  35.0 3.4 %collective-permute-start.5 = (f32[24,128]{1,0:T(8,128)S(1)}, f32[24,128]{1,0:T(8,128)S(1)}, u32[]{:S(2)}, u32[]{:S(2)}) collective-permute-start(f32[24,128]{1,0:T(8,128)S(1)} %add_add_fusion.1), channel_id=1, source_target_pairs={{0,12},{1,13},{2,14},{3,15},{4,8},{5,9},{6,10},{7,11},{8,4},{9,5},... | collective-permute-start | bytes 36872 | tf_op jit(solution)/shard_map/ppermute | solution.py:367
  39.0 12.4 %copy-start = (s32[20480]{0:T(1024)S(1)}, s32[20480]{0:T(1024)}, u32[]{:S(2)}) copy-start(s32[20480]{0:T(1024)} %param.10) | copy-start | bytes 245764
  39.0 12.4 %copy-start.1 = (s32[20480]{0:T(1024)S(1)}, s32[20480]{0:T(1024)}, u32[]{:S(2)}) copy-start(s32[20480]{0:T(1024)} %param.11) | copy-start | bytes 245764
  39.0 12.4 %copy-start.2 = (f32[20480]{0:T(1024)S(1)}, f32[20480]{0:T(1024)}, u32[]{:S(2)}) copy-start(f32[20480]{0:T(1024)} %param.13) | copy-start | bytes 245764
  39.0 12.4 %copy-start.5 = (s32[8192]{0:T(1024)S(1)}, s32[8192]{0:T(1024)}, u32[]{:S(2)}) copy-start(s32[8192]{0:T(1024)} %param.12) | copy-start | bytes 98308
  39.0 12.5 %copy-start.6 = (f32[20480]{0:T(1024)S(1)}, f32[20480]{0:T(1024)}, u32[]{:S(2)}) copy-start(f32[20480]{0:T(1024)} %param.15) | copy-start | bytes 245764
  44.9 29.5 %copy-start.7 = (f32[512,128]{1,0:T(8,128)S(1)}, f32[512,128]{1,0:T(8,128)}, u32[]{:S(2)}) copy-start(f32[512,128]{1,0:T(8,128)} %get-tuple-element.40) | copy-start | bytes 786436
  44.9 32.2 %copy-start.4 = (f32[7,8,128]{2,1,0:T(8,128)S(1)}, f32[7,8,128]{2,1,0:T(8,128)}, u32[]{:S(2)}) copy-start(f32[7,8,128]{2,1,0:T(8,128)} %get-tuple-element.22.state_ref) | copy-start | bytes 86020
  44.9 20.6 %collective-permute-start.10 = (f32[512,128]{1,0:T(8,128)}, f32[512,128]{1,0:T(8,128)S(1)}, u32[]{:S(2)}, u32[]{:S(2)}) collective-permute-start(f32[512,128]{1,0:T(8,128)} %get-tuple-element.38), channel_id=1, source_target_pairs={{0,10},{1,11},{2,8},{3,9},{4,14},{5,15},{6,12},{7,13},{8,2},{9,3},... | collective-permute-start | bytes 786440 | tf_op jit(solution)/shard_map/ppermute | solution.py:367
  48.8 17.3 %collective-permute-start.6 = (f32[512,128]{1,0:T(8,128)}, f32[512,128]{1,0:T(8,128)S(1)}, u32[]{:S(2)}, u32[]{:S(2)}) collective-permute-start(f32[512,128]{1,0:T(8,128)} %get-tuple-element.34), channel_id=1, source_target_pairs={{0,2},{1,3},{2,0},{3,1},{4,6},{5,7},{6,4},{7,5},{8,10},{9,11},{10,... | collective-permute-start | bytes 786440 | tf_op jit(solution)/shard_map/ppermute | solution.py:367
  49.4 16.7 %collective-permute-start.7 = (f32[512,128]{1,0:T(8,128)}, f32[512,128]{1,0:T(8,128)S(1)}, u32[]{:S(2)}, u32[]{:S(2)}) collective-permute-start(f32[512,128]{1,0:T(8,128)} %get-tuple-element.35), channel_id=1, source_target_pairs={{0,4},{1,5},{2,6},{3,7},{4,0},{5,1},{6,2},{7,3},{8,12},{9,13},{10,... | collective-permute-start | bytes 786440 | tf_op jit(solution)/shard_map/ppermute | solution.py:367
  49.4 20.6 %collective-permute-start.8 = (f32[512,128]{1,0:T(8,128)}, f32[512,128]{1,0:T(8,128)S(1)}, u32[]{:S(2)}, u32[]{:S(2)}) collective-permute-start(f32[512,128]{1,0:T(8,128)} %get-tuple-element.36), channel_id=1, source_target_pairs={{0,6},{1,7},{2,4},{3,5},{4,2},{5,3},{6,0},{7,1},{8,14},{9,15},{10,... | collective-permute-start | bytes 786440 | tf_op jit(solution)/shard_map/ppermute | solution.py:367
  51.5 18.5 %collective-permute-start.9 = (f32[512,128]{1,0:T(8,128)}, f32[512,128]{1,0:T(8,128)S(1)}, u32[]{:S(2)}, u32[]{:S(2)}) collective-permute-start(f32[512,128]{1,0:T(8,128)} %get-tuple-element.37), channel_id=1, source_target_pairs={{0,8},{1,9},{2,10},{3,11},{4,12},{5,13},{6,14},{7,15},{8,0},{9,1},... | collective-permute-start | bytes 786440 | tf_op jit(solution)/shard_map/ppermute | solution.py:367
  70.0 1.0 copy-start.3
  70.9 3.1 %copy-start.8 = (f32[512,128]{1,0:T(8,128)S(1)}, f32[512,128]{1,0:T(8,128)}, u32[]{:S(2)}) copy-start(f32[512,128]{1,0:T(8,128)} %get-tuple-element.39) | copy-start | bytes 786436
  71.1 6.0 %collective-permute-start.11 = (f32[3072,128]{1,0:T(8,128)S(1)}, f32[3072,128]{1,0:T(8,128)S(1)}, u32[]{:S(2)}, u32[]{:S(2)}) collective-permute-start(f32[3072,128]{1,0:T(8,128)S(1)} %join.2.rest_0_.rest_1_), channel_id=1, source_target_pairs={{0,1},{1,0},{2,3},{3,2},{4,5},{5,4},{6,7},{7,6},{8,9},{9,8},{10,11... | collective-permute-start | bytes 4718600 | tf_op jit(solution)/shard_map/ppermute | solution.py:367
  74.0 18.4 %collective-permute-start.12 = (f32[512,128]{1,0:T(8,128)S(1)}, f32[512,128]{1,0:T(8,128)S(1)}, u32[]{:S(2)}, u32[]{:S(2)}) collective-permute-start(f32[512,128]{1,0:T(8,128)S(1)} %copy-done.8), channel_id=1, source_target_pairs={{0,12},{1,13},{2,14},{3,15},{4,8},{5,9},{6,10},{7,11},{8,4},{9,5},... | collective-permute-start | bytes 786440 | tf_op jit(solution)/shard_map/ppermute | solution.py:367
  74.4 24.0 %collective-permute-start.13 = (f32[512,128]{1,0:T(8,128)S(1)}, f32[512,128]{1,0:T(8,128)S(1)}, u32[]{:S(2)}, u32[]{:S(2)}) collective-permute-start(f32[512,128]{1,0:T(8,128)S(1)} %copy-done.7), channel_id=1, source_target_pairs={{0,14},{1,15},{2,12},{3,13},{4,10},{5,11},{6,8},{7,9},{8,6},{9,7},... | collective-permute-start | bytes 786440 | tf_op jit(solution)/shard_map/ppermute | solution.py:367
  99.3 3.5 %collective-permute-start.14 = (f32[1024,128]{1,0:T(8,128)}, f32[1024,128]{1,0:T(8,128)}, u32[]{:S(2)}, u32[]{:S(2)}) collective-permute-start(f32[1024,128]{1,0:T(8,128)} %join.3.rest_3_), channel_id=1, source_target_pairs={{0,1},{1,0},{2,3},{3,2},{4,5},{5,4},{6,7},{7,6},{8,9},{9,8},{10,11... | collective-permute-start | bytes 1572872 | tf_op jit(solution)/shard_map/ppermute | solution.py:367
  112.5 1.8 %collective-permute-start.15 = (f32[1,128]{1,0:T(1,128)S(1)}, f32[1,128]{1,0:T(1,128)S(1)}, u32[]{:S(2)}, u32[]{:S(2)}) collective-permute-start(f32[1,128]{1,0:T(1,128)S(1)} %worst1.1), channel_id=1, source_target_pairs={{0,1},{1,0},{2,3},{3,2},{4,5},{5,4},{6,7},{7,6},{8,9},{9,8},{10,11... | collective-permute-start | bytes 1544 | tf_op jit(solution)/shard_map/ppermute | solution.py:367

commit v6 on v5

--- a/solution.py
+++ b/solution.py
@@ -83,7 +83,7 @@
 
 
 def ends_kernel(width, me_ref, ids_ref, from_ref, to_ref, slot_ref, sus_ref, chg_ref, base_ref, zinv_ref,
-                state_ref, pick_ref, own_base_ref, rows_ref, from_v, to_v, slot_v, sus_v, chg_v, base_v,
+                state_ref, pick_ref, rows_ref, from_v, to_v, slot_v, sus_v, chg_v, base_v,
                 zinv_v, ends_v, ends_s, rows, sem, out_sem, zinv_sem):
     total = ids_ref.shape[1]
     blocks = total // LANES
@@ -119,24 +119,18 @@
     copy = pltpu.make_async_copy(ends_v, ends_s, sem.at[0])
     copy.start()
     for t in range(width):
-        own_base_ref[t:t + 1, :] = base_v[pl.ds(me_ref[0] * width + t, 1), :]
+        state_ref[7, t:t + 1, :] = base_v[pl.ds(me_ref[0] * width + t, 1), :]
     copy.wait()
     for copy in zinv_copies:
         copy.wait()
 
-    def block(b, slot):
-        def fetch(g, carry):
-            for i in range(32):
-                o = g * 32 + i
-                head = ends_s[b, o]
-                tail = ends_s[blocks + b, o]
-                for t in range(width):
-                    rows[slot, 0, t, pl.ds(o, 1), :] = zinv_v[pl.ds(head + 8 * t, 1), :]
-                    rows[slot, 1, t, pl.ds(o, 1), :] = zinv_v[pl.ds(tail + 8 * t, 1), :]
-            return carry
-
-        lax.fori_loop(0, LANES // 32, fetch, 0)
-        pltpu.make_async_copy(rows.at[slot], rows_ref.at[b], out_sem.at[slot]).start()
+    def fetch(b, slot):
+        for o in range(LANES):
+            at = pl.ds(o * width, width)
+            rows[slot, 0, at, :] = zinv_v[pl.ds(ends_s[b, o], width, stride=8), :]
+            rows[slot, 1, at, :] = zinv_v[pl.ds(ends_s[blocks + b, o], width, stride=8), :]
+
+    def choose(b, slot):
         square = (LANES, LANES)
         at_h = jnp.broadcast_to(state_ref[4, pl.ds(b, 1), :], square).T
         at_t = jnp.broadcast_to(state_ref[5, pl.ds(b, 1), :], square).T
@@ -145,37 +139,50 @@
         for t in range(width):
             is_h = at_h == lane + float(t * LANES)
             is_t = at_t == lane + float(t * LANES)
-            hh = jnp.where(is_h, rows[slot, 0, t], hh)
-            ht = jnp.where(is_t, rows[slot, 0, t], ht)
-            tt = jnp.where(is_t, rows[slot, 1, t], tt)
+            piece = pl.ds(t, LANES, stride=width)
+            row_h, row_t = rows[slot, 0, piece, :], rows[slot, 1, piece, :]
+            hh = jnp.where(is_h, row_h, hh)
+            ht = jnp.where(is_t, row_h, ht)
+            tt = jnp.where(is_t, row_t, tt)
         for i, pick in enumerate((hh, ht, tt)):
             pick_ref[pl.ds(i * blocks + b, 1), :] = jnp.sum(pick.T, axis=0, keepdims=True)
 
+    def send(b, slot):
+        return pltpu.make_async_copy(rows.at[slot], rows_ref.at[b], out_sem.at[slot])
+
     def pair(i, carry):
         for slot in (0, 1):
+            b = 2 * i + slot
+
             @pl.when(i > 0)
             def _():
-                pltpu.make_async_copy(rows.at[slot], rows_ref.at[2 * i - 2 + slot], out_sem.at[slot]).wait()
-
-            block(2 * i + slot, slot)
+                send(b - 2, slot).wait()
+
+            fetch(b, slot)
+            choose(jnp.maximum(b - 1, 0), 1 - slot)
+            send(b, slot).start()
         return carry
 
+    rows[1] = jnp.zeros_like(rows[1])
     lax.fori_loop(0, blocks // 2, pair, 0)
+    choose(blocks - 1, 1)
     for slot in (0, 1):
-        pltpu.make_async_copy(rows.at[slot], rows_ref.at[blocks - 2 + slot], out_sem.at[slot]).wait()
-
-
-def spread_kernel(chips, me_ref, state_ref, pick_ref, base_ref, rows_ref, inj_ref, dev_ref, *rest):
-    units, (state, pick, base, inj, rows, dev, unit, in_sem, row_sem, out_sem) = rest[:chips], rest[chips:]
-    blocks, _, width = rows.shape[:3]
+        send(blocks - 2 + slot, slot).wait()
+
+
+def spread_kernel(chips, terms, me_ref, state_ref, rows_ref, *rest):
+    pick_refs, (inj_ref, dev_ref, *rest) = rest[:terms], rest[terms:]
+    units, (state, pick, inj, rows, dev, unit, in_sem, row_sem, out_sem) = rest[:chips], rest[chips:]
+    blocks, width = chips, dev.shape[2] // LANES
     me = me_ref[0]
-    small = stage([(state_ref, state), (pick_ref, pick), (base_ref, base)], in_sem)
+    small = stage([(state_ref, state)] + [(p, pick.at[i]) for i, p in enumerate(pick_refs)], in_sem)
     whole = [pltpu.make_async_copy(rows_ref.at[(me >> 1) ^ d], rows.at[d], row_sem.at[d]) for d in range(chips)]
     for copy in whole:
         copy.start()
     for copy in small:
         copy.wait()
-    inj_h, inj_t = newton(state[0], state[1], pick[:blocks], pick[blocks:2 * blocks], pick[2 * blocks:],
+    picks = sum(pick[i] for i in range(terms))
+    inj_h, inj_t = newton(state[0], state[1], picks[:blocks], picks[blocks:2 * blocks], picks[2 * blocks:],
                           state[2], state[3])
     inj[0] = inj_h
     inj[1] = inj_t
@@ -193,9 +200,10 @@
             copy.wait()
         for t in range(width):
             at = slice(t * LANES, (t + 1) * LANES)
-            value = scale_h * rows[d, 0, t] + scale_t * rows[d, 1, t]
+            piece = pl.ds(t, LANES, stride=width)
+            value = scale_h * rows[d, 0, piece, :] + scale_t * rows[d, 1, piece, :]
             dev[slot, :, at] = value
-            unit[slot, at, :] = ((base[t:t + 1, :] + value) * (1.0 / math.pi)).T
+            unit[slot, at, :] = ((state[7, t:t + 1, :] + value) * (1.0 / math.pi)).T
         goal = dev_ref.at[pl.ds(pl.multiple_of(blk * LANES, LANES), LANES)]
         pending[slot] = stage([(dev.at[slot], goal), (unit.at[slot], units[d])], out_sem.at[slot])
     for copy in pending[0] + pending[1] + outs:
@@ -334,7 +342,7 @@
     total = own * n_col
     blocks = total // LANES
     chips = n_col // 2
-    assert own * 2 == LANES and chips & (chips - 1) == 0 and chips > 2
+    assert own * 2 == LANES and cols // LANES <= blocks and chips & (chips - 1) == 0 and chips > 2
     me = lax.axis_index("col")
     where = me[None]
     tab = lambda a: a.reshape(-1, LANES)
@@ -350,13 +358,13 @@
 
     width = cols // LANES
     like = lambda a: pltpu.VMEM(a.shape, a.dtype)
-    row_shape = (2, width, LANES, LANES)
-    state, picks, own_base, rows = pl.pallas_call(
+    row_shape = (2, width * LANES, LANES)
+    state, picks, rows = pl.pallas_call(
         functools.partial(ends_kernel, width),
         name="ends",
-        out_shape=[f32(7, blocks, LANES), f32(3 * blocks, LANES), f32(width, LANES), f32(blocks, *row_shape)],
+        out_shape=[f32(8, blocks, LANES), f32(3 * blocks, LANES), f32(blocks, *row_shape)],
         in_specs=[SMEM, VMEM] + [ANY] * 7,
-        out_specs=[VMEM] * 3 + [ANY],
+        out_specs=[VMEM] * 2 + [ANY],
         scratch_shapes=[like(from2), like(to2), like(slot2), like(sus2), like(chg2), like(base2), like(flat),
                         pltpu.VMEM((2 * blocks, LANES), jnp.int32), pltpu.SMEM((2 * blocks, LANES), jnp.int32),
                         pltpu.VMEM((2,) + row_shape, jnp.float32), pltpu.SemaphoreType.DMA((6,)),
@@ -366,22 +374,25 @@
 
     swap = lambda a, m: lax.ppermute(a, "col", [(i, i ^ m) for i in range(n_col)])
     step = 1
+    terms = [picks]
     while step < n_col:
-        picks = sum([swap(picks, m * step) for m in range(1, min(4, n_col // step))], picks)
+        picks = sum(terms)
+        terms = [picks] + [swap(picks, m * step) for m in range(1, min(4, n_col // step))]
         step *= 4
 
     injections, deviation, *units = pl.pallas_call(
-        functools.partial(spread_kernel, chips),
+        functools.partial(spread_kernel, chips, len(terms)),
         name="spread",
         out_shape=[f32(2, blocks, LANES), f32(total, cols)] + [f32(cols, LANES)] * chips,
-        in_specs=[SMEM] + [ANY] * 4,
+        in_specs=[SMEM] + [ANY] * (2 + len(terms)),
         out_specs=[ANY] * (2 + chips),
-        scratch_shapes=[like(state), like(picks), like(own_base), pltpu.VMEM((2, blocks, LANES), jnp.float32),
-                        like(rows), pltpu.VMEM((2, LANES, cols), jnp.float32),
-                        pltpu.VMEM((2, cols, LANES), jnp.float32), pltpu.SemaphoreType.DMA((3,)),
-                        pltpu.SemaphoreType.DMA((chips,)), pltpu.SemaphoreType.DMA((2, 2))],
-        compiler_params=params(60),
-    )(where, state, picks, own_base, rows)
+        scratch_shapes=[like(state), pltpu.VMEM((len(terms),) + picks.shape, jnp.float32),
+                        pltpu.VMEM((2, blocks, LANES), jnp.float32), like(rows),
+                        pltpu.VMEM((2, LANES, cols), jnp.float32), pltpu.VMEM((2, cols, LANES), jnp.float32),
+                        pltpu.SemaphoreType.DMA((1 + len(terms),)), pltpu.SemaphoreType.DMA((chips,)),
+                        pltpu.SemaphoreType.DMA((2, 2))],
+        compiler_params=params(52),
+    )(where, state, rows, *terms)
 
     half = branch_from.shape[0] // LANES // 2
     f_rel, t_rel, ratio, k_rel, counts = pl.pallas_call(

time: 115 us -> 110 us (0.957)
  Pallas kernels: 55.1 us -> 51.9 us
    pallas_call x1, Pallas kernels: 15.1 us -> 12.4 us  [per_device(): pl.pallas_call(functools.partial(ends_kernel, width), name='ends', out_sh...]
  transfers between devices with their start and end apart: 16 -> 16, of which waited for: 9 -> 11; matrix products, arithmetic and copies ran while one was open for 1% -> 1% of each run, Pallas kernels for 20% -> 21%
where the time goes in v6:
time: 110 us
  Pallas kernels  51.9 us (47%)
  waiting for transfers between devices  24.4 us (22%)
  starting transfers between devices  20.2 us (18%)
  blocking collectives  9.25 us (8%)
  local copies, waits for them, and re-layouts  2.3 us (2%)
  other arithmetic  1.3 us (1%)
    ppermute x16, waiting for transfers between devices, per_device(): lax.ppermute(a, 'col', [(i, i ^ m) for i in range(n_col)])  24.4 us
    ppermute x16, starting transfers between devices, per_device(): lax.ppermute(a, 'col', [(i, i ^ m) for i in range(n_col)])  20.2 us
    pallas_call x2, Pallas kernels, worst_of(): pl.pallas_call(functools.partial(worst_kernel, level), name=f'worst{level...  19.2 us
    pallas_call x1, Pallas kernels, per_device(): pl.pallas_call(functools.partial(prep_kernel, cols, chips), name='prep',...  13.9 us
    pallas_call x1, Pallas kernels, per_device(): pl.pallas_call(functools.partial(ends_kernel, width), name='ends', out_sh...  12.4 us
    psum x1, blocking collectives, per_device(): ids = lax.psum(ids[None], 'col')  9.25 us
    pallas_call x1, Pallas kernels, per_device(): pl.pallas_call(functools.partial(spread_kernel, chips, len(terms)), name=...  5.33 us
  transfers between devices with their start and end apart: 16, of which 11 were waited for; matrix products, arithmetic and copies ran while one was open for 1% of the time, Pallas kernels for 21%

profile of v6, /device:TPU:9, one launch (start us, length us, event | category | flops | bytes accessed | tf_op | source)
XLA Modules:
  0.0 110.1 jit_solution(2240846801269640434)
XLA Ops:
  0.6 0.9 dynamic_update_slice.4
  1.5 9.2 %psum.7.ids_ref = s32[1,1024]{1,0:T(1,128)} all-reduce(s32[1,1024]{1,0:T(1,128)S(1)} %dynamic_update_slice.4), channel_id=1, replica_groups=mesh['parts'=2,'col'=16] {'col'}, use_global_device_ids=true, to_apply=%region_0.0 | all-reduce | flops 1024 | bytes 8192 | tf_op jit(solution)/shard_map/psum | solution.py:357
  10.8 12.4 %ends.1 = (f32[8,8,128]{2,1,0:T(8,128)}, f32[24,128]{1,0:T(8,128)}, f32[8,2,512,128]{3,2,1,0:T(8,128)}) custom-call(s32[1]{0:T(128)} %bitcast.me_ref, s32[1,1024]{1,0:T(1,128)} %psum.7.ids_ref, s32[160,128]{1,0:T(8,128)} %bitcast.17, s32[160,128]{1,0:T(8,128)} %bitcast.19, s32[64,128]{1,0:T(8,128)} %bitcast.23, f32[160,128]{1,0:T(8,128)} %bitcast.21, ...), custom_call_target="tpu_custom_call" | custom-call | tf_op jit(solution)/shard_map/ends/pallas_call | solution.py:362
  23.2 3.2 %collective-permute-start = (f32[24,128]{1,0:T(8,128)}, f32[24,128]{1,0:T(8,128)S(1)}, u32[]{:S(2)}, u32[]{:S(2)}) collective-permute-start(f32[24,128]{1,0:T(8,128)} %get-tuple-element.23), channel_id=1, source_target_pairs={{0,1},{1,0},{2,3},{3,2},{4,5},{5,4},{6,7},{7,6},{8,9},{9,8},{10,11... | collective-permute-start | bytes 36872 | tf_op jit(solution)/shard_map/ppermute | solution.py:375
  26.3 0.6 collective-permute-start.1
  26.9 1.1 %collective-permute-start.2 = (f32[24,128]{1,0:T(8,128)}, f32[24,128]{1,0:T(8,128)S(1)}, u32[]{:S(2)}, u32[]{:S(2)}) collective-permute-start(f32[24,128]{1,0:T(8,128)} %get-tuple-element.23), channel_id=1, source_target_pairs={{0,3},{1,2},{2,1},{3,0},{4,7},{5,6},{6,5},{7,4},{8,11},{9,10},{10,... | collective-permute-start | bytes 36872 | tf_op jit(solution)/shard_map/ppermute | solution.py:375
  28.1 0.0 collective-permute-done
  28.1 1.1 collective-permute-done.1
  29.1 1.1 %collective-permute-done.2 = f32[24,128]{1,0:T(8,128)S(1)} collective-permute-done((f32[24,128]{1,0:T(8,128)}, f32[24,128]{1,0:T(8,128)S(1)}, u32[]{:S(2)}, u32[]{:S(2)}) %collective-permute-start.2) | collective-permute-done | bytes 12320 | tf_op jit(solution)/shard_map/ppermute | solution.py:375
  30.3 0.7 add_add_fusion.rest_0_
  31.0 1.3 %collective-permute-start.3 = (f32[24,128]{1,0:T(8,128)S(1)}, f32[24,128]{1,0:T(8,128)S(1)}, u32[]{:S(2)}, u32[]{:S(2)}) collective-permute-start(f32[24,128]{1,0:T(8,128)S(1)} %add_add_fusion.rest_0_), channel_id=1, source_target_pairs={{0,4},{1,5},{2,6},{3,7},{4,0},{5,1},{6,2},{7,3},{8,12},{9,13},{10,... | collective-permute-start | bytes 36872 | tf_op jit(solution)/shard_map/ppermute | solution.py:375
  32.3 0.1 collective-permute-start.4
  32.3 1.3 %collective-permute-start.5 = (f32[24,128]{1,0:T(8,128)S(1)}, f32[24,128]{1,0:T(8,128)S(1)}, u32[]{:S(2)}, u32[]{:S(2)}) collective-permute-start(f32[24,128]{1,0:T(8,128)S(1)} %add_add_fusion.rest_0_), channel_id=1, source_target_pairs={{0,12},{1,13},{2,14},{3,15},{4,8},{5,9},{6,10},{7,11},{8,4},{9,5},... | collective-permute-start | bytes 36872 | tf_op jit(solution)/shard_map/ppermute | solution.py:375
  33.6 0.0 collective-permute-done.3.rest_1_
  33.6 2.1 %collective-permute-done.4.rest_2_ = f32[24,128]{1,0:T(8,128)S(1)} collective-permute-done((f32[24,128]{1,0:T(8,128)S(1)}, f32[24,128]{1,0:T(8,128)S(1)}, u32[]{:S(2)}, u32[]{:S(2)}) %collective-permute-start.4) | collective-permute-done | bytes 12320 | tf_op jit(solution)/shard_map/ppermute | solution.py:375
  35.7 0.0 collective-permute-done.5.rest_3_
  35.7 0.8 copy-done.3
  36.5 0.0 copy-start.6
  36.5 5.3 %spread.1 = (f32[2,8,128]{2,1,0:T(8,128)S(1)}, f32[1024,512]{1,0:T(8,128)}, f32[512,128]{1,0:T(8,128)S(1)}, f32[512,128]{1,0:T(8,128)S(1)}, f32[512,128]{1,0:T(8...) custom-call(s32[1]{0:T(128)} %bitcast.me_ref, ...), custom_call_target="tpu_custom_call" | custom-call | tf_op jit(solution)/shard_map/spread/pallas_call | solution.py:383
  41.9 3.9 %collective-permute-start.10 = (f32[512,128]{1,0:T(8,128)S(1)}, f32[512,128]{1,0:T(8,128)S(1)}, u32[]{:S(2)}, u32[]{:S(2)}) collective-permute-start(f32[512,128]{1,0:T(8,128)S(1)} %get-tuple-element.36), channel_id=1, source_target_pairs={{0,10},{1,11},{2,8},{3,9},{4,14},{5,15},{6,12},{7,13},{8,2},{9,3},... | collective-permute-start | bytes 786440 | tf_op jit(solution)/shard_map/ppermute | solution.py:375
  45.8 0.6 collective-permute-start.6
  46.4 0.0 collective-permute-start.7
  46.4 2.1 %collective-permute-start.8 = (f32[512,128]{1,0:T(8,128)S(1)}, f32[512,128]{1,0:T(8,128)S(1)}, u32[]{:S(2)}, u32[]{:S(2)}) collective-permute-start(f32[512,128]{1,0:T(8,128)S(1)} %get-tuple-element.34), channel_id=1, source_target_pairs={{0,6},{1,7},{2,4},{3,5},{4,2},{5,3},{6,0},{7,1},{8,14},{9,15},{10,... | collective-permute-start | bytes 786440 | tf_op jit(solution)/shard_map/ppermute | solution.py:375
  48.4 0.0 collective-permute-start.9
  48.5 13.9 %prep.1 = (s32[80,128]{1,0:T(8,128)S(1)}, s32[80,128]{1,0:T(8,128)S(1)}, f32[80,128]{1,0:T(8,128)S(1)}, f32[80,128]{1,0:T(8,128)S(1)}, s32[1,128]{1,0:T(1,128)S(1)}) custom-call(s32[1]{0:T(128)} %bitcast.me_ref, s32[160,128]{1,0:T(8,128)S(1)} %bitcast.18, s32[160,128]{1,0:T(8,128)S(1)} %bitcast.20, s32[64,128]{1,0:T(8,128)S(1)} %bitcast.24, ...), custom_call_target="tpu_custom_call" | custom-call | tf_op jit(solution)/shard_map/prep/pallas_call | solution.py:398
  62.4 0.0 collective-permute-done.10.refs_5_
  62.4 0.5 collective-permute-done.6.refs_1_
  62.9 0.0 collective-permute-done.7.refs_2_
  62.9 3.7 %collective-permute-done.8.refs_3_ = f32[512,128]{1,0:T(8,128)S(1)} collective-permute-done((f32[512,128]{1,0:T(8,128)S(1)}, f32[512,128]{1,0:T(8,128)S(1)}, u32[]{:S(2)}, u32[]{:S(2)}) %collective-permute-start.8) | collective-permute-done | bytes 262176 | tf_op jit(solution)/shard_map/ppermute | solution.py:375
  66.6 0.1 collective-permute-done.9.refs_4_
  66.7 0.2 join.2.rest_0_.rest_1_
  66.9 2.9 %collective-permute-start.11 = (f32[3072,128]{1,0:T(8,128)S(1)}, f32[3072,128]{1,0:T(8,128)S(1)}, u32[]{:S(2)}, u32[]{:S(2)}) collective-permute-start(f32[3072,128]{1,0:T(8,128)S(1)} %join.2.rest_0_.rest_1_), channel_id=1, source_target_pairs={{0,1},{1,0},{2,3},{3,2},{4,5},{5,4},{6,7},{7,6},{8,9},{9,8},{10,11... | collective-permute-start | bytes 4718600 | tf_op jit(solution)/shard_map/ppermute | solution.py:375
  69.7 0.3 collective-permute-start.12
  70.1 0.0 copy-done.7
  70.1 1.6 %collective-permute-start.13 = (f32[512,128]{1,0:T(8,128)S(1)}, f32[512,128]{1,0:T(8,128)S(1)}, u32[]{:S(2)}, u32[]{:S(2)}) collective-permute-start(f32[512,128]{1,0:T(8,128)S(1)} %copy-done.7), channel_id=1, source_target_pairs={{0,14},{1,15},{2,12},{3,13},{4,10},{5,11},{6,8},{7,9},{8,6},{9,7},... | collective-permute-start | bytes 786440 | tf_op jit(solution)/shard_map/ppermute | solution.py:375
  71.7 1.1 collective-permute-done.11.rest_1_.rest_2_
  72.8 9.5 %worst0.1._.rest_0_ = f32[8,128]{1,0:T(8,128)S(1)} custom-call(s32[1]{0:T(128)} %bitcast.me_ref, s32[80,128]{1,0:T(8,128)S(1)} %get-tuple-element.26.f_ref, s32[80,128]{1,0:T(8,128)S(1)} %get-tuple-element.27.t_ref, s32[1,128]{1,0:T(1,128)S(1)} %get-tuple-element.28._.cnt_ref, f32[80,128]{1,0:T(8,128)S(1)} %get-tuple-element.29.ratio_ref, ...), custom_call_target="tpu_custom_call" | custom-call | tf_op jit(solution)/shard_map/worst0/pallas_call | solution.py:423
  82.3 6.6 %collective-permute-done.12.refs_0_ = f32[512,128]{1,0:T(8,128)S(1)} collective-permute-done((f32[512,128]{1,0:T(8,128)S(1)}, f32[512,128]{1,0:T(8,128)S(1)}, u32[]{:S(2)}, u32[]{:S(2)}) %collective-permute-start.12) | collective-permute-done | bytes 262176 | tf_op jit(solution)/shard_map/ppermute | solution.py:375
  88.8 6.1 %collective-permute-done.13.refs_1_ = f32[512,128]{1,0:T(8,128)S(1)} collective-permute-done((f32[512,128]{1,0:T(8,128)S(1)}, f32[512,128]{1,0:T(8,128)S(1)}, u32[]{:S(2)}, u32[]{:S(2)}) %collective-permute-start.13) | collective-permute-done | bytes 262176 | tf_op jit(solution)/shard_map/ppermute | solution.py:375
  94.9 0.9 join.3.rest_3_
  95.8 0.9 collective-permute-start.14
  96.7 1.9 %collective-permute-done.14.rest_4_ = f32[1024,128]{1,0:T(8,128)} collective-permute-done((f32[1024,128]{1,0:T(8,128)}, f32[1024,128]{1,0:T(8,128)}, u32[]{:S(2)}, u32[]{:S(2)}) %collective-permute-start.14) | collective-permute-done | bytes 524320 | tf_op jit(solution)/shard_map/ppermute | solution.py:375
  98.6 0.0 copy-done.4
  98.6 9.7 %worst1.1 = f32[1,128]{1,0:T(1,128)S(1)} custom-call(s32[1]{0:T(128)} %bitcast.me_ref, s32[80,128]{1,0:T(8,128)S(1)} %get-tuple-element.26.f_ref, s32[80,128]{1,0:T(8,128)S(1)} %get-tuple-element.27.t_ref, s32[1,128]{1,0:T(1,128)S(1)} %get-tuple-element.28._.cnt_ref, f32[80,128]{1,0:T(8,128)S(1)} %get-tuple-element.29.ratio_ref, ...), custom_call_target="tpu_custom_call" | custom-call | tf_op jit(solution)/shard_map/worst1/pallas_call | solution.py:423
  108.3 0.4 collective-permute-start.15
  108.7 0.6 constant_dynamic-slice_fusion.2
  109.4 0.2 collective-permute-done.15
  109.6 0.6 fusion.1
  (13 shorter events, 0.0 us)
Async XLA Ops:
  23.2 4.9 %collective-permute-start = (f32[24,128]{1,0:T(8,128)}, f32[24,128]{1,0:T(8,128)S(1)}, u32[]{:S(2)}, u32[]{:S(2)}) collective-permute-start(f32[24,128]{1,0:T(8,128)} %get-tuple-element.23), channel_id=1, source_target_pairs={{0,1},{1,0},{2,3},{3,2},{4,5},{5,4},{6,7},{7,6},{8,9},{9,8},{10,11... | collective-permute-start | bytes 36872 | tf_op jit(solution)/shard_map/ppermute | solution.py:375
  26.3 2.8 %collective-permute-start.1 = (f32[24,128]{1,0:T(8,128)}, f32[24,128]{1,0:T(8,128)S(1)}, u32[]{:S(2)}, u32[]{:S(2)}) collective-permute-start(f32[24,128]{1,0:T(8,128)} %get-tuple-element.23), channel_id=1, source_target_pairs={{0,2},{1,3},{2,0},{3,1},{4,6},{5,7},{6,4},{7,5},{8,10},{9,11},{10,... | collective-permute-start | bytes 36872 | tf_op jit(solution)/shard_map/ppermute | solution.py:375
  26.9 3.3 %collective-permute-start.2 = (f32[24,128]{1,0:T(8,128)}, f32[24,128]{1,0:T(8,128)S(1)}, u32[]{:S(2)}, u32[]{:S(2)}) collective-permute-start(f32[24,128]{1,0:T(8,128)} %get-tuple-element.23), channel_id=1, source_target_pairs={{0,3},{1,2},{2,1},{3,0},{4,7},{5,6},{6,5},{7,4},{8,11},{9,10},{10,... | collective-permute-start | bytes 36872 | tf_op jit(solution)/shard_map/ppermute | solution.py:375
  31.0 2.7 %collective-permute-start.3 = (f32[24,128]{1,0:T(8,128)S(1)}, f32[24,128]{1,0:T(8,128)S(1)}, u32[]{:S(2)}, u32[]{:S(2)}) collective-permute-start(f32[24,128]{1,0:T(8,128)S(1)} %add_add_fusion.rest_0_), channel_id=1, source_target_pairs={{0,4},{1,5},{2,6},{3,7},{4,0},{5,1},{6,2},{7,3},{8,12},{9,13},{10,... | collective-permute-start | bytes 36872 | tf_op jit(solution)/shard_map/ppermute | solution.py:375
  32.3 3.4 %collective-permute-start.4 = (f32[24,128]{1,0:T(8,128)S(1)}, f32[24,128]{1,0:T(8,128)S(1)}, u32[]{:S(2)}, u32[]{:S(2)}) collective-permute-start(f32[24,128]{1,0:T(8,128)S(1)} %add_add_fusion.rest_0_), channel_id=1, source_target_pairs={{0,8},{1,9},{2,10},{3,11},{4,12},{5,13},{6,14},{7,15},{8,0},{9,1},... | collective-permute-start | bytes 36872 | tf_op jit(solution)/shard_map/ppermute | solution.py:375
  32.3 3.4 %collective-permute-start.5 = (f32[24,128]{1,0:T(8,128)S(1)}, f32[24,128]{1,0:T(8,128)S(1)}, u32[]{:S(2)}, u32[]{:S(2)}) collective-permute-start(f32[24,128]{1,0:T(8,128)S(1)} %add_add_fusion.rest_0_), channel_id=1, source_target_pairs={{0,12},{1,13},{2,14},{3,15},{4,8},{5,9},{6,10},{7,11},{8,4},{9,5},... | collective-permute-start | bytes 36872 | tf_op jit(solution)/shard_map/ppermute | solution.py:375
  35.7 0.8 copy-start.3
  36.5 12.0 %copy-start = (s32[20480]{0:T(1024)S(1)}, s32[20480]{0:T(1024)}, u32[]{:S(2)}) copy-start(s32[20480]{0:T(1024)} %param.10) | copy-start | bytes 245764
  36.5 12.0 %copy-start.1 = (s32[20480]{0:T(1024)S(1)}, s32[20480]{0:T(1024)}, u32[]{:S(2)}) copy-start(s32[20480]{0:T(1024)} %param.11) | copy-start | bytes 245764
  36.5 12.0 %copy-start.2 = (f32[20480]{0:T(1024)S(1)}, f32[20480]{0:T(1024)}, u32[]{:S(2)}) copy-start(f32[20480]{0:T(1024)} %param.13) | copy-start | bytes 245764
  36.5 12.0 %copy-start.5 = (s32[8192]{0:T(1024)S(1)}, s32[8192]{0:T(1024)}, u32[]{:S(2)}) copy-start(s32[8192]{0:T(1024)} %param.12) | copy-start | bytes 98308
  36.5 12.0 %copy-start.6 = (f32[20480]{0:T(1024)S(1)}, f32[20480]{0:T(1024)}, u32[]{:S(2)}) copy-start(f32[20480]{0:T(1024)} %param.15) | copy-start | bytes 245764
  41.8 28.2 %copy-start.7 = (f32[512,128]{1,0:T(8,128)S(1)}, f32[512,128]{1,0:T(8,128)}, u32[]{:S(2)}) copy-start(f32[512,128]{1,0:T(8,128)} %get-tuple-element.38) | copy-start | bytes 786436
  41.9 20.6 %collective-permute-start.10 = (f32[512,128]{1,0:T(8,128)S(1)}, f32[512,128]{1,0:T(8,128)S(1)}, u32[]{:S(2)}, u32[]{:S(2)}) collective-permute-start(f32[512,128]{1,0:T(8,128)S(1)} %get-tuple-element.36), channel_id=1, source_target_pairs={{0,10},{1,11},{2,8},{3,9},{4,14},{5,15},{6,12},{7,13},{8,2},{9,3},... | collective-permute-start | bytes 786440 | tf_op jit(solution)/shard_map/ppermute | solution.py:375
  45.8 17.1 %collective-permute-start.6 = (f32[512,128]{1,0:T(8,128)S(1)}, f32[512,128]{1,0:T(8,128)S(1)}, u32[]{:S(2)}, u32[]{:S(2)}) collective-permute-start(f32[512,128]{1,0:T(8,128)S(1)} %get-tuple-element.32), channel_id=1, source_target_pairs={{0,2},{1,3},{2,0},{3,1},{4,6},{5,7},{6,4},{7,5},{8,10},{9,11},{10,... | collective-permute-start | bytes 786440 | tf_op jit(solution)/shard_map/ppermute | solution.py:375
  46.4 16.5 %collective-permute-start.7 = (f32[512,128]{1,0:T(8,128)S(1)}, f32[512,128]{1,0:T(8,128)S(1)}, u32[]{:S(2)}, u32[]{:S(2)}) collective-permute-start(f32[512,128]{1,0:T(8,128)S(1)} %get-tuple-element.33), channel_id=1, source_target_pairs={{0,4},{1,5},{2,6},{3,7},{4,0},{5,1},{6,2},{7,3},{8,12},{9,13},{10,... | collective-permute-start | bytes 786440 | tf_op jit(solution)/shard_map/ppermute | solution.py:375
  46.4 20.2 %collective-permute-start.8 = (f32[512,128]{1,0:T(8,128)S(1)}, f32[512,128]{1,0:T(8,128)S(1)}, u32[]{:S(2)}, u32[]{:S(2)}) collective-permute-start(f32[512,128]{1,0:T(8,128)S(1)} %get-tuple-element.34), channel_id=1, source_target_pairs={{0,6},{1,7},{2,4},{3,5},{4,2},{5,3},{6,0},{7,1},{8,14},{9,15},{10,... | collective-permute-start | bytes 786440 | tf_op jit(solution)/shard_map/ppermute | solution.py:375
  48.4 18.3 %collective-permute-start.9 = (f32[512,128]{1,0:T(8,128)S(1)}, f32[512,128]{1,0:T(8,128)S(1)}, u32[]{:S(2)}, u32[]{:S(2)}) collective-permute-start(f32[512,128]{1,0:T(8,128)S(1)} %get-tuple-element.35), channel_id=1, source_target_pairs={{0,8},{1,9},{2,10},{3,11},{4,12},{5,13},{6,14},{7,15},{8,0},{9,1},... | collective-permute-start | bytes 786440 | tf_op jit(solution)/shard_map/ppermute | solution.py:375
  66.9 5.9 %collective-permute-start.11 = (f32[3072,128]{1,0:T(8,128)S(1)}, f32[3072,128]{1,0:T(8,128)S(1)}, u32[]{:S(2)}, u32[]{:S(2)}) collective-permute-start(f32[3072,128]{1,0:T(8,128)S(1)} %join.2.rest_0_.rest_1_), channel_id=1, source_target_pairs={{0,1},{1,0},{2,3},{3,2},{4,5},{5,4},{6,7},{7,6},{8,9},{9,8},{10,11... | collective-permute-start | bytes 4718600 | tf_op jit(solution)/shard_map/ppermute | solution.py:375
  69.7 19.1 %collective-permute-start.12 = (f32[512,128]{1,0:T(8,128)S(1)}, f32[512,128]{1,0:T(8,128)S(1)}, u32[]{:S(2)}, u32[]{:S(2)}) collective-permute-start(f32[512,128]{1,0:T(8,128)S(1)} %get-tuple-element.37), channel_id=1, source_target_pairs={{0,12},{1,13},{2,14},{3,15},{4,8},{5,9},{6,10},{7,11},{8,4},{9,5},... | collective-permute-start | bytes 786440 | tf_op jit(solution)/shard_map/ppermute | solution.py:375
  70.1 24.9 %collective-permute-start.13 = (f32[512,128]{1,0:T(8,128)S(1)}, f32[512,128]{1,0:T(8,128)S(1)}, u32[]{:S(2)}, u32[]{:S(2)}) collective-permute-start(f32[512,128]{1,0:T(8,128)S(1)} %copy-done.7), channel_id=1, source_target_pairs={{0,14},{1,15},{2,12},{3,13},{4,10},{5,11},{6,8},{7,9},{8,6},{9,7},... | collective-permute-start | bytes 786440 | tf_op jit(solution)/shard_map/ppermute | solution.py:375
  72.8 25.8 %copy-start.4 = (f32[8,8,128]{2,1,0:T(8,128)S(1)}, f32[8,8,128]{2,1,0:T(8,128)}, u32[]{:S(2)}) copy-start(f32[8,8,128]{2,1,0:T(8,128)} %get-tuple-element.21.state_ref) | copy-start | bytes 98308
  95.8 2.8 %collective-permute-start.14 = (f32[1024,128]{1,0:T(8,128)}, f32[1024,128]{1,0:T(8,128)}, u32[]{:S(2)}, u32[]{:S(2)}) collective-permute-start(f32[1024,128]{1,0:T(8,128)} %join.3.rest_3_), channel_id=1, source_target_pairs={{0,1},{1,0},{2,3},{3,2},{4,5},{5,4},{6,7},{7,6},{8,9},{9,8},{10,11... | collective-permute-start | bytes 1572872 | tf_op jit(solution)/shard_map/ppermute | solution.py:375
  108.3 1.3 %collective-permute-start.15 = (f32[1,128]{1,0:T(1,128)S(1)}, f32[1,128]{1,0:T(1,128)S(1)}, u32[]{:S(2)}, u32[]{:S(2)}) collective-permute-start(f32[1,128]{1,0:T(1,128)S(1)} %worst1.1), channel_id=1, source_target_pairs={{0,1},{1,0},{2,3},{3,2},{4,5},{5,4},{6,7},{7,6},{8,9},{9,8},{10,11... | collective-permute-start | bytes 1544 | tf_op jit(solution)/shard_map/ppermute | solution.py:375

commit v7 on v6

--- a/solution.py
+++ b/solution.py
@@ -380,6 +380,7 @@
         terms = [picks] + [swap(picks, m * step) for m in range(1, min(4, n_col // step))]
         step *= 4
 
+    nearby = state + jnp.minimum(me, 0).astype(jnp.float32)
     injections, deviation, *units = pl.pallas_call(
         functools.partial(spread_kernel, chips, len(terms)),
         name="spread",
@@ -392,7 +393,7 @@
                         pltpu.SemaphoreType.DMA((1 + len(terms),)), pltpu.SemaphoreType.DMA((chips,)),
                         pltpu.SemaphoreType.DMA((2, 2))],
         compiler_params=params(52),
-    )(where, state, rows, *terms)
+    )(where, nearby, rows, *terms)
 
     half = branch_from.shape[0] // LANES // 2
     f_rel, t_rel, ratio, k_rel, counts = pl.pallas_call(

time: 110 us -> 110 us (level)
  no operation moved by 1% of the time
where the time goes in v7:
time: 110 us; the launch traced here: 109 us
  Pallas kernels  51.9 us (47%)
  waiting for transfers between devices  23.6 us (21%)
  starting transfers between devices  20.2 us (18%)
  blocking collectives  9.25 us (8%)
  other arithmetic  2.06 us (2%)
  local copies, waits for them, and re-layouts  1.54 us (1%)
    ppermute x16, waiting for transfers between devices, per_device(): lax.ppermute(a, 'col', [(i, i ^ m) for i in range(n_col)])  23.6 us
    ppermute x16, starting transfers between devices, per_device(): lax.ppermute(a, 'col', [(i, i ^ m) for i in range(n_col)])  20.2 us
    pallas_call x2, Pallas kernels, worst_of(): pl.pallas_call(functools.partial(worst_kernel, level), name=f'worst{level...  19.2 us
    pallas_call x1, Pallas kernels, per_device(): pl.pallas_call(functools.partial(prep_kernel, cols, chips), name='prep',...  13.9 us
    pallas_call x1, Pallas kernels, per_device(): pl.pallas_call(functools.partial(ends_kernel, width), name='ends', out_sh...  12.4 us
    psum x1, blocking collectives, per_device(): ids = lax.psum(ids[None], 'col')  9.25 us
    pallas_call x1, Pallas kernels, per_device(): pl.pallas_call(functools.partial(spread_kernel, chips, len(terms)), name=...  5.32 us
  transfers between devices with their start and end apart: 16, of which 11 were waited for; matrix products, arithmetic and copies ran while one was open for 1% of the time, Pallas kernels for 21%

profile of v7, /device:TPU:9, one launch (start us, length us, event | category | flops | bytes accessed | tf_op | source)
XLA Modules:
  0.0 109.4 jit_solution(8074640995823055232)
XLA Ops:
  0.6 0.9 dynamic_update_slice.4
  1.5 9.2 %psum.7.ids_ref = s32[1,1024]{1,0:T(1,128)} all-reduce(s32[1,1024]{1,0:T(1,128)S(1)} %dynamic_update_slice.4), channel_id=1, replica_groups=mesh['parts'=2,'col'=16] {'col'}, use_global_device_ids=true, to_apply=%region_0.0 | all-reduce | flops 1024 | bytes 8192 | tf_op jit(solution)/shard_map/psum | solution.py:357
  10.8 12.4 %ends.1 = (f32[8,8,128]{2,1,0:T(8,128)}, f32[24,128]{1,0:T(8,128)}, f32[8,2,512,128]{3,2,1,0:T(8,128)}) custom-call(s32[1]{0:T(128)} %bitcast.me_ref, s32[1,1024]{1,0:T(1,128)} %psum.7.ids_ref, s32[160,128]{1,0:T(8,128)} %bitcast.17, s32[160,128]{1,0:T(8,128)} %bitcast.19, s32[64,128]{1,0:T(8,128)} %bitcast.23, f32[160,128]{1,0:T(8,128)} %bitcast.21, ...), custom_call_target="tpu_custom_call" | custom-call | tf_op jit(solution)/shard_map/ends/pallas_call | solution.py:362
  23.2 3.2 %collective-permute-start = (f32[24,128]{1,0:T(8,128)}, f32[24,128]{1,0:T(8,128)S(1)}, u32[]{:S(2)}, u32[]{:S(2)}) collective-permute-start(f32[24,128]{1,0:T(8,128)} %get-tuple-element.23), channel_id=1, source_target_pairs={{0,1},{1,0},{2,3},{3,2},{4,5},{5,4},{6,7},{7,6},{8,9},{9,8},{10,11... | collective-permute-start | bytes 36872 | tf_op jit(solution)/shard_map/ppermute | solution.py:375
  26.3 0.6 collective-permute-start.1
  26.9 1.1 %collective-permute-start.2 = (f32[24,128]{1,0:T(8,128)}, f32[24,128]{1,0:T(8,128)S(1)}, u32[]{:S(2)}, u32[]{:S(2)}) collective-permute-start(f32[24,128]{1,0:T(8,128)} %get-tuple-element.23), channel_id=1, source_target_pairs={{0,3},{1,2},{2,1},{3,0},{4,7},{5,6},{6,5},{7,4},{8,11},{9,10},{10,... | collective-permute-start | bytes 36872 | tf_op jit(solution)/shard_map/ppermute | solution.py:375
  28.1 0.0 collective-permute-done
  28.1 1.1 collective-permute-done.1
  29.1 1.1 %collective-permute-done.2 = f32[24,128]{1,0:T(8,128)S(1)} collective-permute-done((f32[24,128]{1,0:T(8,128)}, f32[24,128]{1,0:T(8,128)S(1)}, u32[]{:S(2)}, u32[]{:S(2)}) %collective-permute-start.2) | collective-permute-done | bytes 12320 | tf_op jit(solution)/shard_map/ppermute | solution.py:375
  30.3 0.7 add_add_fusion.rest_0_
  31.0 1.3 %collective-permute-start.3 = (f32[24,128]{1,0:T(8,128)S(1)}, f32[24,128]{1,0:T(8,128)S(1)}, u32[]{:S(2)}, u32[]{:S(2)}) collective-permute-start(f32[24,128]{1,0:T(8,128)S(1)} %add_add_fusion.rest_0_), channel_id=1, source_target_pairs={{0,4},{1,5},{2,6},{3,7},{4,0},{5,1},{6,2},{7,3},{8,12},{9,13},{10,... | collective-permute-start | bytes 36872 | tf_op jit(solution)/shard_map/ppermute | solution.py:375
  32.3 0.1 collective-permute-start.4
  32.3 1.3 %collective-permute-start.5 = (f32[24,128]{1,0:T(8,128)S(1)}, f32[24,128]{1,0:T(8,128)S(1)}, u32[]{:S(2)}, u32[]{:S(2)}) collective-permute-start(f32[24,128]{1,0:T(8,128)S(1)} %add_add_fusion.rest_0_), channel_id=1, source_target_pairs={{0,12},{1,13},{2,14},{3,15},{4,8},{5,9},{6,10},{7,11},{8,4},{9,5},... | collective-permute-start | bytes 36872 | tf_op jit(solution)/shard_map/ppermute | solution.py:375
  33.6 0.8 broadcast_add_fusion.state_ref
  34.4 0.0 collective-permute-done.3.rest_1_
  34.4 1.3 %collective-permute-done.4.rest_2_ = f32[24,128]{1,0:T(8,128)S(1)} collective-permute-done((f32[24,128]{1,0:T(8,128)S(1)}, f32[24,128]{1,0:T(8,128)S(1)}, u32[]{:S(2)}, u32[]{:S(2)}) %collective-permute-start.4) | collective-permute-done | bytes 12320 | tf_op jit(solution)/shard_map/ppermute | solution.py:375
  35.7 0.0 collective-permute-done.5.rest_3_
  35.7 0.0 copy-start.4
  35.7 0.0 copy-start.5
  35.7 5.3 %spread.1 = (f32[2,8,128]{2,1,0:T(8,128)S(1)}, f32[1024,512]{1,0:T(8,128)}, f32[512,128]{1,0:T(8,128)S(1)}, f32[512,128]{1,0:T(8,128)S(1)}, f32[512,128]{1,0:T(8...) custom-call(s32[1]{0:T(128)} %bitcast.me_ref, ...), custom_call_target="tpu_custom_call" | custom-call | tf_op jit(solution)/shard_map/spread/pallas_call | solution.py:384
  41.1 0.0 copy-start.6
  41.1 3.9 %collective-permute-start.10 = (f32[512,128]{1,0:T(8,128)S(1)}, f32[512,128]{1,0:T(8,128)S(1)}, u32[]{:S(2)}, u32[]{:S(2)}) collective-permute-start(f32[512,128]{1,0:T(8,128)S(1)} %get-tuple-element.36), channel_id=1, source_target_pairs={{0,10},{1,11},{2,8},{3,9},{4,14},{5,15},{6,12},{7,13},{8,2},{9,3},... | collective-permute-start | bytes 786440 | tf_op jit(solution)/shard_map/ppermute | solution.py:375
  45.0 0.6 collective-permute-start.6
  45.6 0.0 collective-permute-start.7
  45.6 2.1 %collective-permute-start.8 = (f32[512,128]{1,0:T(8,128)S(1)}, f32[512,128]{1,0:T(8,128)S(1)}, u32[]{:S(2)}, u32[]{:S(2)}) collective-permute-start(f32[512,128]{1,0:T(8,128)S(1)} %get-tuple-element.34), channel_id=1, source_target_pairs={{0,6},{1,7},{2,4},{3,5},{4,2},{5,3},{6,0},{7,1},{8,14},{9,15},{10,... | collective-permute-start | bytes 786440 | tf_op jit(solution)/shard_map/ppermute | solution.py:375
  47.7 0.0 collective-permute-start.9
  47.7 13.9 %prep.1 = (s32[80,128]{1,0:T(8,128)S(1)}, s32[80,128]{1,0:T(8,128)S(1)}, f32[80,128]{1,0:T(8,128)S(1)}, f32[80,128]{1,0:T(8,128)S(1)}, s32[1,128]{1,0:T(1,128)S(1)}) custom-call(s32[1]{0:T(128)} %bitcast.me_ref, s32[160,128]{1,0:T(8,128)S(1)} %bitcast.18, s32[160,128]{1,0:T(8,128)S(1)} %bitcast.20, s32[64,128]{1,0:T(8,128)S(1)} %bitcast.24, ...), custom_call_target="tpu_custom_call" | custom-call | tf_op jit(solution)/shard_map/prep/pallas_call | solution.py:399
  61.6 0.0 collective-permute-done.10.refs_5_
  61.6 0.5 collective-permute-done.6.refs_1_
  62.1 0.0 collective-permute-done.7.refs_2_
  62.1 3.7 %collective-permute-done.8.refs_3_ = f32[512,128]{1,0:T(8,128)S(1)} collective-permute-done((f32[512,128]{1,0:T(8,128)S(1)}, f32[512,128]{1,0:T(8,128)S(1)}, u32[]{:S(2)}, u32[]{:S(2)}) %collective-permute-start.8) | collective-permute-done | bytes 262176 | tf_op jit(solution)/shard_map/ppermute | solution.py:375
  65.8 0.1 collective-permute-done.9.refs_4_
  65.9 0.2 join.2.rest_0_.rest_1_
  66.1 2.9 %collective-permute-start.11 = (f32[3072,128]{1,0:T(8,128)S(1)}, f32[3072,128]{1,0:T(8,128)S(1)}, u32[]{:S(2)}, u32[]{:S(2)}) collective-permute-start(f32[3072,128]{1,0:T(8,128)S(1)} %join.2.rest_0_.rest_1_), channel_id=1, source_target_pairs={{0,1},{1,0},{2,3},{3,2},{4,5},{5,4},{6,7},{7,6},{8,9},{9,8},{10,11... | collective-permute-start | bytes 4718600 | tf_op jit(solution)/shard_map/ppermute | solution.py:375
  69.0 0.3 collective-permute-start.12
  69.3 1.6 %collective-permute-start.13 = (f32[512,128]{1,0:T(8,128)S(1)}, f32[512,128]{1,0:T(8,128)S(1)}, u32[]{:S(2)}, u32[]{:S(2)}) collective-permute-start(f32[512,128]{1,0:T(8,128)S(1)} %copy-done.6), channel_id=1, source_target_pairs={{0,14},{1,15},{2,12},{3,13},{4,10},{5,11},{6,8},{7,9},{8,6},{9,7},... | collective-permute-start | bytes 786440 | tf_op jit(solution)/shard_map/ppermute | solution.py:375
  70.9 1.1 collective-permute-done.11.rest_1_.rest_2_
  72.0 9.5 %worst0.1._.rest_0_ = f32[8,128]{1,0:T(8,128)S(1)} custom-call(s32[1]{0:T(128)} %bitcast.me_ref, s32[80,128]{1,0:T(8,128)S(1)} %get-tuple-element.26.f_ref, s32[80,128]{1,0:T(8,128)S(1)} %get-tuple-element.27.t_ref, s32[1,128]{1,0:T(1,128)S(1)} %get-tuple-element.28._.cnt_ref, f32[80,128]{1,0:T(8,128)S(1)} %get-tuple-element.29.ratio_ref, ...), custom_call_target="tpu_custom_call" | custom-call | tf_op jit(solution)/shard_map/worst0/pallas_call | solution.py:424
  81.5 6.6 %collective-permute-done.12.refs_0_ = f32[512,128]{1,0:T(8,128)S(1)} collective-permute-done((f32[512,128]{1,0:T(8,128)S(1)}, f32[512,128]{1,0:T(8,128)S(1)}, u32[]{:S(2)}, u32[]{:S(2)}) %collective-permute-start.12) | collective-permute-done | bytes 262176 | tf_op jit(solution)/shard_map/ppermute | solution.py:375
  88.1 6.1 %collective-permute-done.13.refs_1_ = f32[512,128]{1,0:T(8,128)S(1)} collective-permute-done((f32[512,128]{1,0:T(8,128)S(1)}, f32[512,128]{1,0:T(8,128)S(1)}, u32[]{:S(2)}, u32[]{:S(2)}) %collective-permute-start.13) | collective-permute-done | bytes 262176 | tf_op jit(solution)/shard_map/ppermute | solution.py:375
  94.2 0.9 join.3.rest_3_
  95.0 0.9 collective-permute-start.14
  95.9 1.9 %collective-permute-done.14.rest_4_ = f32[1024,128]{1,0:T(8,128)} collective-permute-done((f32[1024,128]{1,0:T(8,128)}, f32[1024,128]{1,0:T(8,128)}, u32[]{:S(2)}, u32[]{:S(2)}) %collective-permute-start.14) | collective-permute-done | bytes 524320 | tf_op jit(solution)/shard_map/ppermute | solution.py:375
  97.8 9.7 %worst1.1 = f32[1,128]{1,0:T(1,128)S(1)} custom-call(s32[1]{0:T(128)} %bitcast.me_ref, s32[80,128]{1,0:T(8,128)S(1)} %get-tuple-element.26.f_ref, s32[80,128]{1,0:T(8,128)S(1)} %get-tuple-element.27.t_ref, s32[1,128]{1,0:T(1,128)S(1)} %get-tuple-element.28._.cnt_ref, f32[80,128]{1,0:T(8,128)S(1)} %get-tuple-element.29.ratio_ref, ...), custom_call_target="tpu_custom_call" | custom-call | tf_op jit(solution)/shard_map/worst1/pallas_call | solution.py:424
  107.5 0.4 collective-permute-start.15
  108.0 0.6 constant_dynamic-slice_fusion.2
  108.6 0.2 collective-permute-done.15
  108.8 0.6 fusion.1
  (12 shorter events, 0.0 us)
Async XLA Ops:
  23.2 4.9 %collective-permute-start = (f32[24,128]{1,0:T(8,128)}, f32[24,128]{1,0:T(8,128)S(1)}, u32[]{:S(2)}, u32[]{:S(2)}) collective-permute-start(f32[24,128]{1,0:T(8,128)} %get-tuple-element.23), channel_id=1, source_target_pairs={{0,1},{1,0},{2,3},{3,2},{4,5},{5,4},{6,7},{7,6},{8,9},{9,8},{10,11... | collective-permute-start | bytes 36872 | tf_op jit(solution)/shard_map/ppermute | solution.py:375
  26.3 2.8 %collective-permute-start.1 = (f32[24,128]{1,0:T(8,128)}, f32[24,128]{1,0:T(8,128)S(1)}, u32[]{:S(2)}, u32[]{:S(2)}) collective-permute-start(f32[24,128]{1,0:T(8,128)} %get-tuple-element.23), channel_id=1, source_target_pairs={{0,2},{1,3},{2,0},{3,1},{4,6},{5,7},{6,4},{7,5},{8,10},{9,11},{10,... | collective-permute-start | bytes 36872 | tf_op jit(solution)/shard_map/ppermute | solution.py:375
  26.9 3.3 %collective-permute-start.2 = (f32[24,128]{1,0:T(8,128)}, f32[24,128]{1,0:T(8,128)S(1)}, u32[]{:S(2)}, u32[]{:S(2)}) collective-permute-start(f32[24,128]{1,0:T(8,128)} %get-tuple-element.23), channel_id=1, source_target_pairs={{0,3},{1,2},{2,1},{3,0},{4,7},{5,6},{6,5},{7,4},{8,11},{9,10},{10,... | collective-permute-start | bytes 36872 | tf_op jit(solution)/shard_map/ppermute | solution.py:375
  31.0 3.4 %collective-permute-start.3 = (f32[24,128]{1,0:T(8,128)S(1)}, f32[24,128]{1,0:T(8,128)S(1)}, u32[]{:S(2)}, u32[]{:S(2)}) collective-permute-start(f32[24,128]{1,0:T(8,128)S(1)} %add_add_fusion.rest_0_), channel_id=1, source_target_pairs={{0,4},{1,5},{2,6},{3,7},{4,0},{5,1},{6,2},{7,3},{8,12},{9,13},{10,... | collective-permute-start | bytes 36872 | tf_op jit(solution)/shard_map/ppermute | solution.py:375
  32.3 3.4 %collective-permute-start.4 = (f32[24,128]{1,0:T(8,128)S(1)}, f32[24,128]{1,0:T(8,128)S(1)}, u32[]{:S(2)}, u32[]{:S(2)}) collective-permute-start(f32[24,128]{1,0:T(8,128)S(1)} %add_add_fusion.rest_0_), channel_id=1, source_target_pairs={{0,8},{1,9},{2,10},{3,11},{4,12},{5,13},{6,14},{7,15},{8,0},{9,1},... | collective-permute-start | bytes 36872 | tf_op jit(solution)/shard_map/ppermute | solution.py:375
  32.3 3.4 %collective-permute-start.5 = (f32[24,128]{1,0:T(8,128)S(1)}, f32[24,128]{1,0:T(8,128)S(1)}, u32[]{:S(2)}, u32[]{:S(2)}) collective-permute-start(f32[24,128]{1,0:T(8,128)S(1)} %add_add_fusion.rest_0_), channel_id=1, source_target_pairs={{0,12},{1,13},{2,14},{3,15},{4,8},{5,9},{6,10},{7,11},{8,4},{9,5},... | collective-permute-start | bytes 36872 | tf_op jit(solution)/shard_map/ppermute | solution.py:375
  35.7 12.0 %copy-start = (s32[20480]{0:T(1024)S(1)}, s32[20480]{0:T(1024)}, u32[]{:S(2)}) copy-start(s32[20480]{0:T(1024)} %param.10) | copy-start | bytes 245764
  35.7 12.0 %copy-start.1 = (s32[20480]{0:T(1024)S(1)}, s32[20480]{0:T(1024)}, u32[]{:S(2)}) copy-start(s32[20480]{0:T(1024)} %param.11) | copy-start | bytes 245764
  35.7 12.0 %copy-start.2 = (f32[20480]{0:T(1024)S(1)}, f32[20480]{0:T(1024)}, u32[]{:S(2)}) copy-start(f32[20480]{0:T(1024)} %param.13) | copy-start | bytes 245764
  35.7 12.0 %copy-start.4 = (s32[8192]{0:T(1024)S(1)}, s32[8192]{0:T(1024)}, u32[]{:S(2)}) copy-start(s32[8192]{0:T(1024)} %param.12) | copy-start | bytes 98308
  35.7 12.0 %copy-start.5 = (f32[20480]{0:T(1024)S(1)}, f32[20480]{0:T(1024)}, u32[]{:S(2)}) copy-start(f32[20480]{0:T(1024)} %param.15) | copy-start | bytes 245764
  41.1 28.2 %copy-start.6 = (f32[512,128]{1,0:T(8,128)S(1)}, f32[512,128]{1,0:T(8,128)}, u32[]{:S(2)}) copy-start(f32[512,128]{1,0:T(8,128)} %get-tuple-element.38) | copy-start | bytes 786436
  41.1 30.9 %copy-start.3 = (f32[8,8,128]{2,1,0:T(8,128)S(1)}, f32[8,8,128]{2,1,0:T(8,128)}, u32[]{:S(2)}) copy-start(f32[8,8,128]{2,1,0:T(8,128)} %get-tuple-element.21.state_ref) | copy-start | bytes 98308
  41.1 20.6 %collective-permute-start.10 = (f32[512,128]{1,0:T(8,128)S(1)}, f32[512,128]{1,0:T(8,128)S(1)}, u32[]{:S(2)}, u32[]{:S(2)}) collective-permute-start(f32[512,128]{1,0:T(8,128)S(1)} %get-tuple-element.36), channel_id=1, source_target_pairs={{0,10},{1,11},{2,8},{3,9},{4,14},{5,15},{6,12},{7,13},{8,2},{9,3},... | collective-permute-start | bytes 786440 | tf_op jit(solution)/shard_map/ppermute | solution.py:375
  45.0 17.1 %collective-permute-start.6 = (f32[512,128]{1,0:T(8,128)S(1)}, f32[512,128]{1,0:T(8,128)S(1)}, u32[]{:S(2)}, u32[]{:S(2)}) collective-permute-start(f32[512,128]{1,0:T(8,128)S(1)} %get-tuple-element.32), channel_id=1, source_target_pairs={{0,2},{1,3},{2,0},{3,1},{4,6},{5,7},{6,4},{7,5},{8,10},{9,11},{10,... | collective-permute-start | bytes 786440 | tf_op jit(solution)/shard_map/ppermute | solution.py:375
  45.6 16.5 %collective-permute-start.7 = (f32[512,128]{1,0:T(8,128)S(1)}, f32[512,128]{1,0:T(8,128)S(1)}, u32[]{:S(2)}, u32[]{:S(2)}) collective-permute-start(f32[512,128]{1,0:T(8,128)S(1)} %get-tuple-element.33), channel_id=1, source_target_pairs={{0,4},{1,5},{2,6},{3,7},{4,0},{5,1},{6,2},{7,3},{8,12},{9,13},{10,... | collective-permute-start | bytes 786440 | tf_op jit(solution)/shard_map/ppermute | solution.py:375
  45.6 20.2 %collective-permute-start.8 = (f32[512,128]{1,0:T(8,128)S(1)}, f32[512,128]{1,0:T(8,128)S(1)}, u32[]{:S(2)}, u32[]{:S(2)}) collective-permute-start(f32[512,128]{1,0:T(8,128)S(1)} %get-tuple-element.34), channel_id=1, source_target_pairs={{0,6},{1,7},{2,4},{3,5},{4,2},{5,3},{6,0},{7,1},{8,14},{9,15},{10,... | collective-permute-start | bytes 786440 | tf_op jit(solution)/shard_map/ppermute | solution.py:375
  47.7 18.3 %collective-permute-start.9 = (f32[512,128]{1,0:T(8,128)S(1)}, f32[512,128]{1,0:T(8,128)S(1)}, u32[]{:S(2)}, u32[]{:S(2)}) collective-permute-start(f32[512,128]{1,0:T(8,128)S(1)} %get-tuple-element.35), channel_id=1, source_target_pairs={{0,8},{1,9},{2,10},{3,11},{4,12},{5,13},{6,14},{7,15},{8,0},{9,1},... | collective-permute-start | bytes 786440 | tf_op jit(solution)/shard_map/ppermute | solution.py:375
  66.1 5.9 %collective-permute-start.11 = (f32[3072,128]{1,0:T(8,128)S(1)}, f32[3072,128]{1,0:T(8,128)S(1)}, u32[]{:S(2)}, u32[]{:S(2)}) collective-permute-start(f32[3072,128]{1,0:T(8,128)S(1)} %join.2.rest_0_.rest_1_), channel_id=1, source_target_pairs={{0,1},{1,0},{2,3},{3,2},{4,5},{5,4},{6,7},{7,6},{8,9},{9,8},{10,11... | collective-permute-start | bytes 4718600 | tf_op jit(solution)/shard_map/ppermute | solution.py:375
  69.0 19.1 %collective-permute-start.12 = (f32[512,128]{1,0:T(8,128)S(1)}, f32[512,128]{1,0:T(8,128)S(1)}, u32[]{:S(2)}, u32[]{:S(2)}) collective-permute-start(f32[512,128]{1,0:T(8,128)S(1)} %get-tuple-element.37), channel_id=1, source_target_pairs={{0,12},{1,13},{2,14},{3,15},{4,8},{5,9},{6,10},{7,11},{8,4},{9,5},... | collective-permute-start | bytes 786440 | tf_op jit(solution)/shard_map/ppermute | solution.py:375
  69.3 24.9 %collective-permute-start.13 = (f32[512,128]{1,0:T(8,128)S(1)}, f32[512,128]{1,0:T(8,128)S(1)}, u32[]{:S(2)}, u32[]{:S(2)}) collective-permute-start(f32[512,128]{1,0:T(8,128)S(1)} %copy-done.6), channel_id=1, source_target_pairs={{0,14},{1,15},{2,12},{3,13},{4,10},{5,11},{6,8},{7,9},{8,6},{9,7},... | collective-permute-start | bytes 786440 | tf_op jit(solution)/shard_map/ppermute | solution.py:375
  95.0 2.8 %collective-permute-start.14 = (f32[1024,128]{1,0:T(8,128)}, f32[1024,128]{1,0:T(8,128)}, u32[]{:S(2)}, u32[]{:S(2)}) collective-permute-start(f32[1024,128]{1,0:T(8,128)} %join.3.rest_3_), channel_id=1, source_target_pairs={{0,1},{1,0},{2,3},{3,2},{4,5},{5,4},{6,7},{7,6},{8,9},{9,8},{10,11... | collective-permute-start | bytes 1572872 | tf_op jit(solution)/shard_map/ppermute | solution.py:375
  107.5 1.3 %collective-permute-start.15 = (f32[1,128]{1,0:T(1,128)S(1)}, f32[1,128]{1,0:T(1,128)S(1)}, u32[]{:S(2)}, u32[]{:S(2)}) collective-permute-start(f32[1,128]{1,0:T(1,128)S(1)} %worst1.1), channel_id=1, source_target_pairs={{0,1},{1,0},{2,3},{3,2},{4,5},{5,4},{6,7},{7,6},{8,9},{9,8},{10,11... | collective-permute-start | bytes 1544 | tf_op jit(solution)/shard_map/ppermute | solution.py:375

commit v8 on v7

--- a/solution.py
+++ b/solution.py
@@ -10,6 +10,7 @@
 
 STEPS = 3
 LANES = 128
+SPARE = 64
 LATE = 2
 CHUNKS = 1
 GROUP = 4
@@ -90,7 +91,7 @@
     first = me_ref[0] * width * LANES
     copies = stage([(from_ref, from_v), (to_ref, to_v), (slot_ref, slot_v), (sus_ref, sus_v),
                     (chg_ref, chg_v), (base_ref, base_v)], sem)
-    part = zinv_v.shape[0] // CHUNKS
+    part = zinv_ref.shape[0] // CHUNKS
     cuts = [pl.ds(i * part, part) for i in range(CHUNKS)]
     zinv_copies = stage([(zinv_ref.at[c], zinv_v.at[c]) for c in cuts], zinv_sem)
     for copy in copies:
@@ -294,7 +295,7 @@
     for own, other in zip(pieces[::2], pieces[1::2]):
         size = own.shape[0]
         pairs += [(own, table.at[pl.ds(row, size)]),
-                  (other, table.at[pl.ds(table.shape[0] // 2 + row, size)])]
+                  (other, table.at[pl.ds((table.shape[0] - SPARE) // 2 + row, size)])]
         row += size
     copies = stage(pairs, sem)
     ids = state_ref[6, pl.ds(me_ref[0] >> 1, 1), :]
@@ -365,7 +366,8 @@
         out_shape=[f32(8, blocks, LANES), f32(3 * blocks, LANES), f32(blocks, *row_shape)],
         in_specs=[SMEM, VMEM] + [ANY] * 7,
         out_specs=[VMEM] * 2 + [ANY],
-        scratch_shapes=[like(from2), like(to2), like(slot2), like(sus2), like(chg2), like(base2), like(flat),
+        scratch_shapes=[like(from2), like(to2), like(slot2), like(sus2), like(chg2), like(base2),
+                        pltpu.VMEM((flat.shape[0] + SPARE, LANES), jnp.float32),
                         pltpu.VMEM((2 * blocks, LANES), jnp.int32), pltpu.SMEM((2 * blocks, LANES), jnp.int32),
                         pltpu.VMEM((2,) + row_shape, jnp.float32), pltpu.SemaphoreType.DMA((6,)),
                         pltpu.SemaphoreType.DMA((2,)), pltpu.SemaphoreType.DMA((CHUNKS,))],
@@ -427,7 +429,7 @@
             out_shape=f32(1 if level else 8, LANES),
             in_specs=[SMEM] + [ANY] * 3 + [VMEM] * (3 + level) + [ANY] * (len(operands) - level),
             out_specs=VMEM,
-            scratch_shapes=[pltpu.VMEM((buses, LANES), jnp.float32), pltpu.SMEM(f_rel.shape, jnp.int32),
+            scratch_shapes=[pltpu.VMEM((buses + SPARE, LANES), jnp.float32), pltpu.SMEM(f_rel.shape, jnp.int32),
                             pltpu.SMEM(t_rel.shape, jnp.int32), pltpu.SMEM(counts.shape, jnp.int32),
                             pltpu.VMEM((8, LANES), jnp.float32), pltpu.VMEM((LANES, LANES), jnp.float32),
                             pltpu.SemaphoreType.DMA((3 + len(operands),))],

time: 110 us -> 110 us (level)
  no operation moved by 1% of the time
where the time goes in v8:
time: 110 us; the launch traced here: 109 us
  Pallas kernels  51.9 us (47%)
  waiting for transfers between devices  23.6 us (21%)
  starting transfers between devices  20.2 us (18%)
  blocking collectives  9.25 us (8%)
  other arithmetic  2.06 us (2%)
  local copies, waits for them, and re-layouts  1.54 us (1%)
    ppermute x16, waiting for transfers between devices, per_device(): lax.ppermute(a, 'col', [(i, i ^ m) for i in range(n_col)])  23.6 us
    ppermute x16, starting transfers between devices, per_device(): lax.ppermute(a, 'col', [(i, i ^ m) for i in range(n_col)])  20.2 us
    pallas_call x2, Pallas kernels, worst_of(): pl.pallas_call(functools.partial(worst_kernel, level), name=f'worst{level...  19.2 us
    pallas_call x1, Pallas kernels, per_device(): pl.pallas_call(functools.partial(prep_kernel, cols, chips), name='prep',...  13.9 us
    pallas_call x1, Pallas kernels, per_device(): pl.pallas_call(functools.partial(ends_kernel, width), name='ends', out_sh...  12.4 us
    psum x1, blocking collectives, per_device(): ids = lax.psum(ids[None], 'col')  9.25 us
    pallas_call x1, Pallas kernels, per_device(): pl.pallas_call(functools.partial(spread_kernel, chips, len(terms)), name=...  5.32 us
  transfers between devices with their start and end apart: 16, of which 11 were waited for; matrix products, arithmetic and copies ran while one was open for 1% of the time, Pallas kernels for 21%

profile of v8, /device:TPU:9, one launch (start us, length us, event | category | flops | bytes accessed | tf_op | source)
XLA Modules:
  0.0 109.4 jit_solution(15901052352294754616)
XLA Ops:
  0.6 0.9 dynamic_update_slice.4
  1.5 9.2 %psum.7.ids_ref = s32[1,1024]{1,0:T(1,128)} all-reduce(s32[1,1024]{1,0:T(1,128)S(1)} %dynamic_update_slice.4), channel_id=1, replica_groups=mesh['parts'=2,'col'=16] {'col'}, use_global_device_ids=true, to_apply=%region_0.0 | all-reduce | flops 1024 | bytes 8192 | tf_op jit(solution)/shard_map/psum | solution.py:358
  10.8 12.4 %ends.1 = (f32[8,8,128]{2,1,0:T(8,128)}, f32[24,128]{1,0:T(8,128)}, f32[8,2,512,128]{3,2,1,0:T(8,128)}) custom-call(s32[1]{0:T(128)} %bitcast.me_ref, s32[1,1024]{1,0:T(1,128)} %psum.7.ids_ref, s32[160,128]{1,0:T(8,128)} %bitcast.17, s32[160,128]{1,0:T(8,128)} %bitcast.19, s32[64,128]{1,0:T(8,128)} %bitcast.23, f32[160,128]{1,0:T(8,128)} %bitcast.21, ...), custom_call_target="tpu_custom_call" | custom-call | tf_op jit(solution)/shard_map/ends/pallas_call | solution.py:363
  23.2 3.2 %collective-permute-start = (f32[24,128]{1,0:T(8,128)}, f32[24,128]{1,0:T(8,128)S(1)}, u32[]{:S(2)}, u32[]{:S(2)}) collective-permute-start(f32[24,128]{1,0:T(8,128)} %get-tuple-element.23), channel_id=1, source_target_pairs={{0,1},{1,0},{2,3},{3,2},{4,5},{5,4},{6,7},{7,6},{8,9},{9,8},{10,11... | collective-permute-start | bytes 36872 | tf_op jit(solution)/shard_map/ppermute | solution.py:377
  26.3 0.6 collective-permute-start.1
  26.9 1.1 %collective-permute-start.2 = (f32[24,128]{1,0:T(8,128)}, f32[24,128]{1,0:T(8,128)S(1)}, u32[]{:S(2)}, u32[]{:S(2)}) collective-permute-start(f32[24,128]{1,0:T(8,128)} %get-tuple-element.23), channel_id=1, source_target_pairs={{0,3},{1,2},{2,1},{3,0},{4,7},{5,6},{6,5},{7,4},{8,11},{9,10},{10,... | collective-permute-start | bytes 36872 | tf_op jit(solution)/shard_map/ppermute | solution.py:377
  28.1 0.0 collective-permute-done
  28.1 1.1 collective-permute-done.1
  29.1 1.1 %collective-permute-done.2 = f32[24,128]{1,0:T(8,128)S(1)} collective-permute-done((f32[24,128]{1,0:T(8,128)}, f32[24,128]{1,0:T(8,128)S(1)}, u32[]{:S(2)}, u32[]{:S(2)}) %collective-permute-start.2) | collective-permute-done | bytes 12320 | tf_op jit(solution)/shard_map/ppermute | solution.py:377
  30.3 0.7 add_add_fusion.rest_0_
  31.0 1.3 %collective-permute-start.3 = (f32[24,128]{1,0:T(8,128)S(1)}, f32[24,128]{1,0:T(8,128)S(1)}, u32[]{:S(2)}, u32[]{:S(2)}) collective-permute-start(f32[24,128]{1,0:T(8,128)S(1)} %add_add_fusion.rest_0_), channel_id=1, source_target_pairs={{0,4},{1,5},{2,6},{3,7},{4,0},{5,1},{6,2},{7,3},{8,12},{9,13},{10,... | collective-permute-start | bytes 36872 | tf_op jit(solution)/shard_map/ppermute | solution.py:377
  32.3 0.1 collective-permute-start.4
  32.3 1.3 %collective-permute-start.5 = (f32[24,128]{1,0:T(8,128)S(1)}, f32[24,128]{1,0:T(8,128)S(1)}, u32[]{:S(2)}, u32[]{:S(2)}) collective-permute-start(f32[24,128]{1,0:T(8,128)S(1)} %add_add_fusion.rest_0_), channel_id=1, source_target_pairs={{0,12},{1,13},{2,14},{3,15},{4,8},{5,9},{6,10},{7,11},{8,4},{9,5},... | collective-permute-start | bytes 36872 | tf_op jit(solution)/shard_map/ppermute | solution.py:377
  33.6 0.8 broadcast_add_fusion.state_ref
  34.4 0.0 collective-permute-done.3.rest_1_
  34.4 1.3 %collective-permute-done.4.rest_2_ = f32[24,128]{1,0:T(8,128)S(1)} collective-permute-done((f32[24,128]{1,0:T(8,128)S(1)}, f32[24,128]{1,0:T(8,128)S(1)}, u32[]{:S(2)}, u32[]{:S(2)}) %collective-permute-start.4) | collective-permute-done | bytes 12320 | tf_op jit(solution)/shard_map/ppermute | solution.py:377
  35.7 0.0 collective-permute-done.5.rest_3_
  35.7 0.0 copy-start.4
  35.7 0.0 copy-start.5
  35.7 5.3 %spread.1 = (f32[2,8,128]{2,1,0:T(8,128)S(1)}, f32[1024,512]{1,0:T(8,128)}, f32[512,128]{1,0:T(8,128)S(1)}, f32[512,128]{1,0:T(8,128)S(1)}, f32[512,128]{1,0:T(8...) custom-call(s32[1]{0:T(128)} %bitcast.me_ref, ...), custom_call_target="tpu_custom_call" | custom-call | tf_op jit(solution)/shard_map/spread/pallas_call | solution.py:386
  41.1 3.9 %collective-permute-start.10 = (f32[512,128]{1,0:T(8,128)S(1)}, f32[512,128]{1,0:T(8,128)S(1)}, u32[]{:S(2)}, u32[]{:S(2)}) collective-permute-start(f32[512,128]{1,0:T(8,128)S(1)} %get-tuple-element.36), channel_id=1, source_target_pairs={{0,10},{1,11},{2,8},{3,9},{4,14},{5,15},{6,12},{7,13},{8,2},{9,3},... | collective-permute-start | bytes 786440 | tf_op jit(solution)/shard_map/ppermute | solution.py:377
  45.0 0.6 collective-permute-start.6
  45.6 0.0 collective-permute-start.7
  45.6 2.1 %collective-permute-start.8 = (f32[512,128]{1,0:T(8,128)S(1)}, f32[512,128]{1,0:T(8,128)S(1)}, u32[]{:S(2)}, u32[]{:S(2)}) collective-permute-start(f32[512,128]{1,0:T(8,128)S(1)} %get-tuple-element.34), channel_id=1, source_target_pairs={{0,6},{1,7},{2,4},{3,5},{4,2},{5,3},{6,0},{7,1},{8,14},{9,15},{10,... | collective-permute-start | bytes 786440 | tf_op jit(solution)/shard_map/ppermute | solution.py:377
  47.7 0.0 collective-permute-start.9
  47.7 13.9 %prep.1 = (s32[80,128]{1,0:T(8,128)S(1)}, s32[80,128]{1,0:T(8,128)S(1)}, f32[80,128]{1,0:T(8,128)S(1)}, f32[80,128]{1,0:T(8,128)S(1)}, s32[1,128]{1,0:T(1,128)S(1)}) custom-call(s32[1]{0:T(128)} %bitcast.me_ref, s32[160,128]{1,0:T(8,128)S(1)} %bitcast.18, s32[160,128]{1,0:T(8,128)S(1)} %bitcast.20, s32[64,128]{1,0:T(8,128)S(1)} %bitcast.24, ...), custom_call_target="tpu_custom_call" | custom-call | tf_op jit(solution)/shard_map/prep/pallas_call | solution.py:401
  61.6 0.0 collective-permute-done.10.refs_5_
  61.6 0.5 collective-permute-done.6.refs_1_
  62.1 0.0 collective-permute-done.7.refs_2_
  62.1 3.7 %collective-permute-done.8.refs_3_ = f32[512,128]{1,0:T(8,128)S(1)} collective-permute-done((f32[512,128]{1,0:T(8,128)S(1)}, f32[512,128]{1,0:T(8,128)S(1)}, u32[]{:S(2)}, u32[]{:S(2)}) %collective-permute-start.8) | collective-permute-done | bytes 262176 | tf_op jit(solution)/shard_map/ppermute | solution.py:377
  65.8 0.1 collective-permute-done.9.refs_4_
  65.9 0.2 join.2.rest_0_.rest_1_
  66.1 2.9 %collective-permute-start.11 = (f32[3072,128]{1,0:T(8,128)S(1)}, f32[3072,128]{1,0:T(8,128)S(1)}, u32[]{:S(2)}, u32[]{:S(2)}) collective-permute-start(f32[3072,128]{1,0:T(8,128)S(1)} %join.2.rest_0_.rest_1_), channel_id=1, source_target_pairs={{0,1},{1,0},{2,3},{3,2},{4,5},{5,4},{6,7},{7,6},{8,9},{9,8},{10,11... | collective-permute-start | bytes 4718600 | tf_op jit(solution)/shard_map/ppermute | solution.py:377
  69.0 0.3 collective-permute-start.12
  69.3 0.0 copy-done.6
  69.3 1.6 %collective-permute-start.13 = (f32[512,128]{1,0:T(8,128)S(1)}, f32[512,128]{1,0:T(8,128)S(1)}, u32[]{:S(2)}, u32[]{:S(2)}) collective-permute-start(f32[512,128]{1,0:T(8,128)S(1)} %copy-done.6), channel_id=1, source_target_pairs={{0,14},{1,15},{2,12},{3,13},{4,10},{5,11},{6,8},{7,9},{8,6},{9,7},... | collective-permute-start | bytes 786440 | tf_op jit(solution)/shard_map/ppermute | solution.py:377
  70.9 1.1 collective-permute-done.11.rest_1_.rest_2_
  72.0 9.5 %worst0.1._.rest_0_ = f32[8,128]{1,0:T(8,128)S(1)} custom-call(s32[1]{0:T(128)} %bitcast.me_ref, s32[80,128]{1,0:T(8,128)S(1)} %get-tuple-element.26.f_ref, s32[80,128]{1,0:T(8,128)S(1)} %get-tuple-element.27.t_ref, s32[1,128]{1,0:T(1,128)S(1)} %get-tuple-element.28._.cnt_ref, f32[80,128]{1,0:T(8,128)S(1)} %get-tuple-element.29.ratio_ref, ...), custom_call_target="tpu_custom_call" | custom-call | tf_op jit(solution)/shard_map/worst0/pallas_call | solution.py:426
  81.5 6.6 %collective-permute-done.12.refs_0_ = f32[512,128]{1,0:T(8,128)S(1)} collective-permute-done((f32[512,128]{1,0:T(8,128)S(1)}, f32[512,128]{1,0:T(8,128)S(1)}, u32[]{:S(2)}, u32[]{:S(2)}) %collective-permute-start.12) | collective-permute-done | bytes 262176 | tf_op jit(solution)/shard_map/ppermute | solution.py:377
  88.1 6.1 %collective-permute-done.13.refs_1_ = f32[512,128]{1,0:T(8,128)S(1)} collective-permute-done((f32[512,128]{1,0:T(8,128)S(1)}, f32[512,128]{1,0:T(8,128)S(1)}, u32[]{:S(2)}, u32[]{:S(2)}) %collective-permute-start.13) | collective-permute-done | bytes 262176 | tf_op jit(solution)/shard_map/ppermute | solution.py:377
  94.2 0.9 join.3.rest_3_
  95.0 0.9 collective-permute-start.14
  95.9 1.9 %collective-permute-done.14.rest_4_ = f32[1024,128]{1,0:T(8,128)} collective-permute-done((f32[1024,128]{1,0:T(8,128)}, f32[1024,128]{1,0:T(8,128)}, u32[]{:S(2)}, u32[]{:S(2)}) %collective-permute-start.14) | collective-permute-done | bytes 524320 | tf_op jit(solution)/shard_map/ppermute | solution.py:377
  97.8 9.7 %worst1.1 = f32[1,128]{1,0:T(1,128)S(1)} custom-call(s32[1]{0:T(128)} %bitcast.me_ref, s32[80,128]{1,0:T(8,128)S(1)} %get-tuple-element.26.f_ref, s32[80,128]{1,0:T(8,128)S(1)} %get-tuple-element.27.t_ref, s32[1,128]{1,0:T(1,128)S(1)} %get-tuple-element.28._.cnt_ref, f32[80,128]{1,0:T(8,128)S(1)} %get-tuple-element.29.ratio_ref, ...), custom_call_target="tpu_custom_call" | custom-call | tf_op jit(solution)/shard_map/worst1/pallas_call | solution.py:426
  107.5 0.4 collective-permute-start.15
  108.0 0.6 constant_dynamic-slice_fusion.2
  108.6 0.2 collective-permute-done.15
  108.8 0.6 fusion.1
  (12 shorter events, 0.0 us)
Async XLA Ops:
  23.2 4.9 %collective-permute-start = (f32[24,128]{1,0:T(8,128)}, f32[24,128]{1,0:T(8,128)S(1)}, u32[]{:S(2)}, u32[]{:S(2)}) collective-permute-start(f32[24,128]{1,0:T(8,128)} %get-tuple-element.23), channel_id=1, source_target_pairs={{0,1},{1,0},{2,3},{3,2},{4,5},{5,4},{6,7},{7,6},{8,9},{9,8},{10,11... | collective-permute-start | bytes 36872 | tf_op jit(solution)/shard_map/ppermute | solution.py:377
  26.3 2.8 %collective-permute-start.1 = (f32[24,128]{1,0:T(8,128)}, f32[24,128]{1,0:T(8,128)S(1)}, u32[]{:S(2)}, u32[]{:S(2)}) collective-permute-start(f32[24,128]{1,0:T(8,128)} %get-tuple-element.23), channel_id=1, source_target_pairs={{0,2},{1,3},{2,0},{3,1},{4,6},{5,7},{6,4},{7,5},{8,10},{9,11},{10,... | collective-permute-start | bytes 36872 | tf_op jit(solution)/shard_map/ppermute | solution.py:377
  26.9 3.3 %collective-permute-start.2 = (f32[24,128]{1,0:T(8,128)}, f32[24,128]{1,0:T(8,128)S(1)}, u32[]{:S(2)}, u32[]{:S(2)}) collective-permute-start(f32[24,128]{1,0:T(8,128)} %get-tuple-element.23), channel_id=1, source_target_pairs={{0,3},{1,2},{2,1},{3,0},{4,7},{5,6},{6,5},{7,4},{8,11},{9,10},{10,... | collective-permute-start | bytes 36872 | tf_op jit(solution)/shard_map/ppermute | solution.py:377
  31.0 3.4 %collective-permute-start.3 = (f32[24,128]{1,0:T(8,128)S(1)}, f32[24,128]{1,0:T(8,128)S(1)}, u32[]{:S(2)}, u32[]{:S(2)}) collective-permute-start(f32[24,128]{1,0:T(8,128)S(1)} %add_add_fusion.rest_0_), channel_id=1, source_target_pairs={{0,4},{1,5},{2,6},{3,7},{4,0},{5,1},{6,2},{7,3},{8,12},{9,13},{10,... | collective-permute-start | bytes 36872 | tf_op jit(solution)/shard_map/ppermute | solution.py:377
  32.3 3.4 %collective-permute-start.4 = (f32[24,128]{1,0:T(8,128)S(1)}, f32[24,128]{1,0:T(8,128)S(1)}, u32[]{:S(2)}, u32[]{:S(2)}) collective-permute-start(f32[24,128]{1,0:T(8,128)S(1)} %add_add_fusion.rest_0_), channel_id=1, source_target_pairs={{0,8},{1,9},{2,10},{3,11},{4,12},{5,13},{6,14},{7,15},{8,0},{9,1},... | collective-permute-start | bytes 36872 | tf_op jit(solution)/shard_map/ppermute | solution.py:377
  32.3 3.4 %collective-permute-start.5 = (f32[24,128]{1,0:T(8,128)S(1)}, f32[24,128]{1,0:T(8,128)S(1)}, u32[]{:S(2)}, u32[]{:S(2)}) collective-permute-start(f32[24,128]{1,0:T(8,128)S(1)} %add_add_fusion.rest_0_), channel_id=1, source_target_pairs={{0,12},{1,13},{2,14},{3,15},{4,8},{5,9},{6,10},{7,11},{8,4},{9,5},... | collective-permute-start | bytes 36872 | tf_op jit(solution)/shard_map/ppermute | solution.py:377
  35.7 12.0 %copy-start = (s32[20480]{0:T(1024)S(1)}, s32[20480]{0:T(1024)}, u32[]{:S(2)}) copy-start(s32[20480]{0:T(1024)} %param.10) | copy-start | bytes 245764
  35.7 12.0 %copy-start.1 = (s32[20480]{0:T(1024)S(1)}, s32[20480]{0:T(1024)}, u32[]{:S(2)}) copy-start(s32[20480]{0:T(1024)} %param.11) | copy-start | bytes 245764
  35.7 12.0 %copy-start.2 = (f32[20480]{0:T(1024)S(1)}, f32[20480]{0:T(1024)}, u32[]{:S(2)}) copy-start(f32[20480]{0:T(1024)} %param.13) | copy-start | bytes 245764
  35.7 12.0 %copy-start.4 = (s32[8192]{0:T(1024)S(1)}, s32[8192]{0:T(1024)}, u32[]{:S(2)}) copy-start(s32[8192]{0:T(1024)} %param.12) | copy-start | bytes 98308
  35.7 12.0 %copy-start.5 = (f32[20480]{0:T(1024)S(1)}, f32[20480]{0:T(1024)}, u32[]{:S(2)}) copy-start(f32[20480]{0:T(1024)} %param.15) | copy-start | bytes 245764
  41.1 28.2 %copy-start.6 = (f32[512,128]{1,0:T(8,128)S(1)}, f32[512,128]{1,0:T(8,128)}, u32[]{:S(2)}) copy-start(f32[512,128]{1,0:T(8,128)} %get-tuple-element.38) | copy-start | bytes 786436
  41.1 30.9 %copy-start.3 = (f32[8,8,128]{2,1,0:T(8,128)S(1)}, f32[8,8,128]{2,1,0:T(8,128)}, u32[]{:S(2)}) copy-start(f32[8,8,128]{2,1,0:T(8,128)} %get-tuple-element.21.state_ref) | copy-start | bytes 98308
  41.1 20.6 %collective-permute-start.10 = (f32[512,128]{1,0:T(8,128)S(1)}, f32[512,128]{1,0:T(8,128)S(1)}, u32[]{:S(2)}, u32[]{:S(2)}) collective-permute-start(f32[512,128]{1,0:T(8,128)S(1)} %get-tuple-element.36), channel_id=1, source_target_pairs={{0,10},{1,11},{2,8},{3,9},{4,14},{5,15},{6,12},{7,13},{8,2},{9,3},... | collective-permute-start | bytes 786440 | tf_op jit(solution)/shard_map/ppermute | solution.py:377
  45.0 17.1 %collective-permute-start.6 = (f32[512,128]{1,0:T(8,128)S(1)}, f32[512,128]{1,0:T(8,128)S(1)}, u32[]{:S(2)}, u32[]{:S(2)}) collective-permute-start(f32[512,128]{1,0:T(8,128)S(1)} %get-tuple-element.32), channel_id=1, source_target_pairs={{0,2},{1,3},{2,0},{3,1},{4,6},{5,7},{6,4},{7,5},{8,10},{9,11},{10,... | collective-permute-start | bytes 786440 | tf_op jit(solution)/shard_map/ppermute | solution.py:377
  45.6 16.5 %collective-permute-start.7 = (f32[512,128]{1,0:T(8,128)S(1)}, f32[512,128]{1,0:T(8,128)S(1)}, u32[]{:S(2)}, u32[]{:S(2)}) collective-permute-start(f32[512,128]{1,0:T(8,128)S(1)} %get-tuple-element.33), channel_id=1, source_target_pairs={{0,4},{1,5},{2,6},{3,7},{4,0},{5,1},{6,2},{7,3},{8,12},{9,13},{10,... | collective-permute-start | bytes 786440 | tf_op jit(solution)/shard_map/ppermute | solution.py:377
  45.6 20.2 %collective-permute-start.8 = (f32[512,128]{1,0:T(8,128)S(1)}, f32[512,128]{1,0:T(8,128)S(1)}, u32[]{:S(2)}, u32[]{:S(2)}) collective-permute-start(f32[512,128]{1,0:T(8,128)S(1)} %get-tuple-element.34), channel_id=1, source_target_pairs={{0,6},{1,7},{2,4},{3,5},{4,2},{5,3},{6,0},{7,1},{8,14},{9,15},{10,... | collective-permute-start | bytes 786440 | tf_op jit(solution)/shard_map/ppermute | solution.py:377
  47.7 18.3 %collective-permute-start.9 = (f32[512,128]{1,0:T(8,128)S(1)}, f32[512,128]{1,0:T(8,128)S(1)}, u32[]{:S(2)}, u32[]{:S(2)}) collective-permute-start(f32[512,128]{1,0:T(8,128)S(1)} %get-tuple-element.35), channel_id=1, source_target_pairs={{0,8},{1,9},{2,10},{3,11},{4,12},{5,13},{6,14},{7,15},{8,0},{9,1},... | collective-permute-start | bytes 786440 | tf_op jit(solution)/shard_map/ppermute | solution.py:377
  66.1 5.9 %collective-permute-start.11 = (f32[3072,128]{1,0:T(8,128)S(1)}, f32[3072,128]{1,0:T(8,128)S(1)}, u32[]{:S(2)}, u32[]{:S(2)}) collective-permute-start(f32[3072,128]{1,0:T(8,128)S(1)} %join.2.rest_0_.rest_1_), channel_id=1, source_target_pairs={{0,1},{1,0},{2,3},{3,2},{4,5},{5,4},{6,7},{7,6},{8,9},{9,8},{10,11... | collective-permute-start | bytes 4718600 | tf_op jit(solution)/shard_map/ppermute | solution.py:377
  69.0 19.1 %collective-permute-start.12 = (f32[512,128]{1,0:T(8,128)S(1)}, f32[512,128]{1,0:T(8,128)S(1)}, u32[]{:S(2)}, u32[]{:S(2)}) collective-permute-start(f32[512,128]{1,0:T(8,128)S(1)} %get-tuple-element.37), channel_id=1, source_target_pairs={{0,12},{1,13},{2,14},{3,15},{4,8},{5,9},{6,10},{7,11},{8,4},{9,5},... | collective-permute-start | bytes 786440 | tf_op jit(solution)/shard_map/ppermute | solution.py:377
  69.3 24.9 %collective-permute-start.13 = (f32[512,128]{1,0:T(8,128)S(1)}, f32[512,128]{1,0:T(8,128)S(1)}, u32[]{:S(2)}, u32[]{:S(2)}) collective-permute-start(f32[512,128]{1,0:T(8,128)S(1)} %copy-done.6), channel_id=1, source_target_pairs={{0,14},{1,15},{2,12},{3,13},{4,10},{5,11},{6,8},{7,9},{8,6},{9,7},... | collective-permute-start | bytes 786440 | tf_op jit(solution)/shard_map/ppermute | solution.py:377
  95.0 2.8 %collective-permute-start.14 = (f32[1024,128]{1,0:T(8,128)}, f32[1024,128]{1,0:T(8,128)}, u32[]{:S(2)}, u32[]{:S(2)}) collective-permute-start(f32[1024,128]{1,0:T(8,128)} %join.3.rest_3_), channel_id=1, source_target_pairs={{0,1},{1,0},{2,3},{3,2},{4,5},{5,4},{6,7},{7,6},{8,9},{9,8},{10,11... | collective-permute-start | bytes 1572872 | tf_op jit(solution)/shard_map/ppermute | solution.py:377
  107.5 1.3 %collective-permute-start.15 = (f32[1,128]{1,0:T(1,128)S(1)}, f32[1,128]{1,0:T(1,128)S(1)}, u32[]{:S(2)}, u32[]{:S(2)}) collective-permute-start(f32[1,128]{1,0:T(1,128)S(1)} %worst1.1), channel_id=1, source_target_pairs={{0,1},{1,0},{2,3},{3,2},{4,5},{5,4},{6,7},{7,6},{8,9},{9,8},{10,11... | collective-permute-start | bytes 1544 | tf_op jit(solution)/shard_map/ppermute | solution.py:377
